TPU v7x, 256 devices: a whole 4x4x8 slice. The times are simulated.
256 devices in a mesh: grp: 4 (over x), dev: 64 (over z, y, core).
Axes of the slice: x: 4, y: 4, z: 8, core: 2. Of those that a mesh axis runs over, the one named last changes fastest.
Arguments:
- features: bfloat16 [524288, 256], P(('grp', 'dev')), may hold values from -24 to 24
- weight: bfloat16 [256, 256], replicated, may hold values from -0.375 to 0.375
- cotangent: bfloat16 [524288, 256], P(('grp', 'dev')), may hold values from -6 to 6
- tile_vals: bfloat16 [256, 32, 128, 128], P(('grp', 'dev')), may hold values from -0.375 to 0.375
- tile_rows: int32 [256, 32], P(('grp', 'dev')), may hold values from 0 to 15
- tile_cols: int32 [256, 32], P(('grp', 'dev')), may hold values from 0 to 15
- hub_rows: int32 [256, 32], P(('grp', 'dev')), may hold values from 0 to 2047, as said below
- send_hub: int32 [256, 64, 8], P(('grp', 'dev')), may hold values from -1 to 31, as said below
- mirror_slot: int32 [256, 16384], P(('grp', 'dev')), may hold values from 0 to 511, as said below
- replica_target_row: int32 [256, 16384], P(('grp', 'dev')), may hold values from 0 to 2047
- replica_edge_weight: float32 [256, 16384], P(('grp', 'dev')), may hold values from 0.2 to 1
Outputs:
- activated: bfloat16 [524288, 256], P(('grp', 'dev'))
- feature_grad: bfloat16 [524288, 256], P(('grp', 'dev'))
- weight_grad: float32 [256, 256], P('dev')
Inputs may be any that keep to these rules, and one draw needn't show every extreme that they name: `hub_rows`: the 32 entries of each device are distinct rows of its block. `send_hub`: entry [q, r, c] is the index into q's hub list of the c-th hub row that q sends to device r of its group along dev, or -1 for an empty slot; used slots come first in each bucket, hubs within a bucket are distinct, every bucket uses at least one slot, each device fills all 8 slots of at least one bucket and each device receives at least one full bucket. `mirror_slot`: value s * 8 + c on device g * 64 + r names slot c of the bucket that device g * 64 + s sends to it; only used slots are named.
All inputs are finite; a program needn't handle non-finite values.
Results may differ from a plain program's by a relative error of at most 0.0078.
Values may be sent and summed in bfloat16 or wider, within the bound.
No kernel may reach another device: no remote copies, remote signals or barrier semaphores. Data moves between devices by JAX's collectives and lax.ppermute only.
A program may use at most 64 MiB of HBM per device.

v0:
```python
import math

import jax
import jax.numpy as jnp
from jax import lax
from jax.sharding import PartitionSpec as P


def silu_slope(hidden):
    logistic = jax.nn.sigmoid(hidden)
    return logistic * (1.0 + hidden * (1.0 - logistic))


def tile_part(signal, tile_mats, from_blk, to_blk, pattern):
    rows_dev, columns = signal.shape
    tile_size = tile_mats.shape[-1]
    blocks = rows_dev // tile_size
    picked = signal.reshape(blocks, tile_size, columns)[from_blk]
    product = jnp.einsum(pattern, tile_mats, picked, preferred_element_type=jnp.float32)
    onehot = (to_blk[None, :] == jnp.arange(blocks)[:, None]).astype(jnp.float32)
    placed = jnp.einsum("bt,tif->bif", onehot, product, precision=lax.Precision.HIGHEST)
    return placed.reshape(rows_dev, columns)


def placement_matrix(row_ids, row_count, valid):
    hits = (jnp.arange(row_count, dtype=jnp.int32)[:, None] == row_ids[None, :]) & valid[None, :]
    return hits.astype(jnp.float32)


def hub_part(signal, hub_ids, edge_matrix, global_ids):
    rows_dev, columns = signal.shape
    peers = lax.axis_size("dev")
    partial_value = jnp.einsum(
        "vk,vf->kf", edge_matrix, signal.astype(jnp.float32), precision=lax.Precision.HIGHEST
    )
    hub_count = hub_ids.shape[0]
    all_hubs = lax.all_gather(signal[hub_ids], "dev", axis=0, tiled=True)
    mirrored = all_hubs[global_ids]
    every_slot = jnp.ones(global_ids.shape, bool)
    regroup = placement_matrix(global_ids, peers * hub_count, every_slot)
    by_hub = jnp.dot(regroup, partial_value, precision=lax.Precision.HIGHEST)
    own_share = lax.psum_scatter(by_hub, "dev", scatter_dimension=0, tiled=True)
    placing = placement_matrix(hub_ids, rows_dev, jnp.ones(hub_ids.shape, bool))
    returned = jnp.dot(placing, own_share, precision=lax.Precision.HIGHEST)
    incoming = jnp.dot(edge_matrix, mirrored.astype(jnp.float32), precision=lax.Precision.HIGHEST)
    return incoming + returned


def spread(signal, graph_parts, transpose):
    tile_mats, row_blocks, col_blocks, hub_ids, send_list, edge_matrix, global_ids = graph_parts
    if transpose:
        nearby = tile_part(signal, tile_mats, row_blocks, col_blocks, "tji,tjf->tif")
    else:
        nearby = tile_part(signal, tile_mats, col_blocks, row_blocks, "tij,tjf->tif")
    return nearby + hub_part(signal, hub_ids, edge_matrix, global_ids)


def local(
    features,
    weight,
    cotangent,
    tile_vals,
    tile_rows,
    tile_cols,
    hub_rows,
    send_hub,
    mirror_slot,
    replica_target_row,
    replica_edge_weight,
):
    peers = lax.axis_size("dev")
    send_list = send_hub[0]
    hub_ids = hub_rows[0]
    rows_dev = features.shape[0]
    slot_count = peers * send_list.shape[1]
    edge_matrix = (
        jnp.zeros((rows_dev, slot_count), jnp.float32)
        .at[replica_target_row[0], mirror_slot[0]]
        .add(replica_edge_weight[0])
    )
    arrived = lax.all_to_all(send_list, "dev", split_axis=0, concat_axis=0, tiled=True)
    offsets = jnp.arange(peers, dtype=jnp.int32)[:, None] * hub_ids.shape[0]
    global_ids = (offsets + jnp.maximum(arrived, 0)).reshape(-1)
    graph_parts = (
        tile_vals[0],
        tile_rows[0],
        tile_cols[0],
        hub_ids,
        send_list,
        edge_matrix,
        global_ids,
    )
    aggregated = spread(features, graph_parts, False).astype(jnp.bfloat16)
    hidden = jnp.dot(aggregated, weight, preferred_element_type=jnp.float32)
    activated = jax.nn.silu(hidden).astype(jnp.bfloat16)
    hidden_grad = (cotangent.astype(jnp.float32) * silu_slope(hidden)).astype(jnp.bfloat16)
    upstream = jnp.einsum(
        "vj,ij->vi", hidden_grad, weight, preferred_element_type=jnp.float32
    ).astype(jnp.bfloat16)
    feature_grad = spread(upstream, graph_parts, True).astype(jnp.bfloat16)
    row_share = weight.shape[0] // peers
    node_count = features.shape[0] * peers * lax.axis_size("grp")
    full_grad = jnp.einsum("vi,vj->ij", aggregated, hidden_grad, preferred_element_type=jnp.float32)
    summed = lax.psum(full_grad, ("grp", "dev"))
    own_rows = lax.dynamic_slice_in_dim(summed, lax.axis_index("dev") * row_share, row_share, 0)
    weight_grad = own_rows * (1.0 / math.sqrt(node_count))
    return (activated, feature_grad, weight_grad)


def solution(mesh):
    placed = (
        P(("grp", "dev"), None),
        P(),
        P(("grp", "dev"), None),
        P(("grp", "dev"), None, None, None),
        P(("grp", "dev"), None),
        P(("grp", "dev"), None),
        P(("grp", "dev"), None),
        P(("grp", "dev"), None, None),
        P(("grp", "dev"), None),
        P(("grp", "dev"), None),
        P(("grp", "dev"), None),
    )
    return jax.shard_map(
        local,
        mesh=mesh,
        in_specs=placed,
        out_specs=(P(("grp", "dev"), None), P(("grp", "dev"), None), P("dev", None)),
        check_vma=False,
    )
```

profile of v0, /device:TPU:2, one launch (start us, length us, event | category | flops | bytes accessed | tf_op | source)
XLA Modules:
  0.0 758.4 jit_solution(14424132734868286163)
XLA Ops:
  7.2 0.0 copy-start
  7.2 0.0 all-gather.5.cloned.1.call-start
  7.2 0.7 fusion.23
  8.0 2.6 gather_fusion.1
  10.5 0.0 all-gather.5.cloned.1.call-update
  10.6 1.4 copy.26
  11.9 12.1 %all-to-all-start = ((s32[64,1,8]{2,1,0:T(1,128)}), s32[64,1,8]{2,1,0:T(1,128)S(1)}, u32[]{:S(2)}, u32[]{:S(2)}) async-start(s32[64,1,8]{2,1,0:T(1,128)} %bitcast.13), calls=%async_computation | async-start | bytes 65536 | tf_op jit(solution)/shard_map/all_to_all | solution.py:81
  24.1 0.0 reduce-scatter.3.cloned.1.call-start
  24.1 1.0 compare_select_fusion
  25.1 0.9 multiply_reduce_fusion
  26.0 1.0 and_reduce_fusion
  27.0 88.2 %scatter_custom_fusion = f32[1048576]{0:T(1024)} fusion(s32[16384]{0:T(1024)S(1)} %broadcast_select_fusion, f32[16384]{0:T(1024)} %bitcast.74, f32[]{:T(128)} %constant.13.clone.1), kind=kCustom, calls=%fused_computation.19 | custom fusion | flops 16384 | bytes 4194816
  115.3 5.0 reshape.221
  120.3 0.0 copy-done.1
  120.3 5.6 fusion.27
  125.9 0.1 add.133
  126.0 0.1 add.137
  126.1 0.0 all-to-all-done
  126.1 0.1 broadcast_maximum_fusion
  126.2 0.1 max.30
  126.3 0.0 copy-start.5
  126.3 3.3 fusion.1
  129.6 0.0 reduce-scatter.3.cloned.1.call-update
  129.6 0.2 all-reduce.2.cloned.1.call-start
  129.9 0.1 add.134
  130.0 0.0 copy-done.5
  130.0 2.0 gather_fusion
  132.0 0.0 copy-done
  132.0 4.3 convolution_bitcast_fusion.1
  136.4 5.5 copy.24
  141.9 0.0 copy-done.4
  141.9 3.8 fusion.15
  145.7 2.5 copy.25
  148.2 0.1 max.28
  148.3 0.0 all-gather.5.cloned.1.call-done
  148.4 2.9 gather_fusion.2
  151.3 0.0 copy-start.3
  151.3 4.3 fusion.26
  155.6 116.1 %reduce-scatter.3.cloned.1.call-done = f32[32,256]{1,0:T(8,128)} async-done(((f32[2048,256]{1,0:T(8,128)}), f32[32,256]{1,0:T(8,128)}) %reduce-scatter.3.cloned.1.call-update) | async-done | bytes 32784 | tf_op jit(solution)/shard_map/reduce_scatter | solution.py:42
  271.6 0.0 copy-done.3
  271.6 2.7 fusion.4
  274.4 2.1 multiply_convert_fusion
  276.5 1.2 fusion.30
  277.6 0.0 all-reduce.2.cloned.1.call-update
  277.7 0.0 all-gather.7.cloned.1.call-start
  277.7 0.5 convolution_convert_fusion
  278.2 1.2 gather_fusion.4
  279.4 0.0 all-gather.7.cloned.1.call-update
  279.4 0.3 reduce-scatter.5.cloned.1.call-start
  279.7 5.6 fusion.29
  285.3 3.3 fusion
  288.6 0.0 reduce-scatter.5.cloned.1.call-update
  288.7 2.0 gather_fusion.3
  290.7 4.3 convolution_bitcast_fusion
  295.0 5.5 copy.28
  300.5 3.8 fusion.18
  304.3 2.5 copy.29
  306.9 220.4 %all-reduce.2.cloned.1.call-done = f32[256,256]{1,0:T(8,128)} async-done(((f32[256,256]{1,0:T(8,128)}), f32[256,256]{1,0:T(8,128)}) %all-reduce.2.cloned.1.call-update) | async-done | bytes 262160 | tf_op jit(solution)/shard_map/psum | solution.py:104
  527.3 1.3 dynamic-slice_multiply_fusion
  528.6 76.8 %all-gather.7.cloned.1.call-done = bf16[2048,256]{1,0:T(8,128)(2,1)} async-done(((bf16[32,256]{1,0:T(8,128)(2,1)}), bf16[2048,256]{1,0:T(8,128)(2,1)}) %all-gather.7.cloned.1.call-update) | async-done | bytes 1048592 | tf_op jit(solution)/shard_map/all_gather | solution.py:37
  605.4 2.9 gather_fusion.5
  608.3 4.2 fusion.28
  612.6 135.8 %reduce-scatter.5.cloned.1.call-done = f32[32,256]{1,0:T(8,128)} async-done(((f32[2048,256]{1,0:T(8,128)}), f32[32,256]{1,0:T(8,128)}) %reduce-scatter.5.cloned.1.call-update) | async-done | bytes 32784 | tf_op jit(solution)/shard_map/reduce_scatter | solution.py:42
  748.4 3.6 fusion.5
  (16 shorter events, 0.1 us)
Async XLA Ops:
  7.2 124.9 %copy-start = (bf16[1,32,128,128]{3,2,1,0:T(8,128)(2,1)S(1)}, bf16[1,32,128,128]{3,2,1,0:T(8,128)(2,1)}, u32[]{:S(2)}) copy-start(bf16[1,32,128,128]{3,2,1,0:T(8,128)(2,1)} %param.14) | copy-start | bytes 3145732
  7.2 141.2 %all-gather.5.cloned.1.call-start = ((), (), s32[]{:S(2)}) async-start(), calls=%async_computation.6 | async-start | bytes 1064960 | tf_op jit(solution)/shard_map/all_gather | solution.py:37
  11.9 114.1 %all-to-all-start = ((s32[64,1,8]{2,1,0:T(1,128)}), s32[64,1,8]{2,1,0:T(1,128)S(1)}, u32[]{:S(2)}, u32[]{:S(2)}) async-start(s32[64,1,8]{2,1,0:T(1,128)} %bitcast.13), calls=%async_computation | async-start | bytes 65536 | tf_op jit(solution)/shard_map/all_to_all | solution.py:81
  24.1 247.6 %reduce-scatter.3.cloned.1.call-start = ((), (), s32[]{:S(2)}) async-start(), calls=%async_computation.3 | async-start | bytes 2129920 | tf_op jit(solution)/shard_map/reduce_scatter | solution.py:42
  115.3 5.0 copy-start.1
  126.3 3.7 copy-start.5
  129.6 397.7 %all-reduce.2.cloned.1.call-start = ((), (), s32[]{:S(2)}) async-start(), calls=%async_computation.5 | async-start | bytes 524288 | tf_op jit(solution)/shard_map/psum | solution.py:104
  136.4 5.5 copy-start.4
  151.3 120.3 %copy-start.3 = (s32[1,32]{1,0:T(1,128)S(1)}, s32[1,32]{1,0:T(1,128)}, u32[]{:S(2)}) copy-start(s32[1,32]{1,0:T(1,128)} %param.17) | copy-start | bytes 388
  271.6 2.7 copy-start.2
  271.6 2.7 copy-start.6
  277.7 327.7 %all-gather.7.cloned.1.call-start = ((), (), s32[]{:S(2)}) async-start(), calls=%async_computation.7 | async-start | bytes 1064960 | tf_op jit(solution)/shard_map/all_gather | solution.py:37
  279.4 468.9 %reduce-scatter.5.cloned.1.call-start = ((), (), s32[]{:S(2)}) async-start(), calls=%async_computation.4 | async-start | bytes 2129920 | tf_op jit(solution)/shard_map/reduce_scatter | solution.py:42
Sparse Core Ops, SparseCore 0:
  11.4 79.3 all-gather.4
  129.8 141.8 reduce-scatter.2
  278.6 248.6 all-reduce.1
  530.3 75.0 all-gather.6
  609.8 138.4 reduce-scatter.4
where the time goes:
time: 759 us; the launch traced here: 758 us
  waiting for transfers between devices  549 us (72%)
  other arithmetic  93.3 us (12%)
  matrix products  52.6 us (7%)
  local copies, waits for them, and re-layouts  36.6 us (5%)
  between operations  14 us (2%)
  starting transfers between devices  12.7 us (2%)
    reduce_scatter x2, waiting for transfers between devices, hub_part(): own_share = lax.psum_scatter(by_hub, 'dev', scatter_dimension=0, tiled=True)  252 us
    psum x1, waiting for transfers between devices, local(): summed = lax.psum(full_grad, ('grp', 'dev'))  220 us
    unnamed x4, other arithmetic  90.1 us
    all_gather x2, waiting for transfers between devices, hub_part(): all_hubs = lax.all_gather(signal[hub_ids], 'dev', axis=0, tiled=True)  76.8 us
  transfers between devices with their start and end apart: 6, of which 4 were waited for; matrix products, arithmetic and copies ran while one was open for 22% of the time, Pallas kernels for 0%

commit v1 on v0

v1 whole, which is shorter than its diff:
```python
import functools
import math

import jax
import jax.numpy as jnp
from jax import lax
from jax.experimental import pallas as pl
from jax.experimental.pallas import tpu as pltpu
from jax.sharding import PartitionSpec as P

BF16, F32, I32 = jnp.bfloat16, jnp.float32, jnp.int32
LEVELS = 4095.0
UNROLL = 16
NT = (((1,), (1,)), ((), ()))
TN = (((0,), (0,)), ((), ()))


def dot(a, b, dims=(((1,), (0,)), ((), ()))):
    return lax.dot_general(a, b, dims, preferred_element_type=F32)


def sorted_keys(x):
    n = len(x)
    sub = lax.broadcasted_iota(I32, (8, 128), 0)
    lane = lax.broadcasted_iota(I32, (8, 128), 1)

    def bit(k):
        return ((sub >> (k - 4)) & 1) if k < 7 else ((lane >> (k - 7)) & 1)

    def flips(k, i):
        if k >= 14:
            return 0
        if k < 4:
            return -((i >> k) & 1)
        return -bit(k)

    x = list(x)
    state = [0] * n
    for k in range(1, 15):
        for i in range(n):
            new = flips(k, i)
            change = new ^ state[i]
            if not isinstance(change, int):
                x[i] = x[i] ^ change
            elif change:
                x[i] = ~x[i]
            state[i] = new
        for j in reversed(range(k)):
            if k == 14 and j < 7:
                break
            if j < 4:
                d = 1 << j
                for i in range(n):
                    if not i & d:
                        x[i], x[i + d] = jnp.minimum(x[i], x[i + d]), jnp.maximum(x[i], x[i + d])
            else:
                axis, size, d = (0, 8, 1 << (j - 4)) if j < 7 else (1, 128, 1 << (j - 7))
                high = bit(j) == 1
                for i in range(n):
                    down = pltpu.roll(x[i], d, axis)
                    up = down if 2 * d == size else pltpu.roll(x[i], size - d, axis)
                    x[i] = jnp.where(high, jnp.maximum(x[i], down), jnp.minimum(x[i], up))
    return x


def pair_table(x):
    lane = lax.broadcasted_iota(I32, (8, 128), 1)
    first = jnp.zeros((8, 128), I32)
    window, bucket = lane, first
    for b in range(1, 16):
        below = functools.reduce(jnp.add, [(xi < (b - 8) * (1 << 28)).astype(F32) for xi in x])
        count = jnp.sum(jnp.sum(below, axis=0, keepdims=True), axis=1, keepdims=True)
        count = jnp.broadcast_to(count.astype(I32), (8, 128))
        first = first + (count <= 256 * lane).astype(I32)
        here = lane == 63 + b
        window = jnp.where(here, jnp.minimum(count >> 8, 63), window)
        bucket = jnp.where(here, jnp.where((count & 255) != 0, b, -1), bucket)
    bucket = jnp.where(lane < 64, first, jnp.where(lane < 79, bucket, -1))
    window = jnp.where(lane < 79, window, 0)
    return jnp.where(lax.broadcasted_iota(I32, (8, 128), 0) == 0, window, bucket)


def one_hot(mask):
    return jnp.where(mask, 1.0, 0.0).astype(BF16)


def hub_copies(signal, hub_row, send_row):
    hubs, rows = hub_row.shape[1], signal.shape[0]
    square = jnp.broadcast_to(hub_row, (hubs, hubs)).astype(F32)
    diagonal = lax.broadcasted_iota(I32, (hubs, hubs), 0) == lax.broadcasted_iota(I32, (hubs, hubs), 1)
    hub_col = jnp.sum(jnp.where(diagonal, square, 0.0), axis=1, keepdims=True).astype(I32)
    pick = one_hot(lax.broadcasted_iota(I32, (hubs, rows), 1) == hub_col)
    hub_values = dot(pick, signal).astype(BF16)
    return dot(slot_matrix(hubs, send_row), hub_values, TN)


def slot_matrix(hubs, send_row):
    return one_hot(lax.broadcasted_iota(I32, (hubs, send_row.shape[1]), 0) == send_row)


def packed(copies, partial):
    columns = copies.shape[1]
    both = jnp.concatenate([copies.reshape(-1, 8, columns), partial.reshape(-1, 8, columns)], axis=1)
    return both.astype(BF16)


def unpacked(received):
    both = received.astype(F32)
    columns = both.shape[-1]
    return both[:, :8].reshape(-1, columns).astype(BF16), both[:, 8:].reshape(-1, columns).astype(BF16)


def edge_kernel(target_ref, slot_ref, strength_ref, signal_ref, hub_ref, send_ref, matrix_ref, matrix_t_ref, out_ref,
                keys, total, table, table_smem, sem):
    x = []
    for i in range(16):
        row, slot = target_ref[8 * i:8 * i + 8, :], slot_ref[8 * i:8 * i + 8, :]
        level = jnp.round(strength_ref[8 * i:8 * i + 8, :] * LEVELS).astype(I32)
        x.append((((row >> 8) - 4) << 29) | ((slot >> 8) << 28) | ((row & 255) << 20) | ((slot & 255) << 12) | level)
    table[...] = pair_table(x)
    copy = pltpu.make_async_copy(table, table_smem, sem)
    copy.start()
    total[...] = jnp.zeros_like(total)
    keys[...] = jnp.concatenate(sorted_keys(x), axis=0).T
    copy.wait()
    place = lax.broadcasted_iota(I32, (256, 128), 0).astype(F32).astype(BF16)

    def spread(row):
        return jnp.broadcast_to(row.astype(F32), (256, 128)).astype(BF16)

    def product(n):
        window, bucket = table_smem[0, n], table_smem[1, n]
        left, right = [], []
        for half in range(2):
            key = keys[pl.ds(2 * window + half, 1), :]
            row = jnp.where((key >> 28) + 8 == bucket, (key >> 20) & 255, -1)
            level = (key & 4095).astype(F32) * (1.0 / LEVELS)
            left.append(jnp.where(place == spread(row), spread(level), jnp.zeros((), BF16)))
            right.append(jnp.where(place == spread((key >> 12) & 255), jnp.ones((), BF16), jnp.zeros((), BF16)))
        return jnp.maximum(bucket, 0), dot(jnp.concatenate(left, axis=1), jnp.concatenate(right, axis=1), NT)

    def step(i, carry):
        for bucket, value in [product(i * UNROLL + u) for u in range(UNROLL)]:
            total[bucket] += value
        return carry

    lax.fori_loop(0, 80 // UNROLL, step, 0)
    eye = one_hot(lax.broadcasted_iota(I32, (256, 256), 0) == lax.broadcasted_iota(I32, (256, 256), 1))
    for i in range(8):
        for j in range(2):
            tile = total[2 * i + j].astype(BF16)
            matrix_ref[256 * i:256 * i + 256, 256 * j:256 * j + 256] = tile
            matrix_t_ref[256 * j:256 * j + 256, 256 * i:256 * i + 256] = dot(eye, tile, NT).astype(BF16)
    signal = signal_ref[...]
    out_ref[...] = packed(hub_copies(signal, hub_ref[...], send_ref[...]), dot(matrix_t_ref[...], signal))


def tile_kernel(transpose, tiles_ref, from_ref, to_ref, signal_ref, out_ref):
    out_ref[...] = jnp.zeros_like(out_ref)
    for t in range(tiles_ref.shape[0]):
        source = signal_ref[pl.ds(pl.multiple_of(from_ref[0, t] * 128, 128), 128), :]
        value = dot(tiles_ref[t], source, TN) if transpose else dot(tiles_ref[t], source)
        out_ref[pl.ds(pl.multiple_of(to_ref[0, t] * 128, 128), 128), :] += value


def layer_kernel(received_ref, matrix_ref, matrix_t_ref, near_ref, cotangent_ref, weight_ref, hub_ref, send_ref,
                 hub_smem, activated_ref, upstream_ref, grad_ref, out_ref, total):
    mirrored, returned = unpacked(received_ref[...])
    hubs = hub_ref.shape[1]
    back = dot(slot_matrix(hubs, send_ref[...]), returned)
    for i in range(8):
        rows = slice(256 * i, 256 * i + 256)
        total[rows, :] = near_ref[rows, :] + dot(matrix_ref[rows, :], mirrored)
    for h in range(hubs):
        total[pl.ds(hub_smem[0, h], 1), :] += back[h:h + 1, :]
    weight = weight_ref[...]
    grad = None
    for i in range(8):
        rows = slice(256 * i, 256 * i + 256)
        aggregated = total[rows, :].astype(BF16)
        hidden = dot(aggregated, weight)
        logistic = jax.nn.sigmoid(hidden)
        activated_ref[rows, :] = (hidden * logistic).astype(BF16)
        slope = logistic * (1.0 + hidden * (1.0 - logistic))
        hidden_grad = (cotangent_ref[rows, :].astype(F32) * slope).astype(BF16)
        term = dot(aggregated, hidden_grad, TN)
        grad = term if grad is None else grad + term
        upstream_ref[rows, :] = dot(hidden_grad, weight, NT).astype(BF16)
    grad_ref[...] = grad.astype(BF16)
    upstream = upstream_ref[...]
    out_ref[...] = packed(hub_copies(upstream, hub_ref[...], send_ref[...]), dot(matrix_t_ref[...], upstream))


def final_kernel(received_ref, matrix_ref, near_ref, send_ref, hub_smem, out_ref, total):
    mirrored, returned = unpacked(received_ref[...])
    hubs = hub_smem.shape[1]
    back = dot(slot_matrix(hubs, send_ref[...]), returned)
    for i in range(8):
        rows = slice(256 * i, 256 * i + 256)
        total[rows, :] = near_ref[rows, :] + dot(matrix_ref[rows, :], mirrored)
    for h in range(hubs):
        total[pl.ds(hub_smem[0, h], 1), :] += back[h:h + 1, :]
    out_ref[...] = total[...].astype(BF16)


def run(kernel, name, operands, outs, scratch=(), smem=(), flops=0):
    specs = [pl.BlockSpec(memory_space=pltpu.SMEM) if i in smem else pl.BlockSpec() for i in range(len(operands))]
    size = sum(math.prod(a.shape) * a.dtype.itemsize for a in operands)
    size += sum(math.prod(s) * jnp.dtype(d).itemsize for s, d in outs)
    return pl.pallas_call(
        kernel,
        out_shape=[jax.ShapeDtypeStruct(s, d) for s, d in outs],
        in_specs=specs,
        out_specs=[pl.BlockSpec() for _ in outs],
        scratch_shapes=list(scratch),
        compiler_params=pltpu.CompilerParams(vmem_limit_bytes=48 << 20),
        cost_estimate=pl.CostEstimate(flops=flops, bytes_accessed=size, transcendentals=0),
        name=name,
    )(*operands)


def exchange(x):
    return lax.all_to_all(x, "dev", split_axis=0, concat_axis=0, tiled=True)


def local(
    features,
    weight,
    cotangent,
    tile_vals,
    tile_rows,
    tile_cols,
    hub_rows,
    send_hub,
    mirror_slot,
    replica_target_row,
    replica_edge_weight,
):
    peers = lax.axis_size("dev")
    groups = lax.axis_size("grp")
    rows, columns = features.shape
    send = send_hub.reshape(1, -1)
    slots = send.shape[1]
    tiles = tile_vals[0]
    square = (128, 128)

    matrix, matrix_t, outgoing = run(
        edge_kernel, "edges",
        (replica_target_row.reshape(square), mirror_slot.reshape(square), replica_edge_weight.reshape(square),
         features, hub_rows, send),
        [((rows, slots), BF16), ((slots, rows), BF16), ((peers, 16, columns), BF16)],
        [pltpu.VMEM(square, I32), pltpu.VMEM((16, 256, 256), F32), pltpu.VMEM((8, 128), I32),
         pltpu.SMEM((8, 128), I32), pltpu.SemaphoreType.DMA],
        flops=1 << 33,
    )
    received = exchange(outgoing)
    (near,) = run(
        functools.partial(tile_kernel, False), "tiles", (tiles, tile_cols, tile_rows, features),
        [((rows, columns), F32)], smem=(1, 2), flops=1 << 31,
    )
    activated, upstream, grad, outgoing = run(
        layer_kernel, "layer",
        (received, matrix, matrix_t, near, cotangent, weight, hub_rows, send, hub_rows),
        [((rows, columns), BF16), ((rows, columns), BF16), (weight.shape, BF16), ((peers, 16, columns), BF16)],
        [pltpu.VMEM((rows, columns), F32)], smem=(8,), flops=1 << 32,
    )
    received = exchange(outgoing)
    (near,) = run(
        functools.partial(tile_kernel, True), "tiles_t", (tiles, tile_rows, tile_cols, upstream),
        [((rows, columns), F32)], smem=(1, 2), flops=1 << 31,
    )
    share = weight.shape[0] // peers
    own = jnp.sum(exchange(grad.reshape(peers, share, -1)).astype(F32), axis=0)
    scale = 1.0 / math.sqrt(rows * peers * groups)
    weight_grad = own
    for shift in range(1, groups):
        weight_grad = weight_grad + lax.ppermute(own, "grp", [(g, (g + shift) % groups) for g in range(groups)])
    weight_grad = weight_grad * scale
    (feature_grad,) = run(
        final_kernel, "final", (received, matrix, near, send, hub_rows), [((rows, columns), BF16)],
        [pltpu.VMEM((rows, columns), F32)], smem=(4,), flops=1 << 31,
    )
    return (activated, feature_grad, weight_grad)


def solution(mesh):
    placed = (
        P(("grp", "dev"), None),
        P(),
        P(("grp", "dev"), None),
        P(("grp", "dev"), None, None, None),
        P(("grp", "dev"), None),
        P(("grp", "dev"), None),
        P(("grp", "dev"), None),
        P(("grp", "dev"), None, None),
        P(("grp", "dev"), None),
        P(("grp", "dev"), None),
        P(("grp", "dev"), None),
    )
    return jax.shard_map(
        local,
        mesh=mesh,
        in_specs=placed,
        out_specs=(P(("grp", "dev"), None), P(("grp", "dev"), None), P("dev", None)),
        check_vma=False,
    )
```

time: 759 us -> 105 us (0.14)
  waiting for transfers between devices: 549 us -> 21.7 us
  other arithmetic: 93.3 us -> 0.69 us
  matrix products: 52.6 us -> 0 us
  Pallas kernels: 0 us -> 22.5 us
  local copies, waits for them, and re-layouts: 36.6 us -> 18.8 us
  blocking collectives: 0 us -> 16.6 us
  between operations: 14 us -> 0.77 us
  starting transfers between devices: 12.7 us -> 21.7 us
    reduce_scatter x2 -> x0, waiting for transfers between devices: 252 us -> none  [hub_part(): own_share = lax.psum_scatter(by_hub, 'dev', scatter_dimension=0, tiled=True)]
    psum x1 -> x0, waiting for transfers between devices: 220 us -> none  [local(): summed = lax.psum(full_grad, ('grp', 'dev'))]
    unnamed x4 -> x0, other arithmetic: 90.1 us -> none
    all_gather x2 -> x0, waiting for transfers between devices: 76.8 us -> none  [hub_part(): all_hubs = lax.all_gather(signal[hub_ids], 'dev', axis=0, tiled=True)]
    dot_general x15 -> x0, matrix products: 52.6 us -> none  [the longest x2 11.2 us: hub_part(): jnp.einsum('vk,vf->kf', edge_matrix, signal.astype(jnp.float32), precisio...]
    pallas_call x0 -> x5, Pallas kernels: none -> 22.5 us  [run(): pl.pallas_call(kernel, out_shape=[jax.ShapeDtypeStruct(s, d) for s, d in...]
    all_to_all x1 -> x2, waiting for transfers between devices: 0.01 us -> 21.7 us  [exchange(): return lax.all_to_all(x, 'dev', split_axis=0, concat_axis=0, tiled=True)]
    unnamed x15 -> x45, local copies, waits for them, and re-layouts: 1.42 us -> 18.7 us
  transfers between devices with their start and end apart: 6 -> 5, of which waited for: 4 -> 2; matrix products, arithmetic and copies ran while one was open for 22% -> 1% of each run, Pallas kernels for 0% -> 3%
where the time goes in v1:
time: 105 us; the launch traced here: 103 us
  Pallas kernels  22.5 us (21%)
  starting transfers between devices  21.7 us (21%)
  waiting for transfers between devices  21.7 us (21%)
  local copies, waits for them, and re-layouts  18.8 us (18%)
  blocking collectives  16.6 us (16%)
    pallas_call x5, Pallas kernels, run(): pl.pallas_call(kernel, out_shape=[jax.ShapeDtypeStruct(s, d) for s, d in...  22.5 us
    all_to_all x2, waiting for transfers between devices, exchange(): return lax.all_to_all(x, 'dev', split_axis=0, concat_axis=0, tiled=True)  21.7 us
    unnamed x45, local copies, waits for them, and re-layouts  18.7 us
    all_to_all x2, starting transfers between devices, exchange(): return lax.all_to_all(x, 'dev', split_axis=0, concat_axis=0, tiled=True)  16.7 us
    all_to_all x1, blocking collectives, exchange(): return lax.all_to_all(x, 'dev', split_axis=0, concat_axis=0, tiled=True)  16.6 us
    ppermute x3, starting transfers between devices, local(): lax.ppermute(own, 'grp', [(g, (g + shift) % groups) for g in range(groups)])  5 us
  transfers between devices with their start and end apart: 5, of which 2 were waited for; matrix products, arithmetic and copies ran while one was open for 1% of the time, Pallas kernels for 3%

profile of v1, /device:TPU:2, one launch (start us, length us, event | category | flops | bytes accessed | tf_op | source)
XLA Modules:
  0.0 102.8 jit_solution(12722766326028634798)
XLA Ops:
  0.6 0.8 copy.15
  1.4 0.1 reshape.24.send_ref
  1.5 0.0 copy-start
  1.5 1.2 %copy-done = bf16[2048,256]{1,0:T(8,128)(2,1)S(1)} copy-done((bf16[2048,256]{1,0:T(8,128)(2,1)S(1)}, bf16[2048,256]{1,0:T(8,128)(2,1)}, u32[]{:S(2)}) %copy-start) | copy-done | bytes 1048600
  2.7 0.0 copy-start.6
  2.7 0.8 copy-done.6
  3.6 0.0 copy-start.7
  3.6 0.8 copy-done.7
  4.4 0.0 copy-start.8
  4.4 0.8 copy-done.8
  5.2 0.0 copy-start.11
  5.2 0.7 copy-done.11
  5.9 0.0 copy-start.1
  5.9 0.0 copy-start.9
  5.9 0.0 copy-start.10
  5.9 10.3 %edges.1 = (bf16[2048,512]{1,0:T(8,128)(2,1)S(1)}, bf16[512,2048]{1,0:T(8,128)(2,1)S(1)}, bf16[64,16,256]{2,1,0:T(8,128)(2,1)}) custom-call(s32[128,128]{1,0:T(8,128)S(1)} %bitcast.6, s32[128,128]{1,0:T(8,128)S(1)} %bitcast.7, f32[128,128]{1,0:T(8,128)S(1)} %bitcast.8, bf16[2048,256]{1,0:T(8,128)(2,1)S(1)} %copy-done, s32[1,32]{1,0:T(1,128)S(1)} %copy-done.11, ...), custom_call_target="tpu_custom_call" | custom-call | flops 8589934592 | bytes 5965952 | tf_op jit(solution)/shard_map/edges/pallas_call | solution.py:210
  16.2 0.0 copy-start.13
  16.2 1.3 %copy-done.13 = bf16[2048,512]{1,0:T(8,128)(2,1)} copy-done((bf16[2048,512]{1,0:T(8,128)(2,1)}, bf16[2048,512]{1,0:T(8,128)(2,1)S(1)}, u32[]{:S(2)}) %copy-start.13) | copy-done | bytes 2097176
  17.5 0.0 copy-start.21
  17.5 1.3 %copy-done.21 = bf16[512,2048]{1,0:T(8,128)(2,1)} copy-done((bf16[512,2048]{1,0:T(8,128)(2,1)}, bf16[512,2048]{1,0:T(8,128)(2,1)S(1)}, u32[]{:S(2)}) %copy-start.21) | copy-done | bytes 2097176
  18.8 12.1 %all-to-all-start = ((bf16[64,16,256]{2,1,0:T(8,128)(2,1)}), bf16[64,16,256]{2,1,0:T(8,128)(2,1)S(1)}, u32[]{:S(2)}, u32[]{:S(2)}) async-start(bf16[64,16,256]{2,1,0:T(8,128)(2,1)} %get-tuple-element.10), calls=%async_computation | async-start | bytes 1048576 | tf_op jit(solution)/shard_map/all_to_all | solution.py:223
  30.9 0.0 copy-done.1
  31.0 0.0 copy-done.9
  31.0 0.0 copy-done.10
  31.0 0.0 copy-start.3
  31.0 1.2 %copy-done.3 = bf16[1,32,128,128]{3,2,1,0:T(8,128)(2,1)S(1)} copy-done((bf16[1,32,128,128]{3,2,1,0:T(8,128)(2,1)S(1)}, bf16[1,32,128,128]{3,2,1,0:T(8,128)(2,1)}, u32[]{:S(2)}) %copy-start.3) | copy-done | bytes 1048600
  32.2 0.0 copy-start.2
  32.2 0.0 copy-start.5
  32.2 0.0 copy-start.12
  32.2 1.3 %tiles.1.near_ref = f32[2048,256]{1,0:T(8,128)S(1)} custom-call(bf16[32,128,128]{2,1,0:T(8,128)(2,1)S(1)} %bitcast.4, s32[1,32]{1,0:T(1,128)S(1)} %copy-done.9, s32[1,32]{1,0:T(1,128)S(1)} %copy-done.10, bf16[2048,256]{1,0:T(8,128)(2,1)S(1)} %copy-done.1), custom_call_target="tpu_custom_call" | custom-call | flops 2147483648 | bytes 4194560 | tf_op jit(solution)/shard_map/tiles/pallas_call | solution.py:210
  33.6 0.0 copy-start.18
  33.6 1.3 %copy-done.18 = f32[2048,256]{1,0:T(8,128)} copy-done((f32[2048,256]{1,0:T(8,128)}, f32[2048,256]{1,0:T(8,128)S(1)}, u32[]{:S(2)}) %copy-start.18) | copy-done | bytes 2097176
  34.9 13.7 %all-to-all-done.received_ref = bf16[64,16,256]{2,1,0:T(8,128)(2,1)S(1)} async-done(((bf16[64,16,256]{2,1,0:T(8,128)(2,1)}), bf16[64,16,256]{2,1,0:T(8,128)(2,1)S(1)}, u32[]{:S(2)}, u32[]{:S(2)}) %all-to-all-start) | async-done | bytes 524320 | tf_op jit(solution)/shard_map/all_to_all | solution.py:223
  48.6 0.0 copy-done.2
  48.6 0.0 copy-done.5
  48.6 0.0 copy-done.12
  48.6 0.0 copy-start.14
  48.6 1.6 %copy-done.14 = bf16[2048,512]{1,0:T(8,128)(2,1)S(1)} copy-done((bf16[2048,512]{1,0:T(8,128)(2,1)S(1)}, bf16[2048,512]{1,0:T(8,128)(2,1)}, u32[]{:S(2)}) %copy-start.14) | copy-done | bytes 2097176
  50.2 0.0 copy-start.4
  50.2 6.9 %layer.1 = (bf16[2048,256]{1,0:T(8,128)(2,1)}, bf16[2048,256]{1,0:T(8,128)(2,1)S(1)}, bf16[256,256]{1,0:T(8,128)(2,1)S(1)}, bf16[64,16,256]{2,1,0:T(8,128)(2,1)}) custom-call(bf16[64,16,256]{2,1,0:T(8,128)(2,1)S(1)} %all-to-all-done.received_ref, bf16[2048,512]{1,0:T(8,128)(2,1)S(1)} %copy-done.14, bf16[512,2048]{1,0:T(8,128)(2,1)} %copy-done.21, ...), custom_call_target="tpu_custom_call" | custom-call | flops 4294967296 | bytes 10750208 | tf_op jit(solution)/shard_map/layer/pallas_call | solution.py:210
  57.2 0.0 copy-start.19
  57.2 1.0 copy-done.19
  58.2 16.6 %all_to_all.15 = bf16[64,4,256]{2,1,0:T(4,128)(2,1)S(1)} all-to-all(bf16[64,4,256]{2,1,0:T(4,128)(2,1)S(1)} %reshape.25), channel_id=1, replica_groups=mesh['grp'=4,'dev'=64] {'dev'}, dimensions={0} | all-to-all | bytes 262144 | tf_op jit(solution)/shard_map/all_to_all | solution.py:223
  74.8 4.6 %all-to-all-start.1 = ((bf16[64,16,256]{2,1,0:T(8,128)(2,1)}), bf16[64,16,256]{2,1,0:T(8,128)(2,1)S(1)}, u32[]{:S(2)}, u32[]{:S(2)}) async-start(bf16[64,16,256]{2,1,0:T(8,128)(2,1)} %get-tuple-element.14), calls=%async_computation.1 | async-start | bytes 1048576 | tf_op jit(solution)/shard_map/all_to_all | solution.py:223
  79.4 0.1 convert_reduce_fusion
  79.5 0.8 collective-permute-start.2
  80.3 2.4 %collective-permute-start.1 = (f32[4,256]{1,0:T(4,128)S(1)}, f32[4,256]{1,0:T(4,128)S(1)}, u32[]{:S(2)}, u32[]{:S(2)}) collective-permute-start(f32[4,256]{1,0:T(4,128)S(1)} %convert_reduce_fusion), channel_id=1, source_target_pairs={{0,128},{64,192},{128,0},{192,64},{1,129},{65,193},{129,1},{193,65... | collective-permute-start | bytes 12296 | tf_op jit(solution)/shard_map/ppermute | solution.py:277
  82.7 1.8 %collective-permute-start = (f32[4,256]{1,0:T(4,128)S(1)}, f32[4,256]{1,0:T(4,128)S(1)}, u32[]{:S(2)}, u32[]{:S(2)}) collective-permute-start(f32[4,256]{1,0:T(4,128)S(1)} %convert_reduce_fusion), channel_id=1, source_target_pairs={{0,64},{64,128},{128,192},{192,0},{1,65},{65,129},{129,193},{193,1... | collective-permute-start | bytes 12296 | tf_op jit(solution)/shard_map/ppermute | solution.py:277
  84.5 0.0 copy-done.4
  84.5 0.0 copy-start.20
  84.5 1.2 %copy-done.20 = bf16[2048,256]{1,0:T(8,128)(2,1)S(1)} copy-done((bf16[2048,256]{1,0:T(8,128)(2,1)S(1)}, bf16[2048,256]{1,0:T(8,128)(2,1)}, u32[]{:S(2)}) %copy-start.20) | copy-done | bytes 1048600
  85.8 1.4 %tiles_t.1.near_ref = f32[2048,256]{1,0:T(8,128)S(1)} custom-call(bf16[32,128,128]{2,1,0:T(8,128)(2,1)S(1)} %bitcast.5, s32[1,32]{1,0:T(1,128)S(1)} %copy-done.10, s32[1,32]{1,0:T(1,128)S(1)} %copy-done.9, bf16[2048,256]{1,0:T(8,128)(2,1)S(1)} %copy-done.20), custom_call_target="tpu_custom_call" | custom-call | flops 2147483648 | bytes 4194560 | tf_op jit(solution)/shard_map/tiles_t/pallas_call | solution.py:210
  87.2 0.0 copy-start.16
  87.2 1.3 %copy-done.16 = f32[2048,256]{1,0:T(8,128)} copy-done((f32[2048,256]{1,0:T(8,128)}, f32[2048,256]{1,0:T(8,128)S(1)}, u32[]{:S(2)}) %copy-start.16) | copy-done | bytes 2097176
  88.5 0.0 collective-permute-done.2
  88.5 0.0 collective-permute-done.1
  88.5 0.0 collective-permute-done
  88.5 0.6 add_multiply_fusion
  89.1 8.0 %all-to-all-done.1.received_ref = bf16[64,16,256]{2,1,0:T(8,128)(2,1)S(1)} async-done(((bf16[64,16,256]{2,1,0:T(8,128)(2,1)}), bf16[64,16,256]{2,1,0:T(8,128)(2,1)S(1)}, u32[]{:S(2)}, u32[]{:S(2)}) %all-to-all-start.1) | async-done | bytes 524320 | tf_op jit(solution)/shard_map/all_to_all | solution.py:223
  97.1 0.0 copy-start.15
  97.1 1.6 %copy-done.15 = bf16[2048,512]{1,0:T(8,128)(2,1)S(1)} copy-done((bf16[2048,512]{1,0:T(8,128)(2,1)S(1)}, bf16[2048,512]{1,0:T(8,128)(2,1)}, u32[]{:S(2)}) %copy-start.15) | copy-done | bytes 2097176
  98.7 0.0 copy-start.17
  98.7 1.6 %copy-done.17 = f32[2048,256]{1,0:T(8,128)S(1)} copy-done((f32[2048,256]{1,0:T(8,128)S(1)}, f32[2048,256]{1,0:T(8,128)}, u32[]{:S(2)}) %copy-start.17) | copy-done | bytes 2097176
  100.3 2.5 %final.1 = bf16[2048,256]{1,0:T(8,128)(2,1)} custom-call(bf16[64,16,256]{2,1,0:T(8,128)(2,1)S(1)} %all-to-all-done.1.received_ref, bf16[2048,512]{1,0:T(8,128)(2,1)S(1)} %copy-done.15, f32[2048,256]{1,0:T(8,128)S(1)} %copy-done.17, s32[1,512]{1,0:T(1,128)S(1)} %reshape.24.send_ref, s32[1,32]{1,0:T(1,128)S(1)} %copy-done.12), custom_call_target="tpu_custom_call" | custom-call | flops 2147483648 | bytes 5769344 | tf_op jit(solution)/shard_map/final/pallas_call | solution.py:210
  (1 shorter events, 0.0 us)
Async XLA Ops:
  1.5 1.2 %copy-start = (bf16[2048,256]{1,0:T(8,128)(2,1)S(1)}, bf16[2048,256]{1,0:T(8,128)(2,1)}, u32[]{:S(2)}) copy-start(bf16[2048,256]{1,0:T(8,128)(2,1)} %signal_ref.3) | copy-start | bytes 3145732
  2.7 0.8 copy-start.6
  3.6 0.8 copy-start.7
  4.4 0.8 copy-start.8
  5.2 0.7 copy-start.11
  5.9 25.1 %copy-start.1 = (bf16[2048,256]{1,0:T(8,128)(2,1)S(1)}, bf16[2048,256]{1,0:T(8,128)(2,1)}, u32[]{:S(2)}) copy-start(bf16[2048,256]{1,0:T(8,128)(2,1)} %signal_ref.3) | copy-start | bytes 3145732
  5.9 25.1 %copy-start.9 = (s32[1,32]{1,0:T(1,128)S(1)}, s32[1,32]{1,0:T(1,128)}, u32[]{:S(2)}) copy-start(s32[1,32]{1,0:T(1,128)} %to_ref.3) | copy-start | bytes 388
  5.9 25.1 %copy-start.10 = (s32[1,32]{1,0:T(1,128)S(1)}, s32[1,32]{1,0:T(1,128)}, u32[]{:S(2)}) copy-start(s32[1,32]{1,0:T(1,128)} %from_ref.3) | copy-start | bytes 388
  16.2 1.3 %copy-start.13 = (bf16[2048,512]{1,0:T(8,128)(2,1)}, bf16[2048,512]{1,0:T(8,128)(2,1)S(1)}, u32[]{:S(2)}) copy-start(bf16[2048,512]{1,0:T(8,128)(2,1)S(1)} %get-tuple-element.11.matrix_ref) | copy-start | bytes 6291460
  17.5 1.3 %copy-start.21 = (bf16[512,2048]{1,0:T(8,128)(2,1)}, bf16[512,2048]{1,0:T(8,128)(2,1)S(1)}, u32[]{:S(2)}) copy-start(bf16[512,2048]{1,0:T(8,128)(2,1)S(1)} %get-tuple-element.12.matrix_t_ref) | copy-start | bytes 6291460
  18.8 29.8 %all-to-all-start = ((bf16[64,16,256]{2,1,0:T(8,128)(2,1)}), bf16[64,16,256]{2,1,0:T(8,128)(2,1)S(1)}, u32[]{:S(2)}, u32[]{:S(2)}) async-start(bf16[64,16,256]{2,1,0:T(8,128)(2,1)} %get-tuple-element.10), calls=%async_computation | async-start | bytes 1048576 | tf_op jit(solution)/shard_map/all_to_all | solution.py:223
  31.0 1.2 %copy-start.3 = (bf16[1,32,128,128]{3,2,1,0:T(8,128)(2,1)S(1)}, bf16[1,32,128,128]{3,2,1,0:T(8,128)(2,1)}, u32[]{:S(2)}) copy-start(bf16[1,32,128,128]{3,2,1,0:T(8,128)(2,1)} %param.14) | copy-start | bytes 3145732
  32.2 16.4 %copy-start.2 = (bf16[2048,256]{1,0:T(8,128)(2,1)S(1)}, bf16[2048,256]{1,0:T(8,128)(2,1)}, u32[]{:S(2)}) copy-start(bf16[2048,256]{1,0:T(8,128)(2,1)} %cotangent_ref.1) | copy-start | bytes 3145732
  32.2 16.4 %copy-start.5 = (bf16[256,256]{1,0:T(8,128)(2,1)S(1)}, bf16[256,256]{1,0:T(8,128)(2,1)}, u32[]{:S(2)}) copy-start(bf16[256,256]{1,0:T(8,128)(2,1)} %weight_ref.1) | copy-start | bytes 393220
  32.2 16.4 %copy-start.12 = (s32[1,32]{1,0:T(1,128)S(1)}, s32[1,32]{1,0:T(1,128)}, u32[]{:S(2)}) copy-start(s32[1,32]{1,0:T(1,128)} %hub_smem.3) | copy-start | bytes 388
  33.6 1.4 %copy-start.18 = (f32[2048,256]{1,0:T(8,128)}, f32[2048,256]{1,0:T(8,128)S(1)}, u32[]{:S(2)}) copy-start(f32[2048,256]{1,0:T(8,128)S(1)} %tiles.1.near_ref) | copy-start | bytes 6291460
  48.6 1.6 %copy-start.14 = (bf16[2048,512]{1,0:T(8,128)(2,1)S(1)}, bf16[2048,512]{1,0:T(8,128)(2,1)}, u32[]{:S(2)}) copy-start(bf16[2048,512]{1,0:T(8,128)(2,1)} %copy-done.13) | copy-start | bytes 6291460
  50.2 34.3 %copy-start.4 = (bf16[1,32,128,128]{3,2,1,0:T(8,128)(2,1)S(1)}, bf16[1,32,128,128]{3,2,1,0:T(8,128)(2,1)}, u32[]{:S(2)}) copy-start(bf16[1,32,128,128]{3,2,1,0:T(8,128)(2,1)} %param.14) | copy-start | bytes 3145732
  57.2 1.0 copy-start.19
  74.8 22.3 %all-to-all-start.1 = ((bf16[64,16,256]{2,1,0:T(8,128)(2,1)}), bf16[64,16,256]{2,1,0:T(8,128)(2,1)S(1)}, u32[]{:S(2)}, u32[]{:S(2)}) async-start(bf16[64,16,256]{2,1,0:T(8,128)(2,1)} %get-tuple-element.14), calls=%async_computation.1 | async-start | bytes 1048576 | tf_op jit(solution)/shard_map/all_to_all | solution.py:223
  79.5 9.0 %collective-permute-start.2 = (f32[4,256]{1,0:T(4,128)S(1)}, f32[4,256]{1,0:T(4,128)S(1)}, u32[]{:S(2)}, u32[]{:S(2)}) collective-permute-start(f32[4,256]{1,0:T(4,128)S(1)} %convert_reduce_fusion), channel_id=1, source_target_pairs={{0,192},{64,0},{128,64},{192,128},{1,193},{65,1},{129,65},{193,129... | collective-permute-start | bytes 12296 | tf_op jit(solution)/shard_map/ppermute | solution.py:277
  80.3 8.2 %collective-permute-start.1 = (f32[4,256]{1,0:T(4,128)S(1)}, f32[4,256]{1,0:T(4,128)S(1)}, u32[]{:S(2)}, u32[]{:S(2)}) collective-permute-start(f32[4,256]{1,0:T(4,128)S(1)} %convert_reduce_fusion), channel_id=1, source_target_pairs={{0,128},{64,192},{128,0},{192,64},{1,129},{65,193},{129,1},{193,65... | collective-permute-start | bytes 12296 | tf_op jit(solution)/shard_map/ppermute | solution.py:277
  82.7 5.8 %collective-permute-start = (f32[4,256]{1,0:T(4,128)S(1)}, f32[4,256]{1,0:T(4,128)S(1)}, u32[]{:S(2)}, u32[]{:S(2)}) collective-permute-start(f32[4,256]{1,0:T(4,128)S(1)} %convert_reduce_fusion), channel_id=1, source_target_pairs={{0,64},{64,128},{128,192},{192,0},{1,65},{65,129},{129,193},{193,1... | collective-permute-start | bytes 12296 | tf_op jit(solution)/shard_map/ppermute | solution.py:277
  84.5 1.2 %copy-start.20 = (bf16[2048,256]{1,0:T(8,128)(2,1)S(1)}, bf16[2048,256]{1,0:T(8,128)(2,1)}, u32[]{:S(2)}) copy-start(bf16[2048,256]{1,0:T(8,128)(2,1)} %copy-done.19) | copy-start | bytes 3145732
  87.2 1.3 %copy-start.16 = (f32[2048,256]{1,0:T(8,128)}, f32[2048,256]{1,0:T(8,128)S(1)}, u32[]{:S(2)}) copy-start(f32[2048,256]{1,0:T(8,128)S(1)} %tiles_t.1.near_ref) | copy-start | bytes 6291460
  97.1 1.6 %copy-start.15 = (bf16[2048,512]{1,0:T(8,128)(2,1)S(1)}, bf16[2048,512]{1,0:T(8,128)(2,1)}, u32[]{:S(2)}) copy-start(bf16[2048,512]{1,0:T(8,128)(2,1)} %copy-done.13) | copy-start | bytes 6291460
  98.7 1.6 %copy-start.17 = (f32[2048,256]{1,0:T(8,128)S(1)}, f32[2048,256]{1,0:T(8,128)}, u32[]{:S(2)}) copy-start(f32[2048,256]{1,0:T(8,128)} %copy-done.16) | copy-start | bytes 6291460

commit v2 on v1

v2 whole, which is shorter than its diff:
```python
import functools
import math

import jax
import jax.numpy as jnp
from jax import lax
from jax.experimental import pallas as pl
from jax.experimental.pallas import tpu as pltpu
from jax.sharding import PartitionSpec as P

BF16, F32, I32 = jnp.bfloat16, jnp.float32, jnp.int32
LEVELS = 4095.0
UNROLL = 16
NT = (((1,), (1,)), ((), ()))
TN = (((0,), (0,)), ((), ()))


def dot(a, b, dims=(((1,), (0,)), ((), ()))):
    return lax.dot_general(a, b, dims, preferred_element_type=F32)


def sorted_keys(x):
    n = len(x)
    sub = lax.broadcasted_iota(I32, (8, 128), 0)
    lane = lax.broadcasted_iota(I32, (8, 128), 1)

    def bit(k):
        return ((sub >> (k - 4)) & 1) if k < 7 else ((lane >> (k - 7)) & 1)

    def flips(k, i):
        if k >= 14:
            return 0
        if k < 4:
            return -((i >> k) & 1)
        return -bit(k)

    x = list(x)
    state = [0] * n
    for k in range(1, 15):
        for i in range(n):
            new = flips(k, i)
            change = new ^ state[i]
            if not isinstance(change, int):
                x[i] = x[i] ^ change
            elif change:
                x[i] = ~x[i]
            state[i] = new
        for j in reversed(range(k)):
            if k == 14 and j < 7:
                break
            if j < 4:
                d = 1 << j
                for i in range(n):
                    if not i & d:
                        x[i], x[i + d] = jnp.minimum(x[i], x[i + d]), jnp.maximum(x[i], x[i + d])
            else:
                axis, size, d = (0, 8, 1 << (j - 4)) if j < 7 else (1, 128, 1 << (j - 7))
                high = bit(j) == 1
                for i in range(n):
                    down = pltpu.roll(x[i], d, axis)
                    up = down if 2 * d == size else pltpu.roll(x[i], size - d, axis)
                    x[i] = jnp.where(high, jnp.maximum(x[i], down), jnp.minimum(x[i], up))
    return x


def pair_table(x):
    lane = lax.broadcasted_iota(I32, (8, 128), 1)
    first = jnp.zeros((8, 128), I32)
    window, bucket = lane, first
    for b in range(1, 32):
        below = functools.reduce(jnp.add, [(xi < (b - 16) * (1 << 27)).astype(F32) for xi in x])
        count = jnp.sum(jnp.sum(below, axis=0, keepdims=True), axis=1, keepdims=True)
        count = jnp.broadcast_to(count.astype(I32), (8, 128))
        first = first + (count <= 256 * lane).astype(I32)
        here = lane == 63 + b
        window = jnp.where(here, jnp.minimum(count >> 8, 63), window)
        bucket = jnp.where(here, jnp.where((count & 255) != 0, b, -1), bucket)
    bucket = jnp.where(lane < 64, first, jnp.where(lane < 95, bucket, -1))
    window = jnp.where(lane < 95, window, 0)
    return jnp.where(lax.broadcasted_iota(I32, (8, 128), 0) == 0, window, bucket)


def one_hot(mask):
    return jnp.where(mask, 1.0, 0.0).astype(BF16)


def hub_copies(signal, hub_row, send_row):
    hubs, rows = hub_row.shape[1], signal.shape[0]
    square = jnp.broadcast_to(hub_row, (hubs, hubs)).astype(F32)
    diagonal = lax.broadcasted_iota(I32, (hubs, hubs), 0) == lax.broadcasted_iota(I32, (hubs, hubs), 1)
    hub_col = jnp.sum(jnp.where(diagonal, square, 0.0), axis=1, keepdims=True).astype(I32)
    pick = one_hot(lax.broadcasted_iota(I32, (hubs, rows), 1) == hub_col)
    hub_values = dot(pick, signal).astype(BF16)
    return dot(slot_matrix(hubs, send_row), hub_values, TN)


def slot_matrix(hubs, send_row):
    return one_hot(lax.broadcasted_iota(I32, (hubs, send_row.shape[1]), 0) == send_row)


def send_order(send_t):
    slots, peers = send_t.shape
    count = slots * peers
    expand = one_hot(lax.broadcasted_iota(I32, (peers, count), 1) // slots == lax.broadcasted_iota(I32, (peers, count), 0))
    wide = dot(send_t.astype(F32).astype(BF16), expand)
    mine = lax.broadcasted_iota(I32, (slots, count), 1) % slots == lax.broadcasted_iota(I32, (slots, count), 0)
    return jnp.sum(jnp.where(mine, wide, 0.0), axis=0, keepdims=True).astype(I32)


def shares(grad):
    left, right = grad[:, :128].reshape(-1, 8, 128), grad[:, 128:].reshape(-1, 8, 128)
    upper = lax.broadcasted_iota(I32, left.shape, 1) < 4
    even = jnp.where(upper, left, pltpu.roll(right, 4, 1))
    odd = jnp.where(upper, pltpu.roll(left, 4, 1), right)
    return jnp.stack([even, odd], axis=1).reshape(-1, 8, 128)


def halves(x):
    return [x[:, :128].reshape(-1, 8, 128), x[:, 128:].reshape(-1, 8, 128)]


def joined(received, at):
    return jnp.concatenate([received[:, i:i + 8].reshape(-1, 128) for i in (at, at + 8)], axis=1).astype(BF16)


def edge_kernel(target_hbm, slot_hbm, strength_hbm, signal_hbm, hub_hbm, send_hbm, matrix_t_hbm, send_ref, out_ref,
                target, slots, strength, signal, hub, send, matrix_t, keys, total, table, table_smem, sems):
    loads = [pltpu.make_async_copy(src, dst, sems.at[i]) for i, (src, dst) in enumerate(
        [(target_hbm, target), (slot_hbm, slots), (strength_hbm, strength), (signal_hbm, signal), (hub_hbm, hub),
         (send_hbm, send)])]
    for copy in loads:
        copy.start()
    for copy in loads[:3]:
        copy.wait()
    x = []
    for i in range(16):
        row, slot = target[8 * i:8 * i + 8, :], slots[8 * i:8 * i + 8, :]
        level = jnp.round(strength[8 * i:8 * i + 8, :] * LEVELS).astype(I32)
        x.append((((row >> 8) - 4) << 29) | ((slot >> 7) << 27) | ((row & 255) << 19) | ((slot & 127) << 12) | level)
    table[...] = pair_table(x)
    copy = pltpu.make_async_copy(table, table_smem, sems.at[6])
    copy.start()
    total[...] = jnp.zeros_like(total)
    keys[...] = jnp.concatenate(sorted_keys(x), axis=0).T
    copy.wait()
    place = lax.broadcasted_iota(I32, (256, 128), 0).astype(F32).astype(BF16)

    def spread(row, count):
        return jnp.broadcast_to(row.astype(F32), (count, 128)).astype(BF16)

    def product(n):
        window, bucket = table_smem[0, n], table_smem[1, n]
        left, right = [], []
        for half in range(2):
            key = keys[pl.ds(2 * window + half, 1), :]
            row = jnp.where((key >> 27) + 16 == bucket, (key >> 19) & 255, -1)
            level = (key & 4095).astype(F32) * (1.0 / LEVELS)
            slot = (key >> 12) & 127
            left.append(jnp.where(place[:128] == spread(slot, 128), jnp.ones((), BF16), jnp.zeros((), BF16)))
            right.append(jnp.where(place == spread(row, 256), spread(level, 256), jnp.zeros((), BF16)))
        return jnp.maximum(bucket, 0), dot(jnp.concatenate(left, axis=1), jnp.concatenate(right, axis=1), NT)

    def step(i, carry):
        for bucket, value in [product(i * UNROLL + u) for u in range(UNROLL)]:
            total[bucket] += value
        return carry

    lax.fori_loop(0, 96 // UNROLL, step, 0)
    for i in range(8):
        for j in range(4):
            matrix_t[128 * j:128 * j + 128, 256 * i:256 * i + 256] = total[4 * i + j].astype(BF16)
    store = pltpu.make_async_copy(matrix_t, matrix_t_hbm, sems.at[7])
    store.start()
    for copy in loads[3:]:
        copy.wait()
    send_row = send_order(send[...])
    send_ref[...] = send_row
    value = signal[...]
    copies, partial = hub_copies(value, hub[...], send_row), dot(matrix_t[...], value)
    columns = value.shape[1]
    both = jnp.concatenate([copies.reshape(-1, 8, columns), partial.reshape(-1, 8, columns)], axis=1)
    out_ref[...] = both.astype(BF16)
    store.wait()


def tile_products(transpose, tiles_ref, from_ref, to_ref, signal_ref, out_ref):
    out_ref[...] = jnp.zeros_like(out_ref)
    for t in range(tiles_ref.shape[0]):
        source = signal_ref[pl.ds(pl.multiple_of(from_ref[0, t] * 128, 128), 128), :]
        value = dot(tiles_ref[t], source, TN) if transpose else dot(tiles_ref[t], source)
        out_ref[pl.ds(pl.multiple_of(to_ref[0, t] * 128, 128), 128), :] += value


def near_kernel(tiles_ref, from_ref, to_ref, signal_ref, matrix_t_ref, out_ref, matrix_ref):
    tile_products(False, tiles_ref, from_ref, to_ref, signal_ref, out_ref)
    eye = one_hot(lax.broadcasted_iota(I32, (256, 256), 0) == lax.broadcasted_iota(I32, (256, 256), 1))
    for i in range(8):
        for j in range(2):
            rows, slots = slice(256 * i, 256 * i + 256), slice(256 * j, 256 * j + 256)
            matrix_ref[rows, slots] = dot(eye, matrix_t_ref[slots, rows], NT).astype(BF16)


def gather_sums(near_ref, matrix_ref, mirrored, returned, send_ref, hub_smem, total):
    hubs = hub_smem.shape[1]
    back = dot(slot_matrix(hubs, send_ref[...]), returned)
    for i in range(8):
        rows = slice(256 * i, 256 * i + 256)
        total[rows, :] = near_ref[rows, :] + dot(matrix_ref[rows, :], mirrored)
    for h in range(hubs):
        total[pl.ds(hub_smem[0, h], 1), :] += back[h:h + 1, :]


def layer_kernel(received_ref, matrix_ref, matrix_t_ref, near_ref, cotangent_ref, weight_ref, hub_ref, send_ref,
                 hub_smem, activated_ref, upstream_ref, out_ref, total):
    received = received_ref[...].astype(F32)
    columns = received.shape[2]
    mirrored, returned = received[:, :8].reshape(-1, columns), received[:, 8:].reshape(-1, columns)
    gather_sums(near_ref, matrix_ref, mirrored.astype(BF16), returned.astype(BF16), send_ref, hub_smem, total)
    weight = weight_ref[...]
    grad = None
    for i in range(8):
        rows = slice(256 * i, 256 * i + 256)
        aggregated = total[rows, :].astype(BF16)
        hidden = dot(aggregated, weight)
        logistic = jax.nn.sigmoid(hidden)
        activated_ref[rows, :] = (hidden * logistic).astype(BF16)
        slope = logistic * (1.0 + hidden * (1.0 - logistic))
        hidden_grad = (cotangent_ref[rows, :].astype(F32) * slope).astype(BF16)
        term = dot(aggregated, hidden_grad, TN)
        grad = term if grad is None else grad + term
        upstream_ref[rows, :] = dot(hidden_grad, weight, NT).astype(BF16)
    upstream = upstream_ref[...]
    copies = hub_copies(upstream, hub_ref[...], send_ref[...])
    partial = dot(matrix_t_ref[...], upstream)
    out_ref[...] = jnp.concatenate(halves(copies) + halves(partial) + [shares(grad)], axis=1).astype(BF16)


def final_kernel(received_ref, matrix_ref, near_ref, send_ref, hub_smem, out_ref, total):
    received = received_ref[...].astype(F32)
    gather_sums(near_ref, matrix_ref, joined(received, 0), joined(received, 16), send_ref, hub_smem, total)
    out_ref[...] = total[...].astype(BF16)


def share_kernel(received_ref, out_ref):
    own = jnp.sum(received_ref[:, 32:, :].astype(F32), axis=0)
    out_ref[...] = jnp.concatenate([own[:4], own[4:]], axis=1)


def run(kernel, name, operands, outs, scratch=(), smem=(), hbm=(), hbm_out=(), flops=0, limit=24):
    def spec(i, listed, in_smem=()):
        if i in in_smem:
            return pl.BlockSpec(memory_space=pltpu.SMEM)
        return pl.BlockSpec(memory_space=pl.ANY) if i in listed else pl.BlockSpec()

    size = sum(math.prod(a.shape) * a.dtype.itemsize for a in operands)
    size += sum(math.prod(s) * jnp.dtype(d).itemsize for s, d in outs)
    return pl.pallas_call(
        kernel,
        out_shape=[jax.ShapeDtypeStruct(s, d) for s, d in outs],
        in_specs=[spec(i, hbm, smem) for i in range(len(operands))],
        out_specs=[spec(i, hbm_out) for i in range(len(outs))],
        scratch_shapes=list(scratch),
        compiler_params=pltpu.CompilerParams(vmem_limit_bytes=limit << 20),
        cost_estimate=pl.CostEstimate(flops=flops, bytes_accessed=size, transcendentals=0),
        name=name,
    )(*operands)


def exchange(x):
    return lax.all_to_all(x, "dev", split_axis=0, concat_axis=0, tiled=True)


def local(
    features,
    weight,
    cotangent,
    tile_vals,
    tile_rows,
    tile_cols,
    hub_rows,
    send_hub,
    mirror_slot,
    replica_target_row,
    replica_edge_weight,
):
    peers = lax.axis_size("dev")
    groups = lax.axis_size("grp")
    rows, columns = features.shape
    send_t = send_hub[0].T
    slots = send_t.size
    tiles = tile_vals[0]
    square = (128, 128)

    matrix_t, send, outgoing = run(
        edge_kernel, "edges",
        (replica_target_row.reshape(square), mirror_slot.reshape(square), replica_edge_weight.reshape(square),
         features, hub_rows, send_t),
        [((slots, rows), BF16), ((1, slots), I32), ((peers, 16, columns), BF16)],
        [pltpu.VMEM(square, I32), pltpu.VMEM(square, I32), pltpu.VMEM(square, F32), pltpu.VMEM((rows, columns), BF16),
         pltpu.VMEM(hub_rows.shape, I32), pltpu.VMEM(send_t.shape, I32), pltpu.VMEM((slots, rows), BF16),
         pltpu.VMEM(square, I32), pltpu.VMEM((32, 128, 256), F32), pltpu.VMEM((8, 128), I32),
         pltpu.SMEM((8, 128), I32), pltpu.SemaphoreType.DMA((8,))],
        hbm=range(6), hbm_out=(0,), flops=1 << 33, limit=56,
    )
    received = exchange(outgoing)
    near, matrix = run(
        near_kernel, "near", (tiles, tile_cols, tile_rows, features, matrix_t),
        [((rows, columns), F32), ((rows, slots), BF16)], smem=(1, 2), flops=1 << 31,
    )
    activated, upstream, outgoing = run(
        layer_kernel, "layer",
        (received, matrix, matrix_t, near, cotangent, weight, hub_rows, send, hub_rows),
        [((rows, columns), BF16), ((rows, columns), BF16), ((peers, 40, 128), BF16)],
        [pltpu.VMEM((rows, columns), F32)], smem=(8,), flops=1 << 32,
    )
    received = exchange(outgoing)
    (near,) = run(
        functools.partial(tile_products, True), "near_t", (tiles, tile_rows, tile_cols, upstream),
        [((rows, columns), F32)], smem=(1, 2), flops=1 << 31,
    )
    (own,) = run(share_kernel, "share", (received,), [((weight.shape[0] // peers, columns), F32)])
    summed = own
    for shift in range(1, groups):
        summed = summed + lax.ppermute(own, "grp", [(g, (g + shift) % groups) for g in range(groups)])
    scale = 1.0 / math.sqrt(rows * peers * groups)
    weight_grad = summed * scale
    (feature_grad,) = run(
        final_kernel, "final", (received, matrix, near, send, hub_rows), [((rows, columns), BF16)],
        [pltpu.VMEM((rows, columns), F32)], smem=(4,), flops=1 << 31,
    )
    return (activated, feature_grad, weight_grad)


def solution(mesh):
    placed = (
        P(("grp", "dev"), None),
        P(),
        P(("grp", "dev"), None),
        P(("grp", "dev"), None, None, None),
        P(("grp", "dev"), None),
        P(("grp", "dev"), None),
        P(("grp", "dev"), None),
        P(("grp", "dev"), None, None),
        P(("grp", "dev"), None),
        P(("grp", "dev"), None),
        P(("grp", "dev"), None),
    )
    return jax.shard_map(
        local,
        mesh=mesh,
        in_specs=placed,
        out_specs=(P(("grp", "dev"), None), P(("grp", "dev"), None), P("dev", None)),
        check_vma=False,
    )
```

time: 105 us -> 90.1 us (0.86); the launches traced: 103 us -> 89.6 us
  blocking collectives: 16.6 us -> 0 us
  waiting for transfers between devices: 21.7 us -> 25.5 us
  local copies, waits for them, and re-layouts: 18.8 us -> 16.6 us
    all_to_all x1 -> x0, blocking collectives: 16.6 us -> none  [exchange(): return lax.all_to_all(x, 'dev', split_axis=0, concat_axis=0, tiled=True)]
    all_to_all x2, waiting for transfers between devices: 21.7 us -> 25.5 us  [exchange(): return lax.all_to_all(x, 'dev', split_axis=0, concat_axis=0, tiled=True)]
    unnamed x45 -> x40, local copies, waits for them, and re-layouts: 18.7 us -> 16.6 us
    all_to_all x2, starting transfers between devices: 16.7 us -> 17.9 us  [exchange(): return lax.all_to_all(x, 'dev', split_axis=0, concat_axis=0, tiled=True)]
    pallas_call x5 -> x6, Pallas kernels: 22.5 us -> 23.4 us  [run(): pl.pallas_call(kernel, out_shape=[jax.ShapeDtypeStruct(s, d) for s, d in...]
  transfers between devices with their start and end apart: 5 -> 5, of which waited for: 2 -> 2; matrix products, arithmetic and copies ran while one was open for 1% -> 0% of each run, Pallas kernels for 3% -> 6%
where the time goes in v2:
time: 90.1 us; the launch traced here: 89.6 us
  waiting for transfers between devices  25.5 us (28%)
  Pallas kernels  23.4 us (26%)
  starting transfers between devices  22.7 us (25%)
  local copies, waits for them, and re-layouts  16.6 us (18%)
    all_to_all x2, waiting for transfers between devices, exchange(): return lax.all_to_all(x, 'dev', split_axis=0, concat_axis=0, tiled=True)  25.5 us
    pallas_call x6, Pallas kernels, run(): pl.pallas_call(kernel, out_shape=[jax.ShapeDtypeStruct(s, d) for s, d in...  23.4 us
    all_to_all x2, starting transfers between devices, exchange(): return lax.all_to_all(x, 'dev', split_axis=0, concat_axis=0, tiled=True)  17.9 us
    unnamed x40, local copies, waits for them, and re-layouts  16.6 us
    ppermute x3, starting transfers between devices, local(): lax.ppermute(own, 'grp', [(g, (g + shift) % groups) for g in range(groups)])  4.83 us
  transfers between devices with their start and end apart: 5, of which 2 were waited for; matrix products, arithmetic and copies ran while one was open for 0% of the time, Pallas kernels for 6%

profile of v2, /device:TPU:2, one launch (start us, length us, event | category | flops | bytes accessed | tf_op | source)
XLA Modules:
  0.0 89.6 jit_solution(33617712269796451)
XLA Ops:
  0.6 0.0 copy-start
  0.6 0.0 copy-start.5
  0.7 0.0 copy-start.6
  0.7 12.1 %edges.1 = (bf16[512,2048]{1,0:T(8,128)(2,1)}, s32[1,512]{1,0:T(1,128)}, bf16[64,16,256]{2,1,0:T(8,128)(2,1)}) custom-call(s32[128,128]{1,0:T(8,128)} %bitcast.9, s32[128,128]{1,0:T(8,128)} %bitcast.10, f32[128,128]{1,0:T(8,128)} %bitcast.11, bf16[2048,256]{1,0:T(8,128)(2,1)} %signal_ref.1, s32[1,32]{1,0:T(1,128)} %hub_smem.3, s32[8,64]{1,0:T(8,128)} %bitcast.12), custom_call_target="tpu_custom_call" | custom-call | flops 8589934592 | bytes 3870848 | tf_op jit(solution)/shard_map/edges/pallas_call | solution.py:257
  12.8 12.1 %all-to-all-start = ((bf16[64,16,256]{2,1,0:T(8,128)(2,1)}), bf16[64,16,256]{2,1,0:T(8,128)(2,1)S(1)}, u32[]{:S(2)}, u32[]{:S(2)}) async-start(bf16[64,16,256]{2,1,0:T(8,128)(2,1)} %get-tuple-element.11), calls=%async_computation | async-start | bytes 1048576 | tf_op jit(solution)/shard_map/all_to_all | solution.py:270
  24.9 0.0 copy-done
  25.0 0.0 copy-done.5
  25.0 0.0 copy-done.6
  25.0 0.0 copy-start.2
  25.0 1.2 %copy-done.2 = bf16[1,32,128,128]{3,2,1,0:T(8,128)(2,1)S(1)} copy-done((bf16[1,32,128,128]{3,2,1,0:T(8,128)(2,1)S(1)}, bf16[1,32,128,128]{3,2,1,0:T(8,128)(2,1)}, u32[]{:S(2)}) %copy-start.2) | copy-done | bytes 1048600
  26.2 0.0 copy-start.13
  26.2 1.6 %copy-done.13 = bf16[512,2048]{1,0:T(8,128)(2,1)S(1)} copy-done((bf16[512,2048]{1,0:T(8,128)(2,1)S(1)}, bf16[512,2048]{1,0:T(8,128)(2,1)}, u32[]{:S(2)}) %copy-start.13) | copy-done | bytes 2097176
  27.8 0.0 copy-start.1
  27.8 0.0 copy-start.4
  27.8 0.0 copy-start.7
  27.8 0.0 copy-start.19
  27.8 1.9 %near.1 = (f32[2048,256]{1,0:T(8,128)S(1)}, bf16[2048,512]{1,0:T(8,128)(2,1)S(1)}) custom-call(bf16[32,128,128]{2,1,0:T(8,128)(2,1)S(1)} %bitcast.7, s32[1,32]{1,0:T(1,128)S(1)} %copy-done.5, s32[1,32]{1,0:T(1,128)S(1)} %copy-done.6, bf16[2048,256]{1,0:T(8,128)(2,1)S(1)} %copy-done, bf16[512,2048]{1,0:T(8,128)(2,1)S(1)} %copy-done.13), custom_call_target="tpu_custom_call" | custom-call | flops 2147483648 | bytes 8388864 | tf_op jit(solution)/shard_map/near/pallas_call | solution.py:257
  29.7 0.0 copy-start.8
  29.7 1.3 %copy-done.8 = bf16[2048,512]{1,0:T(8,128)(2,1)} copy-done((bf16[2048,512]{1,0:T(8,128)(2,1)}, bf16[2048,512]{1,0:T(8,128)(2,1)S(1)}, u32[]{:S(2)}) %copy-start.8) | copy-done | bytes 2097176
  31.1 0.0 copy-start.15
  31.1 1.4 %copy-done.15 = f32[2048,256]{1,0:T(8,128)} copy-done((f32[2048,256]{1,0:T(8,128)}, f32[2048,256]{1,0:T(8,128)S(1)}, u32[]{:S(2)}) %copy-start.15) | copy-done | bytes 2097176
  32.4 10.2 %all-to-all-done.received_ref = bf16[64,16,256]{2,1,0:T(8,128)(2,1)S(1)} async-done(((bf16[64,16,256]{2,1,0:T(8,128)(2,1)}), bf16[64,16,256]{2,1,0:T(8,128)(2,1)S(1)}, u32[]{:S(2)}, u32[]{:S(2)}) %all-to-all-start) | async-done | bytes 524320 | tf_op jit(solution)/shard_map/all_to_all | solution.py:270
  42.6 0.0 copy-done.1
  42.6 0.0 copy-done.4
  42.6 0.0 copy-done.7
  42.6 0.0 copy-done.19
  42.6 0.0 copy-start.9
  42.6 1.6 %copy-done.9 = bf16[2048,512]{1,0:T(8,128)(2,1)S(1)} copy-done((bf16[2048,512]{1,0:T(8,128)(2,1)S(1)}, bf16[2048,512]{1,0:T(8,128)(2,1)}, u32[]{:S(2)}) %copy-start.9) | copy-done | bytes 2097176
  44.2 0.0 copy-start.14
  44.2 1.6 %copy-done.14 = bf16[512,2048]{1,0:T(8,128)(2,1)S(1)} copy-done((bf16[512,2048]{1,0:T(8,128)(2,1)S(1)}, bf16[512,2048]{1,0:T(8,128)(2,1)}, u32[]{:S(2)}) %copy-start.14) | copy-done | bytes 2097176
  45.8 0.0 copy-start.16
  45.8 1.6 %copy-done.16 = f32[2048,256]{1,0:T(8,128)S(1)} copy-done((f32[2048,256]{1,0:T(8,128)S(1)}, f32[2048,256]{1,0:T(8,128)}, u32[]{:S(2)}) %copy-start.16) | copy-done | bytes 2097176
  47.4 5.4 %layer.1 = (bf16[2048,256]{1,0:T(8,128)(2,1)}, bf16[2048,256]{1,0:T(8,128)(2,1)S(1)}, bf16[64,40,128]{2,1,0:T(8,128)(2,1)}) custom-call(bf16[64,16,256]{2,1,0:T(8,128)(2,1)S(1)} %all-to-all-done.received_ref, bf16[2048,512]{1,0:T(8,128)(2,1)S(1)} %copy-done.9, bf16[512,2048]{1,0:T(8,128)(2,1)S(1)} %copy-done.14, f32[2048,256]{1,0:T(8,128)S(1)} %copy-done.16, ...), custom_call_target="tpu_custom_call" | custom-call | flops 4294967296 | bytes 10750208 | tf_op jit(solution)/shard_map/layer/pallas_call | solution.py:257
  52.8 0.0 copy-start.17
  52.8 1.0 %copy-done.17 = bf16[2048,256]{1,0:T(8,128)(2,1)} copy-done((bf16[2048,256]{1,0:T(8,128)(2,1)}, bf16[2048,256]{1,0:T(8,128)(2,1)S(1)}, u32[]{:S(2)}) %copy-start.17) | copy-done | bytes 1048600
  53.7 5.8 %all-to-all-start.1 = ((bf16[64,40,128]{2,1,0:T(8,128)(2,1)}), bf16[64,40,128]{2,1,0:T(8,128)(2,1)S(1)}, u32[]{:S(2)}, u32[]{:S(2)}) async-start(bf16[64,40,128]{2,1,0:T(8,128)(2,1)} %get-tuple-element.17), calls=%async_computation.1 | async-start | bytes 1310720 | tf_op jit(solution)/shard_map/all_to_all | solution.py:270
  59.5 0.0 copy-start.3
  59.6 1.2 %copy-done.3 = bf16[1,32,128,128]{3,2,1,0:T(8,128)(2,1)S(1)} copy-done((bf16[1,32,128,128]{3,2,1,0:T(8,128)(2,1)S(1)}, bf16[1,32,128,128]{3,2,1,0:T(8,128)(2,1)}, u32[]{:S(2)}) %copy-start.3) | copy-done | bytes 1048600
  60.8 0.0 copy-start.18
  60.8 1.2 %copy-done.18 = bf16[2048,256]{1,0:T(8,128)(2,1)S(1)} copy-done((bf16[2048,256]{1,0:T(8,128)(2,1)S(1)}, bf16[2048,256]{1,0:T(8,128)(2,1)}, u32[]{:S(2)}) %copy-start.18) | copy-done | bytes 1048600
  62.0 0.0 copy-start.10
  62.0 1.4 %near_t.1.near_ref = f32[2048,256]{1,0:T(8,128)S(1)} custom-call(bf16[32,128,128]{2,1,0:T(8,128)(2,1)S(1)} %bitcast.8, s32[1,32]{1,0:T(1,128)S(1)} %copy-done.6, s32[1,32]{1,0:T(1,128)S(1)} %copy-done.5, bf16[2048,256]{1,0:T(8,128)(2,1)S(1)} %copy-done.18), custom_call_target="tpu_custom_call" | custom-call | flops 2147483648 | bytes 4194560 | tf_op jit(solution)/shard_map/near_t/pallas_call | solution.py:257
  63.4 0.0 copy-start.11
  63.4 1.3 %copy-done.11 = f32[2048,256]{1,0:T(8,128)} copy-done((f32[2048,256]{1,0:T(8,128)}, f32[2048,256]{1,0:T(8,128)S(1)}, u32[]{:S(2)}) %copy-start.11) | copy-done | bytes 2097176
  64.7 15.3 %all-to-all-done.1.received_ref = bf16[64,40,128]{2,1,0:T(8,128)(2,1)S(1)} async-done(((bf16[64,40,128]{2,1,0:T(8,128)(2,1)}), bf16[64,40,128]{2,1,0:T(8,128)(2,1)S(1)}, u32[]{:S(2)}, u32[]{:S(2)}) %all-to-all-start.1) | async-done | bytes 655392 | tf_op jit(solution)/shard_map/all_to_all | solution.py:270
  80.0 0.1 share.1
  80.1 0.6 collective-permute-start.2
  80.7 2.4 %collective-permute-start.1 = (f32[4,256]{1,0:T(4,128)S(1)}, f32[4,256]{1,0:T(4,128)S(1)}, u32[]{:S(2)}, u32[]{:S(2)}) collective-permute-start(f32[4,256]{1,0:T(4,128)S(1)} %share.1), channel_id=1, source_target_pairs={{0,128},{64,192},{128,0},{192,64},{1,129},{65,193},{129,1},{193,65... | collective-permute-start | bytes 12296 | tf_op jit(solution)/shard_map/ppermute | solution.py:324
  83.1 1.8 %collective-permute-start = (f32[4,256]{1,0:T(4,128)S(1)}, f32[4,256]{1,0:T(4,128)S(1)}, u32[]{:S(2)}, u32[]{:S(2)}) collective-permute-start(f32[4,256]{1,0:T(4,128)S(1)} %share.1), channel_id=1, source_target_pairs={{0,64},{64,128},{128,192},{192,0},{1,65},{65,129},{129,193},{193,1... | collective-permute-start | bytes 12296 | tf_op jit(solution)/shard_map/ppermute | solution.py:324
  84.9 0.0 copy-done.10
  84.9 0.0 copy-start.12
  84.9 1.6 %copy-done.12 = f32[2048,256]{1,0:T(8,128)S(1)} copy-done((f32[2048,256]{1,0:T(8,128)S(1)}, f32[2048,256]{1,0:T(8,128)}, u32[]{:S(2)}) %copy-start.12) | copy-done | bytes 2097176
  86.5 2.5 %final.1 = bf16[2048,256]{1,0:T(8,128)(2,1)} custom-call(bf16[64,40,128]{2,1,0:T(8,128)(2,1)S(1)} %all-to-all-done.1.received_ref, bf16[2048,512]{1,0:T(8,128)(2,1)S(1)} %copy-done.10, f32[2048,256]{1,0:T(8,128)S(1)} %copy-done.12, s32[1,512]{1,0:T(1,128)S(1)} %copy-done.19, s32[1,32]{1,0:T(1,128)S(1)} %copy-done.7), custom_call_target="tpu_custom_call" | custom-call | flops 2147483648 | bytes 5900416 | tf_op jit(solution)/shard_map/final/pallas_call | solution.py:257
  89.0 0.0 collective-permute-done.2
  89.0 0.0 collective-permute-done.1
  89.0 0.0 collective-permute-done
  89.0 0.6 add_multiply_fusion
Async XLA Ops:
  0.6 24.3 %copy-start = (bf16[2048,256]{1,0:T(8,128)(2,1)S(1)}, bf16[2048,256]{1,0:T(8,128)(2,1)}, u32[]{:S(2)}) copy-start(bf16[2048,256]{1,0:T(8,128)(2,1)} %signal_ref.1) | copy-start | bytes 3145732
  0.6 24.3 %copy-start.5 = (s32[1,32]{1,0:T(1,128)S(1)}, s32[1,32]{1,0:T(1,128)}, u32[]{:S(2)}) copy-start(s32[1,32]{1,0:T(1,128)} %to_ref.3) | copy-start | bytes 388
  0.7 24.3 %copy-start.6 = (s32[1,32]{1,0:T(1,128)S(1)}, s32[1,32]{1,0:T(1,128)}, u32[]{:S(2)}) copy-start(s32[1,32]{1,0:T(1,128)} %from_ref.3) | copy-start | bytes 388
  12.8 29.8 %all-to-all-start = ((bf16[64,16,256]{2,1,0:T(8,128)(2,1)}), bf16[64,16,256]{2,1,0:T(8,128)(2,1)S(1)}, u32[]{:S(2)}, u32[]{:S(2)}) async-start(bf16[64,16,256]{2,1,0:T(8,128)(2,1)} %get-tuple-element.11), calls=%async_computation | async-start | bytes 1048576 | tf_op jit(solution)/shard_map/all_to_all | solution.py:270
  25.0 1.2 %copy-start.2 = (bf16[1,32,128,128]{3,2,1,0:T(8,128)(2,1)S(1)}, bf16[1,32,128,128]{3,2,1,0:T(8,128)(2,1)}, u32[]{:S(2)}) copy-start(bf16[1,32,128,128]{3,2,1,0:T(8,128)(2,1)} %param.14) | copy-start | bytes 3145732
  26.2 1.6 %copy-start.13 = (bf16[512,2048]{1,0:T(8,128)(2,1)S(1)}, bf16[512,2048]{1,0:T(8,128)(2,1)}, u32[]{:S(2)}) copy-start(bf16[512,2048]{1,0:T(8,128)(2,1)} %get-tuple-element.12.matrix_t_ref) | copy-start | bytes 6291460
  27.8 14.8 %copy-start.1 = (bf16[2048,256]{1,0:T(8,128)(2,1)S(1)}, bf16[2048,256]{1,0:T(8,128)(2,1)}, u32[]{:S(2)}) copy-start(bf16[2048,256]{1,0:T(8,128)(2,1)} %cotangent_ref.1) | copy-start | bytes 3145732
  27.8 14.8 %copy-start.4 = (bf16[256,256]{1,0:T(8,128)(2,1)S(1)}, bf16[256,256]{1,0:T(8,128)(2,1)}, u32[]{:S(2)}) copy-start(bf16[256,256]{1,0:T(8,128)(2,1)} %weight_ref.1) | copy-start | bytes 393220
  27.8 14.8 %copy-start.7 = (s32[1,32]{1,0:T(1,128)S(1)}, s32[1,32]{1,0:T(1,128)}, u32[]{:S(2)}) copy-start(s32[1,32]{1,0:T(1,128)} %hub_smem.3) | copy-start | bytes 388
  27.8 14.8 %copy-start.19 = (s32[1,512]{1,0:T(1,128)S(1)}, s32[1,512]{1,0:T(1,128)}, u32[]{:S(2)}) copy-start(s32[1,512]{1,0:T(1,128)} %get-tuple-element.15.send_ref) | copy-start | bytes 6148
  29.7 1.3 %copy-start.8 = (bf16[2048,512]{1,0:T(8,128)(2,1)}, bf16[2048,512]{1,0:T(8,128)(2,1)S(1)}, u32[]{:S(2)}) copy-start(bf16[2048,512]{1,0:T(8,128)(2,1)S(1)} %get-tuple-element.13.matrix_ref) | copy-start | bytes 6291460
  31.1 1.4 %copy-start.15 = (f32[2048,256]{1,0:T(8,128)}, f32[2048,256]{1,0:T(8,128)S(1)}, u32[]{:S(2)}) copy-start(f32[2048,256]{1,0:T(8,128)S(1)} %get-tuple-element.14.near_ref) | copy-start | bytes 6291460
  42.6 1.6 %copy-start.9 = (bf16[2048,512]{1,0:T(8,128)(2,1)S(1)}, bf16[2048,512]{1,0:T(8,128)(2,1)}, u32[]{:S(2)}) copy-start(bf16[2048,512]{1,0:T(8,128)(2,1)} %copy-done.8) | copy-start | bytes 6291460
  44.2 1.6 %copy-start.14 = (bf16[512,2048]{1,0:T(8,128)(2,1)S(1)}, bf16[512,2048]{1,0:T(8,128)(2,1)}, u32[]{:S(2)}) copy-start(bf16[512,2048]{1,0:T(8,128)(2,1)} %get-tuple-element.12.matrix_t_ref) | copy-start | bytes 6291460
  45.8 1.6 %copy-start.16 = (f32[2048,256]{1,0:T(8,128)S(1)}, f32[2048,256]{1,0:T(8,128)}, u32[]{:S(2)}) copy-start(f32[2048,256]{1,0:T(8,128)} %copy-done.15) | copy-start | bytes 6291460
  52.8 1.0 %copy-start.17 = (bf16[2048,256]{1,0:T(8,128)(2,1)}, bf16[2048,256]{1,0:T(8,128)(2,1)S(1)}, u32[]{:S(2)}) copy-start(bf16[2048,256]{1,0:T(8,128)(2,1)S(1)} %get-tuple-element.18.signal_ref) | copy-start | bytes 3145732
  53.7 26.3 %all-to-all-start.1 = ((bf16[64,40,128]{2,1,0:T(8,128)(2,1)}), bf16[64,40,128]{2,1,0:T(8,128)(2,1)S(1)}, u32[]{:S(2)}, u32[]{:S(2)}) async-start(bf16[64,40,128]{2,1,0:T(8,128)(2,1)} %get-tuple-element.17), calls=%async_computation.1 | async-start | bytes 1310720 | tf_op jit(solution)/shard_map/all_to_all | solution.py:270
  59.5 1.2 %copy-start.3 = (bf16[1,32,128,128]{3,2,1,0:T(8,128)(2,1)S(1)}, bf16[1,32,128,128]{3,2,1,0:T(8,128)(2,1)}, u32[]{:S(2)}) copy-start(bf16[1,32,128,128]{3,2,1,0:T(8,128)(2,1)} %param.14) | copy-start | bytes 3145732
  60.8 1.2 %copy-start.18 = (bf16[2048,256]{1,0:T(8,128)(2,1)S(1)}, bf16[2048,256]{1,0:T(8,128)(2,1)}, u32[]{:S(2)}) copy-start(bf16[2048,256]{1,0:T(8,128)(2,1)} %copy-done.17) | copy-start | bytes 3145732
  62.0 22.9 %copy-start.10 = (bf16[2048,512]{1,0:T(8,128)(2,1)S(1)}, bf16[2048,512]{1,0:T(8,128)(2,1)}, u32[]{:S(2)}) copy-start(bf16[2048,512]{1,0:T(8,128)(2,1)} %copy-done.8) | copy-start | bytes 6291460
  63.4 1.3 %copy-start.11 = (f32[2048,256]{1,0:T(8,128)}, f32[2048,256]{1,0:T(8,128)S(1)}, u32[]{:S(2)}) copy-start(f32[2048,256]{1,0:T(8,128)S(1)} %near_t.1.near_ref) | copy-start | bytes 6291460
  80.1 8.9 %collective-permute-start.2 = (f32[4,256]{1,0:T(4,128)S(1)}, f32[4,256]{1,0:T(4,128)S(1)}, u32[]{:S(2)}, u32[]{:S(2)}) collective-permute-start(f32[4,256]{1,0:T(4,128)S(1)} %share.1), channel_id=1, source_target_pairs={{0,192},{64,0},{128,64},{192,128},{1,193},{65,1},{129,65},{193,129... | collective-permute-start | bytes 12296 | tf_op jit(solution)/shard_map/ppermute | solution.py:324
  80.7 8.3 %collective-permute-start.1 = (f32[4,256]{1,0:T(4,128)S(1)}, f32[4,256]{1,0:T(4,128)S(1)}, u32[]{:S(2)}, u32[]{:S(2)}) collective-permute-start(f32[4,256]{1,0:T(4,128)S(1)} %share.1), channel_id=1, source_target_pairs={{0,128},{64,192},{128,0},{192,64},{1,129},{65,193},{129,1},{193,65... | collective-permute-start | bytes 12296 | tf_op jit(solution)/shard_map/ppermute | solution.py:324
  83.1 5.9 %collective-permute-start = (f32[4,256]{1,0:T(4,128)S(1)}, f32[4,256]{1,0:T(4,128)S(1)}, u32[]{:S(2)}, u32[]{:S(2)}) collective-permute-start(f32[4,256]{1,0:T(4,128)S(1)} %share.1), channel_id=1, source_target_pairs={{0,64},{64,128},{128,192},{192,0},{1,65},{65,129},{129,193},{193,1... | collective-permute-start | bytes 12296 | tf_op jit(solution)/shard_map/ppermute | solution.py:324
  84.9 1.6 %copy-start.12 = (f32[2048,256]{1,0:T(8,128)S(1)}, f32[2048,256]{1,0:T(8,128)}, u32[]{:S(2)}) copy-start(f32[2048,256]{1,0:T(8,128)} %copy-done.11) | copy-start | bytes 6291460

commit v3 on v2

--- a/solution.py
+++ b/solution.py
@@ -10,7 +10,10 @@
 
 BF16, F32, I32 = jnp.bfloat16, jnp.float32, jnp.int32
 LEVELS = 4095.0
-UNROLL = 16
+UNROLL = 32
+LARGE = 60
+MOST = 52
+BLOCKS = 4
 NT = (((1,), (1,)), ((), ()))
 TN = (((0,), (0,)), ((), ()))
 
@@ -191,54 +194,101 @@
         out_ref[pl.ds(pl.multiple_of(to_ref[0, t] * 128, 128), 128), :] += value
 
 
-def near_kernel(tiles_ref, from_ref, to_ref, signal_ref, matrix_t_ref, out_ref, matrix_ref):
-    tile_products(False, tiles_ref, from_ref, to_ref, signal_ref, out_ref)
+def start(copies, sems):
+    made = [pltpu.make_async_copy(src, dst, sems.at[i]) for i, (src, dst) in enumerate(copies)]
+    for copy in made:
+        copy.start()
+    return made
+
+
+def rows_of(i):
+    return slice(256 * i, 256 * i + 256)
+
+
+def near_kernel(tiles_ref, from_ref, to_ref, signal_ref, matrix_t_ref, near_hbm, matrix_hbm, near, matrix, sems):
     eye = one_hot(lax.broadcasted_iota(I32, (256, 256), 0) == lax.broadcasted_iota(I32, (256, 256), 1))
     for i in range(8):
         for j in range(2):
-            rows, slots = slice(256 * i, 256 * i + 256), slice(256 * j, 256 * j + 256)
-            matrix_ref[rows, slots] = dot(eye, matrix_t_ref[slots, rows], NT).astype(BF16)
-
-
-def gather_sums(near_ref, matrix_ref, mirrored, returned, send_ref, hub_smem, total):
+            matrix[rows_of(i), rows_of(j)] = dot(eye, matrix_t_ref[rows_of(j), rows_of(i)], NT).astype(BF16)
+    tile_products(False, tiles_ref, from_ref, to_ref, signal_ref, near)
+    for copy in start([(matrix, matrix_hbm), (near, near_hbm)], sems):
+        copy.wait()
+
+
+def blocks(rows):
+    return [slice(i * rows // BLOCKS, (i + 1) * rows // BLOCKS) for i in range(BLOCKS)]
+
+
+def sums_loads(matrix_hbm, near_hbm, matrix, total):
+    pairs = []
+    for rows in blocks(total.shape[0]):
+        pairs += [(matrix_hbm.at[rows], matrix.at[rows]), (near_hbm.at[rows], total.at[rows])]
+    return pairs
+
+
+def gather_sums(loads, matrix, mirrored, returned, send, hub_smem, total):
     hubs = hub_smem.shape[1]
-    back = dot(slot_matrix(hubs, send_ref[...]), returned)
-    for i in range(8):
-        rows = slice(256 * i, 256 * i + 256)
-        total[rows, :] = near_ref[rows, :] + dot(matrix_ref[rows, :], mirrored)
+    back = dot(slot_matrix(hubs, send), returned)
+    for i, rows in enumerate(blocks(total.shape[0])):
+        for copy in loads[2 * i:2 * i + 2]:
+            copy.wait()
+        total[rows, :] += dot(matrix[rows, :], mirrored)
     for h in range(hubs):
         total[pl.ds(hub_smem[0, h], 1), :] += back[h:h + 1, :]
 
 
-def layer_kernel(received_ref, matrix_ref, matrix_t_ref, near_ref, cotangent_ref, weight_ref, hub_ref, send_ref,
-                 hub_smem, activated_ref, upstream_ref, out_ref, total):
+def layer_kernel(received_ref, matrix_hbm, matrix_t_hbm, near_hbm, cotangent_hbm, weight_hbm, hub_hbm, send_hbm,
+                 hub_smem, activated_hbm, upstream_hbm, out_hbm,
+                 matrix, matrix_t, total, cotangent, weight_ref, hub, send, activated, upstream,
+                 outgoing, sems):
+    loads = start(
+        [(send_hbm, send), (hub_hbm, hub), (weight_hbm, weight_ref)]
+        + sums_loads(matrix_hbm, near_hbm, matrix, total)
+        + [(cotangent_hbm, cotangent), (matrix_t_hbm, matrix_t)], sems)
+    for copy in loads[:3]:
+        copy.wait()
     received = received_ref[...].astype(F32)
     columns = received.shape[2]
     mirrored, returned = received[:, :8].reshape(-1, columns), received[:, 8:].reshape(-1, columns)
-    gather_sums(near_ref, matrix_ref, mirrored.astype(BF16), returned.astype(BF16), send_ref, hub_smem, total)
+    gather_sums(loads[3:3 + 2 * BLOCKS], matrix, mirrored.astype(BF16), returned.astype(BF16), send[...], hub_smem, total)
     weight = weight_ref[...]
+    loads[3 + 2 * BLOCKS].wait()
     grad = None
+    stores = []
     for i in range(8):
-        rows = slice(256 * i, 256 * i + 256)
+        rows = rows_of(i)
         aggregated = total[rows, :].astype(BF16)
         hidden = dot(aggregated, weight)
         logistic = jax.nn.sigmoid(hidden)
-        activated_ref[rows, :] = (hidden * logistic).astype(BF16)
+        activated[rows, :] = (hidden * logistic).astype(BF16)
         slope = logistic * (1.0 + hidden * (1.0 - logistic))
-        hidden_grad = (cotangent_ref[rows, :].astype(F32) * slope).astype(BF16)
+        hidden_grad = (cotangent[rows, :].astype(F32) * slope).astype(BF16)
         term = dot(aggregated, hidden_grad, TN)
         grad = term if grad is None else grad + term
-        upstream_ref[rows, :] = dot(hidden_grad, weight, NT).astype(BF16)
-    upstream = upstream_ref[...]
-    copies = hub_copies(upstream, hub_ref[...], send_ref[...])
-    partial = dot(matrix_t_ref[...], upstream)
-    out_ref[...] = jnp.concatenate(halves(copies) + halves(partial) + [shares(grad)], axis=1).astype(BF16)
-
-
-def final_kernel(received_ref, matrix_ref, near_ref, send_ref, hub_smem, out_ref, total):
+        upstream[rows, :] = dot(hidden_grad, weight, NT).astype(BF16)
+    stores = start([(upstream, upstream_hbm), (activated, activated_hbm)], sems.at[pl.ds(22, 2)])
+    value = upstream[...]
+    loads[4 + 2 * BLOCKS].wait()
+    partial = dot(matrix_t[...], value)
+    copies = hub_copies(value, hub[...], send[...])
+    outgoing[...] = jnp.concatenate(halves(copies) + halves(partial) + [shares(grad)], axis=1).astype(BF16)
+    stores += start([(outgoing, out_hbm)], sems.at[pl.ds(24, 1)])
+    for copy in stores:
+        copy.wait()
+
+
+def final_kernel(received_ref, matrix_hbm, near_hbm, send_hbm, hub_smem, out_hbm, matrix, total, send, result, sems):
+    loads = start([(send_hbm, send)] + sums_loads(matrix_hbm, near_hbm, matrix, total), sems)
+    loads[0].wait()
     received = received_ref[...].astype(F32)
-    gather_sums(near_ref, matrix_ref, joined(received, 0), joined(received, 16), send_ref, hub_smem, total)
-    out_ref[...] = total[...].astype(BF16)
+    mirrored, returned = joined(received, 0), joined(received, 16)
+    gather_sums(loads[1:], matrix, mirrored, returned, send[...], hub_smem, total)
+    stores = []
+    for i in range(8):
+        result[rows_of(i), :] = total[rows_of(i), :].astype(BF16)
+        stores += start([(result.at[rows_of(i)], out_hbm.at[rows_of(i)])], sems.at[pl.ds(18 + i, 1)])
+    for copy in stores:
+        copy.wait()
 
 
 def share_kernel(received_ref, out_ref):
@@ -300,25 +350,34 @@
          pltpu.VMEM(hub_rows.shape, I32), pltpu.VMEM(send_t.shape, I32), pltpu.VMEM((slots, rows), BF16),
          pltpu.VMEM(square, I32), pltpu.VMEM((32, 128, 256), F32), pltpu.VMEM((8, 128), I32),
          pltpu.SMEM((8, 128), I32), pltpu.SemaphoreType.DMA((8,))],
-        hbm=range(6), hbm_out=(0,), flops=1 << 33, limit=56,
+        hbm=range(6), hbm_out=(0,), flops=1 << 33, limit=LARGE,
     )
     received = exchange(outgoing)
+    wide, tall, flat = pltpu.VMEM((rows, slots), BF16), pltpu.VMEM((slots, rows), BF16), pltpu.VMEM((rows, columns), BF16)
+    sums, send_row = pltpu.VMEM((rows, columns), F32), pltpu.VMEM((1, slots), I32)
     near, matrix = run(
         near_kernel, "near", (tiles, tile_cols, tile_rows, features, matrix_t),
-        [((rows, columns), F32), ((rows, slots), BF16)], smem=(1, 2), flops=1 << 31,
+        [((rows, columns), F32), ((rows, slots), BF16)], [sums, wide, pltpu.SemaphoreType.DMA((2,))],
+        smem=(1, 2), hbm_out=(0, 1), flops=1 << 31, limit=LARGE,
     )
     activated, upstream, outgoing = run(
         layer_kernel, "layer",
         (received, matrix, matrix_t, near, cotangent, weight, hub_rows, send, hub_rows),
         [((rows, columns), BF16), ((rows, columns), BF16), ((peers, 40, 128), BF16)],
-        [pltpu.VMEM((rows, columns), F32)], smem=(8,), flops=1 << 32,
+        [wide, tall, sums, flat, pltpu.VMEM(weight.shape, BF16),
+         pltpu.VMEM(hub_rows.shape, I32), send_row, flat, flat,
+         pltpu.VMEM((peers, 40, 128), BF16), pltpu.SemaphoreType.DMA((25,))],
+        smem=(8,), hbm=range(1, 8), hbm_out=(0, 1, 2), flops=1 << 32, limit=MOST,
     )
     received = exchange(outgoing)
     (near,) = run(
         functools.partial(tile_products, True), "near_t", (tiles, tile_rows, tile_cols, upstream),
-        [((rows, columns), F32)], smem=(1, 2), flops=1 << 31,
-    )
-    (own,) = run(share_kernel, "share", (received,), [((weight.shape[0] // peers, columns), F32)])
+        [((rows, columns), F32)], smem=(1, 2), flops=1 << 31, limit=LARGE,
+    )
+    (own,) = run(
+        share_kernel, "share", (received,), [((weight.shape[0] // peers, columns), F32)],
+        limit=MOST,
+    )
     summed = own
     for shift in range(1, groups):
         summed = summed + lax.ppermute(own, "grp", [(g, (g + shift) % groups) for g in range(groups)])
@@ -326,7 +385,8 @@
     weight_grad = summed * scale
     (feature_grad,) = run(
         final_kernel, "final", (received, matrix, near, send, hub_rows), [((rows, columns), BF16)],
-        [pltpu.VMEM((rows, columns), F32)], smem=(4,), flops=1 << 31,
+        [wide, sums, send_row, flat, pltpu.SemaphoreType.DMA((26,))],
+        smem=(4,), hbm=range(1, 4), hbm_out=(0,), flops=1 << 31, limit=MOST,
     )
     return (activated, feature_grad, weight_grad)
 

time: 90.1 us -> 86.8 us (0.963)
  local copies, waits for them, and re-layouts: 16.6 us -> 0.02 us
  Pallas kernels: 23.4 us -> 33.5 us
  waiting for transfers between devices: 25.5 us -> 28.7 us
    unnamed x40 -> x6, local copies, waits for them, and re-layouts: 16.6 us -> 0.02 us
    pallas_call x6, Pallas kernels: 23.4 us -> 33.5 us  [run(): pl.pallas_call(kernel, out_shape=[jax.ShapeDtypeStruct(s, d) for s, d in...]
    all_to_all x2, waiting for transfers between devices: 25.5 us -> 28.7 us  [exchange(): return lax.all_to_all(x, 'dev', split_axis=0, concat_axis=0, tiled=True)]
  transfers between devices with their start and end apart: 5 -> 5, of which waited for: 2 -> 2; matrix products, arithmetic and copies ran while one was open for 0% -> 0% of each run, Pallas kernels for 6% -> 16%
where the time goes in v3:
time: 86.8 us; the launch traced here: 86.5 us
  Pallas kernels  33.5 us (39%)
  waiting for transfers between devices  28.7 us (33%)
  starting transfers between devices  22.9 us (26%)
    pallas_call x6, Pallas kernels, run(): pl.pallas_call(kernel, out_shape=[jax.ShapeDtypeStruct(s, d) for s, d in...  33.5 us
    all_to_all x2, waiting for transfers between devices, exchange(): return lax.all_to_all(x, 'dev', split_axis=0, concat_axis=0, tiled=True)  28.7 us
    all_to_all x2, starting transfers between devices, exchange(): return lax.all_to_all(x, 'dev', split_axis=0, concat_axis=0, tiled=True)  18.1 us
    ppermute x3, starting transfers between devices, local(): lax.ppermute(own, 'grp', [(g, (g + shift) % groups) for g in range(groups)])  4.83 us
  transfers between devices with their start and end apart: 5, of which 2 were waited for; matrix products, arithmetic and copies ran while one was open for 0% of the time, Pallas kernels for 16%

profile of v3, /device:TPU:2, one launch (start us, length us, event | category | flops | bytes accessed | tf_op | source)
XLA Modules:
  0.0 86.5 jit_solution(3351142412172312639)
XLA Ops:
  0.6 11.6 %edges.1 = (bf16[512,2048]{1,0:T(8,128)(2,1)}, s32[1,512]{1,0:T(1,128)}, bf16[64,16,256]{2,1,0:T(8,128)(2,1)}) custom-call(s32[128,128]{1,0:T(8,128)} %bitcast.9, s32[128,128]{1,0:T(8,128)} %bitcast.10, f32[128,128]{1,0:T(8,128)} %bitcast.11, bf16[2048,256]{1,0:T(8,128)(2,1)} %signal_ref.1, s32[1,32]{1,0:T(1,128)} %hub_smem.3, s32[8,64]{1,0:T(8,128)} %bitcast.12), custom_call_target="tpu_custom_call" | custom-call | flops 8589934592 | bytes 3870848 | tf_op jit(solution)/shard_map/edges/pallas_call | solution.py:307
  12.2 12.1 %all-to-all-start = ((bf16[64,16,256]{2,1,0:T(8,128)(2,1)}), bf16[64,16,256]{2,1,0:T(8,128)(2,1)S(1)}, u32[]{:S(2)}, u32[]{:S(2)}) async-start(bf16[64,16,256]{2,1,0:T(8,128)(2,1)} %get-tuple-element.11), calls=%async_computation | async-start | bytes 1048576 | tf_op jit(solution)/shard_map/all_to_all | solution.py:320
  24.3 0.0 copy-start
  24.4 0.0 copy-start.1
  24.4 0.0 copy-start.2
  24.4 5.5 %near.1 = (f32[2048,256]{1,0:T(8,128)}, bf16[2048,512]{1,0:T(8,128)(2,1)}) custom-call(bf16[32,128,128]{2,1,0:T(8,128)(2,1)} %bitcast.7, s32[1,32]{1,0:T(1,128)} %to_ref.3, s32[1,32]{1,0:T(1,128)} %from_ref.3, bf16[2048,256]{1,0:T(8,128)(2,1)} %signal_ref.1, bf16[512,2048]{1,0:T(8,128)(2,1)} %get-tuple-element.12.matrix_t_ref.matrix_t_hbm), custom_call_target="tpu_custom_call" | custom-call | flops 2147483648 | bytes 8388864 | tf_op jit(solution)/shard_map/near/pallas_call | solution.py:307
  29.9 12.1 %all-to-all-done.received_ref = bf16[64,16,256]{2,1,0:T(8,128)(2,1)S(1)} async-done(((bf16[64,16,256]{2,1,0:T(8,128)(2,1)}), bf16[64,16,256]{2,1,0:T(8,128)(2,1)S(1)}, u32[]{:S(2)}, u32[]{:S(2)}) %all-to-all-start) | async-done | bytes 524320 | tf_op jit(solution)/shard_map/all_to_all | solution.py:320
  42.0 0.0 copy-done
  42.0 0.0 copy-done.1
  42.0 0.0 copy-done.2
  42.0 8.0 %layer.1 = (bf16[2048,256]{1,0:T(8,128)(2,1)}, bf16[2048,256]{1,0:T(8,128)(2,1)}, bf16[64,40,128]{2,1,0:T(8,128)(2,1)}) custom-call(bf16[64,16,256]{2,1,0:T(8,128)(2,1)S(1)} %all-to-all-done.received_ref, bf16[2048,512]{1,0:T(8,128)(2,1)} %get-tuple-element.13.matrix_hbm, bf16[512,2048]{1,0:T(8,128)(2,1)} %get-tuple-element.12.matrix_t_ref.matrix_t_hbm, ...), custom_call_target="tpu_custom_call" | custom-call | flops 4294967296 | bytes 10750208 | tf_op jit(solution)/shard_map/layer/pallas_call | solution.py:307
  50.0 6.0 %all-to-all-start.1 = ((bf16[64,40,128]{2,1,0:T(8,128)(2,1)}), bf16[64,40,128]{2,1,0:T(8,128)(2,1)S(1)}, u32[]{:S(2)}, u32[]{:S(2)}) async-start(bf16[64,40,128]{2,1,0:T(8,128)(2,1)} %get-tuple-element.17), calls=%async_computation.1 | async-start | bytes 1310720 | tf_op jit(solution)/shard_map/all_to_all | solution.py:320
  56.0 3.7 %near_t.1.near_hbm = f32[2048,256]{1,0:T(8,128)} custom-call(bf16[32,128,128]{2,1,0:T(8,128)(2,1)} %bitcast.8, s32[1,32]{1,0:T(1,128)} %from_ref.3, s32[1,32]{1,0:T(1,128)} %to_ref.3, bf16[2048,256]{1,0:T(8,128)(2,1)} %get-tuple-element.18.signal_ref), custom_call_target="tpu_custom_call" | custom-call | flops 2147483648 | bytes 4194560 | tf_op jit(solution)/shard_map/near_t/pallas_call | solution.py:307
  59.7 16.6 %all-to-all-done.1.received_ref = bf16[64,40,128]{2,1,0:T(8,128)(2,1)S(1)} async-done(((bf16[64,40,128]{2,1,0:T(8,128)(2,1)}), bf16[64,40,128]{2,1,0:T(8,128)(2,1)S(1)}, u32[]{:S(2)}, u32[]{:S(2)}) %all-to-all-start.1) | async-done | bytes 655392 | tf_op jit(solution)/shard_map/all_to_all | solution.py:320
  76.2 0.1 share.1
  76.3 0.6 collective-permute-start.2
  76.9 2.4 %collective-permute-start.1 = (f32[4,256]{1,0:T(4,128)S(1)}, f32[4,256]{1,0:T(4,128)S(1)}, u32[]{:S(2)}, u32[]{:S(2)}) collective-permute-start(f32[4,256]{1,0:T(4,128)S(1)} %share.1), channel_id=1, source_target_pairs={{0,128},{64,192},{128,0},{192,64},{1,129},{65,193},{129,1},{193,65... | collective-permute-start | bytes 12296 | tf_op jit(solution)/shard_map/ppermute | solution.py:383
  79.3 1.8 %collective-permute-start = (f32[4,256]{1,0:T(4,128)S(1)}, f32[4,256]{1,0:T(4,128)S(1)}, u32[]{:S(2)}, u32[]{:S(2)}) collective-permute-start(f32[4,256]{1,0:T(4,128)S(1)} %share.1), channel_id=1, source_target_pairs={{0,64},{64,128},{128,192},{192,0},{1,65},{65,129},{129,193},{193,1... | collective-permute-start | bytes 12296 | tf_op jit(solution)/shard_map/ppermute | solution.py:383
  81.1 4.7 %final.1 = bf16[2048,256]{1,0:T(8,128)(2,1)} custom-call(bf16[64,40,128]{2,1,0:T(8,128)(2,1)S(1)} %all-to-all-done.1.received_ref, bf16[2048,512]{1,0:T(8,128)(2,1)} %get-tuple-element.13.matrix_hbm, f32[2048,256]{1,0:T(8,128)} %near_t.1.near_hbm, s32[1,512]{1,0:T(1,128)S(1)} %copy-done.2, s32[1,32]{1,0:T(1,128)S(1)} %copy-done.1), custom_call_target="tpu_custom_call" | custom-call | flops 2147483648 | bytes 5900416 | tf_op jit(solution)/shard_map/final/pallas_call | solution.py:307
  85.9 0.0 collective-permute-done.2
  85.9 0.0 collective-permute-done.1
  85.9 0.0 collective-permute-done
  85.9 0.6 add_multiply_fusion
Async XLA Ops:
  12.2 29.8 %all-to-all-start = ((bf16[64,16,256]{2,1,0:T(8,128)(2,1)}), bf16[64,16,256]{2,1,0:T(8,128)(2,1)S(1)}, u32[]{:S(2)}, u32[]{:S(2)}) async-start(bf16[64,16,256]{2,1,0:T(8,128)(2,1)} %get-tuple-element.11), calls=%async_computation | async-start | bytes 1048576 | tf_op jit(solution)/shard_map/all_to_all | solution.py:320
  24.3 17.7 %copy-start = (bf16[256,256]{1,0:T(8,128)(2,1)S(1)}, bf16[256,256]{1,0:T(8,128)(2,1)}, u32[]{:S(2)}) copy-start(bf16[256,256]{1,0:T(8,128)(2,1)} %weight_hbm.1) | copy-start | bytes 393220
  24.4 17.6 %copy-start.1 = (s32[1,32]{1,0:T(1,128)S(1)}, s32[1,32]{1,0:T(1,128)}, u32[]{:S(2)}) copy-start(s32[1,32]{1,0:T(1,128)} %hub_smem.3) | copy-start | bytes 388
  24.4 17.6 %copy-start.2 = (s32[1,512]{1,0:T(1,128)S(1)}, s32[1,512]{1,0:T(1,128)}, u32[]{:S(2)}) copy-start(s32[1,512]{1,0:T(1,128)} %get-tuple-element.15.send_hbm) | copy-start | bytes 6148
  50.0 26.3 %all-to-all-start.1 = ((bf16[64,40,128]{2,1,0:T(8,128)(2,1)}), bf16[64,40,128]{2,1,0:T(8,128)(2,1)S(1)}, u32[]{:S(2)}, u32[]{:S(2)}) async-start(bf16[64,40,128]{2,1,0:T(8,128)(2,1)} %get-tuple-element.17), calls=%async_computation.1 | async-start | bytes 1310720 | tf_op jit(solution)/shard_map/all_to_all | solution.py:320
  76.3 9.6 %collective-permute-start.2 = (f32[4,256]{1,0:T(4,128)S(1)}, f32[4,256]{1,0:T(4,128)S(1)}, u32[]{:S(2)}, u32[]{:S(2)}) collective-permute-start(f32[4,256]{1,0:T(4,128)S(1)} %share.1), channel_id=1, source_target_pairs={{0,192},{64,0},{128,64},{192,128},{1,193},{65,1},{129,65},{193,129... | collective-permute-start | bytes 12296 | tf_op jit(solution)/shard_map/ppermute | solution.py:383
  76.9 9.0 %collective-permute-start.1 = (f32[4,256]{1,0:T(4,128)S(1)}, f32[4,256]{1,0:T(4,128)S(1)}, u32[]{:S(2)}, u32[]{:S(2)}) collective-permute-start(f32[4,256]{1,0:T(4,128)S(1)} %share.1), channel_id=1, source_target_pairs={{0,128},{64,192},{128,0},{192,64},{1,129},{65,193},{129,1},{193,65... | collective-permute-start | bytes 12296 | tf_op jit(solution)/shard_map/ppermute | solution.py:383
  79.3 6.6 %collective-permute-start = (f32[4,256]{1,0:T(4,128)S(1)}, f32[4,256]{1,0:T(4,128)S(1)}, u32[]{:S(2)}, u32[]{:S(2)}) collective-permute-start(f32[4,256]{1,0:T(4,128)S(1)} %share.1), channel_id=1, source_target_pairs={{0,64},{64,128},{128,192},{192,0},{1,65},{65,129},{129,193},{193,1... | collective-permute-start | bytes 12296 | tf_op jit(solution)/shard_map/ppermute | solution.py:383

commit v4 on v3

--- a/solution.py
+++ b/solution.py
@@ -10,7 +10,14 @@
 
 BF16, F32, I32 = jnp.bfloat16, jnp.float32, jnp.int32
 LEVELS = 4095.0
-UNROLL = 32
+UNROLL = 64
+EDGES = 16384
+WINDOWS = 64
+ROW_BITS, SLOT_BITS = 7, 7
+BUCKETS = (2048 >> ROW_BITS) * (512 >> SLOT_BITS)
+KEY_SHIFT = ROW_BITS + SLOT_BITS + 12
+PAIRS = WINDOWS + BUCKETS - 1
+STEPS = -(-PAIRS // UNROLL)
 LARGE = 60
 MOST = 52
 BLOCKS = 4
@@ -70,16 +77,17 @@
     lane = lax.broadcasted_iota(I32, (8, 128), 1)
     first = jnp.zeros((8, 128), I32)
     window, bucket = lane, first
-    for b in range(1, 32):
-        below = functools.reduce(jnp.add, [(xi < (b - 16) * (1 << 27)).astype(F32) for xi in x])
+    size = EDGES // WINDOWS
+    for b in range(1, BUCKETS):
+        below = functools.reduce(jnp.add, [(xi < (b - BUCKETS // 2) * (1 << KEY_SHIFT)).astype(F32) for xi in x])
         count = jnp.sum(jnp.sum(below, axis=0, keepdims=True), axis=1, keepdims=True)
         count = jnp.broadcast_to(count.astype(I32), (8, 128))
-        first = first + (count <= 256 * lane).astype(I32)
-        here = lane == 63 + b
-        window = jnp.where(here, jnp.minimum(count >> 8, 63), window)
-        bucket = jnp.where(here, jnp.where((count & 255) != 0, b, -1), bucket)
-    bucket = jnp.where(lane < 64, first, jnp.where(lane < 95, bucket, -1))
-    window = jnp.where(lane < 95, window, 0)
+        first = first + (count <= size * lane).astype(I32)
+        here = lane == WINDOWS - 1 + b
+        window = jnp.where(here, jnp.minimum(count // size, WINDOWS - 1), window)
+        bucket = jnp.where(here, jnp.where(count % size != 0, b, -1), bucket)
+    bucket = jnp.where(lane < WINDOWS, first, jnp.where(lane < PAIRS, bucket, -1))
+    window = jnp.where(lane < PAIRS, window, 0)
     return jnp.where(lax.broadcasted_iota(I32, (8, 128), 0) == 0, window, bucket)
 
 
@@ -139,13 +147,17 @@
     for i in range(16):
         row, slot = target[8 * i:8 * i + 8, :], slots[8 * i:8 * i + 8, :]
         level = jnp.round(strength[8 * i:8 * i + 8, :] * LEVELS).astype(I32)
-        x.append((((row >> 8) - 4) << 29) | ((slot >> 7) << 27) | ((row & 255) << 19) | ((slot & 127) << 12) | level)
+        bucket = (row >> ROW_BITS) * (512 >> SLOT_BITS) + (slot >> SLOT_BITS) - BUCKETS // 2
+        place_in = ((row & (1 << ROW_BITS) - 1) << SLOT_BITS) | (slot & (1 << SLOT_BITS) - 1)
+        x.append((bucket << KEY_SHIFT) | (place_in << 12) | level)
     table[...] = pair_table(x)
     copy = pltpu.make_async_copy(table, table_smem, sems.at[6])
     copy.start()
     total[...] = jnp.zeros_like(total)
     keys[...] = jnp.concatenate(sorted_keys(x), axis=0).T
     copy.wait()
+    rows_in, slots_in = 1 << ROW_BITS, 1 << SLOT_BITS
+    lines = 128 // WINDOWS
     place = lax.broadcasted_iota(I32, (256, 128), 0).astype(F32).astype(BF16)
 
     def spread(row, count):
@@ -154,13 +166,13 @@
     def product(n):
         window, bucket = table_smem[0, n], table_smem[1, n]
         left, right = [], []
-        for half in range(2):
-            key = keys[pl.ds(2 * window + half, 1), :]
-            row = jnp.where((key >> 27) + 16 == bucket, (key >> 19) & 255, -1)
+        for line in range(lines):
+            key = keys[pl.ds(lines * window + line, 1), :]
+            row = jnp.where((key >> KEY_SHIFT) + BUCKETS // 2 == bucket, (key >> (SLOT_BITS + 12)) & (rows_in - 1), -1)
             level = (key & 4095).astype(F32) * (1.0 / LEVELS)
-            slot = (key >> 12) & 127
-            left.append(jnp.where(place[:128] == spread(slot, 128), jnp.ones((), BF16), jnp.zeros((), BF16)))
-            right.append(jnp.where(place == spread(row, 256), spread(level, 256), jnp.zeros((), BF16)))
+            slot = (key >> 12) & (slots_in - 1)
+            left.append(jnp.where(place[:slots_in] == spread(slot, slots_in), jnp.ones((), BF16), jnp.zeros((), BF16)))
+            right.append(jnp.where(place[:rows_in] == spread(row, rows_in), spread(level, rows_in), jnp.zeros((), BF16)))
         return jnp.maximum(bucket, 0), dot(jnp.concatenate(left, axis=1), jnp.concatenate(right, axis=1), NT)
 
     def step(i, carry):
@@ -168,10 +180,11 @@
             total[bucket] += value
         return carry
 
-    lax.fori_loop(0, 96 // UNROLL, step, 0)
-    for i in range(8):
-        for j in range(4):
-            matrix_t[128 * j:128 * j + 128, 256 * i:256 * i + 256] = total[4 * i + j].astype(BF16)
+    lax.fori_loop(0, STEPS, step, 0)
+    across = 512 >> SLOT_BITS
+    for i in range(2048 >> ROW_BITS):
+        for j in range(across):
+            matrix_t[slots_in * j:slots_in * (j + 1), rows_in * i:rows_in * (i + 1)] = total[across * i + j].astype(BF16)
     store = pltpu.make_async_copy(matrix_t, matrix_t_hbm, sems.at[7])
     store.start()
     for copy in loads[3:]:
@@ -255,24 +268,24 @@
     loads[3 + 2 * BLOCKS].wait()
     grad = None
     stores = []
-    for i in range(8):
-        rows = rows_of(i)
+    for i, rows in enumerate(blocks(total.shape[0])):
         aggregated = total[rows, :].astype(BF16)
         hidden = dot(aggregated, weight)
         logistic = jax.nn.sigmoid(hidden)
         activated[rows, :] = (hidden * logistic).astype(BF16)
         slope = logistic * (1.0 + hidden * (1.0 - logistic))
         hidden_grad = (cotangent[rows, :].astype(F32) * slope).astype(BF16)
+        upstream[rows, :] = dot(hidden_grad, weight, NT).astype(BF16)
         term = dot(aggregated, hidden_grad, TN)
         grad = term if grad is None else grad + term
-        upstream[rows, :] = dot(hidden_grad, weight, NT).astype(BF16)
-    stores = start([(upstream, upstream_hbm), (activated, activated_hbm)], sems.at[pl.ds(22, 2)])
+        stores += start([(upstream.at[rows], upstream_hbm.at[rows]), (activated.at[rows], activated_hbm.at[rows])],
+                        sems.at[pl.ds(5 + 2 * BLOCKS + 2 * i, 2)])
     value = upstream[...]
     loads[4 + 2 * BLOCKS].wait()
     partial = dot(matrix_t[...], value)
     copies = hub_copies(value, hub[...], send[...])
     outgoing[...] = jnp.concatenate(halves(copies) + halves(partial) + [shares(grad)], axis=1).astype(BF16)
-    stores += start([(outgoing, out_hbm)], sems.at[pl.ds(24, 1)])
+    stores += start([(outgoing, out_hbm)], sems.at[pl.ds(5 + 4 * BLOCKS, 1)])
     for copy in stores:
         copy.wait()
 
@@ -348,7 +361,7 @@
         [((slots, rows), BF16), ((1, slots), I32), ((peers, 16, columns), BF16)],
         [pltpu.VMEM(square, I32), pltpu.VMEM(square, I32), pltpu.VMEM(square, F32), pltpu.VMEM((rows, columns), BF16),
          pltpu.VMEM(hub_rows.shape, I32), pltpu.VMEM(send_t.shape, I32), pltpu.VMEM((slots, rows), BF16),
-         pltpu.VMEM(square, I32), pltpu.VMEM((32, 128, 256), F32), pltpu.VMEM((8, 128), I32),
+         pltpu.VMEM(square, I32), pltpu.VMEM((BUCKETS, 1 << SLOT_BITS, 1 << ROW_BITS), F32), pltpu.VMEM((8, 128), I32),
          pltpu.SMEM((8, 128), I32), pltpu.SemaphoreType.DMA((8,))],
         hbm=range(6), hbm_out=(0,), flops=1 << 33, limit=LARGE,
     )
@@ -366,7 +379,7 @@
         [((rows, columns), BF16), ((rows, columns), BF16), ((peers, 40, 128), BF16)],
         [wide, tall, sums, flat, pltpu.VMEM(weight.shape, BF16),
          pltpu.VMEM(hub_rows.shape, I32), send_row, flat, flat,
-         pltpu.VMEM((peers, 40, 128), BF16), pltpu.SemaphoreType.DMA((25,))],
+         pltpu.VMEM((peers, 40, 128), BF16), pltpu.SemaphoreType.DMA((6 + 4 * BLOCKS,))],
         smem=(8,), hbm=range(1, 8), hbm_out=(0, 1, 2), flops=1 << 32, limit=MOST,
     )
     received = exchange(outgoing)

time: 86.8 us -> 84.3 us (0.971)
  Pallas kernels: 33.5 us -> 31.1 us
    pallas_call x6, Pallas kernels: 33.5 us -> 31.1 us  [run(): pl.pallas_call(kernel, out_shape=[jax.ShapeDtypeStruct(s, d) for s, d in...]
  transfers between devices with their start and end apart: 5 -> 5, of which waited for: 2 -> 2; matrix products, arithmetic and copies ran while one was open for 0% -> 0% of each run, Pallas kernels for 16% -> 17%
where the time goes in v4:
time: 84.3 us; the launch traced here: 84 us
  Pallas kernels  31.1 us (37%)
  waiting for transfers between devices  28.7 us (34%)
  starting transfers between devices  22.9 us (27%)
    pallas_call x6, Pallas kernels, run(): pl.pallas_call(kernel, out_shape=[jax.ShapeDtypeStruct(s, d) for s, d in...  31.1 us
    all_to_all x2, waiting for transfers between devices, exchange(): return lax.all_to_all(x, 'dev', split_axis=0, concat_axis=0, tiled=True)  28.7 us
    all_to_all x2, starting transfers between devices, exchange(): return lax.all_to_all(x, 'dev', split_axis=0, concat_axis=0, tiled=True)  18.1 us
    ppermute x3, starting transfers between devices, local(): lax.ppermute(own, 'grp', [(g, (g + shift) % groups) for g in range(groups)])  4.84 us
  transfers between devices with their start and end apart: 5, of which 2 were waited for; matrix products, arithmetic and copies ran while one was open for 0% of the time, Pallas kernels for 17%

profile of v4, /device:TPU:2, one launch (start us, length us, event | category | flops | bytes accessed | tf_op | source)
XLA Modules:
  0.0 84.0 jit_solution(12185535359715764263)
XLA Ops:
  0.6 9.9 %edges.1 = (bf16[512,2048]{1,0:T(8,128)(2,1)}, s32[1,512]{1,0:T(1,128)}, bf16[64,16,256]{2,1,0:T(8,128)(2,1)}) custom-call(s32[128,128]{1,0:T(8,128)} %bitcast.9, s32[128,128]{1,0:T(8,128)} %bitcast.10, f32[128,128]{1,0:T(8,128)} %bitcast.11, bf16[2048,256]{1,0:T(8,128)(2,1)} %signal_ref.1, s32[1,32]{1,0:T(1,128)} %hub_smem.3, s32[8,64]{1,0:T(8,128)} %bitcast.12), custom_call_target="tpu_custom_call" | custom-call | flops 8589934592 | bytes 3870848 | tf_op jit(solution)/shard_map/edges/pallas_call | solution.py:320
  10.6 12.1 %all-to-all-start = ((bf16[64,16,256]{2,1,0:T(8,128)(2,1)}), bf16[64,16,256]{2,1,0:T(8,128)(2,1)S(1)}, u32[]{:S(2)}, u32[]{:S(2)}) async-start(bf16[64,16,256]{2,1,0:T(8,128)(2,1)} %get-tuple-element.11), calls=%async_computation | async-start | bytes 1048576 | tf_op jit(solution)/shard_map/all_to_all | solution.py:333
  22.7 0.0 copy-start
  22.7 0.0 copy-start.1
  22.7 0.0 copy-start.2
  22.7 5.5 %near.1 = (f32[2048,256]{1,0:T(8,128)}, bf16[2048,512]{1,0:T(8,128)(2,1)}) custom-call(bf16[32,128,128]{2,1,0:T(8,128)(2,1)} %bitcast.7, s32[1,32]{1,0:T(1,128)} %to_ref.3, s32[1,32]{1,0:T(1,128)} %from_ref.3, bf16[2048,256]{1,0:T(8,128)(2,1)} %signal_ref.1, bf16[512,2048]{1,0:T(8,128)(2,1)} %get-tuple-element.12.matrix_t_ref.matrix_t_hbm), custom_call_target="tpu_custom_call" | custom-call | flops 2147483648 | bytes 8388864 | tf_op jit(solution)/shard_map/near/pallas_call | solution.py:320
  28.2 12.1 %all-to-all-done.received_ref = bf16[64,16,256]{2,1,0:T(8,128)(2,1)S(1)} async-done(((bf16[64,16,256]{2,1,0:T(8,128)(2,1)}), bf16[64,16,256]{2,1,0:T(8,128)(2,1)S(1)}, u32[]{:S(2)}, u32[]{:S(2)}) %all-to-all-start) | async-done | bytes 524320 | tf_op jit(solution)/shard_map/all_to_all | solution.py:333
  40.3 0.0 copy-done
  40.3 0.0 copy-done.1
  40.3 0.0 copy-done.2
  40.3 7.2 %layer.1 = (bf16[2048,256]{1,0:T(8,128)(2,1)}, bf16[2048,256]{1,0:T(8,128)(2,1)}, bf16[64,40,128]{2,1,0:T(8,128)(2,1)}) custom-call(bf16[64,16,256]{2,1,0:T(8,128)(2,1)S(1)} %all-to-all-done.received_ref, bf16[2048,512]{1,0:T(8,128)(2,1)} %get-tuple-element.13.matrix_hbm, bf16[512,2048]{1,0:T(8,128)(2,1)} %get-tuple-element.12.matrix_t_ref.matrix_t_hbm, ...), custom_call_target="tpu_custom_call" | custom-call | flops 4294967296 | bytes 10750208 | tf_op jit(solution)/shard_map/layer/pallas_call | solution.py:320
  47.5 6.0 %all-to-all-start.1 = ((bf16[64,40,128]{2,1,0:T(8,128)(2,1)}), bf16[64,40,128]{2,1,0:T(8,128)(2,1)S(1)}, u32[]{:S(2)}, u32[]{:S(2)}) async-start(bf16[64,40,128]{2,1,0:T(8,128)(2,1)} %get-tuple-element.17), calls=%async_computation.1 | async-start | bytes 1310720 | tf_op jit(solution)/shard_map/all_to_all | solution.py:333
  53.5 3.7 %near_t.1.near_hbm = f32[2048,256]{1,0:T(8,128)} custom-call(bf16[32,128,128]{2,1,0:T(8,128)(2,1)} %bitcast.8, s32[1,32]{1,0:T(1,128)} %from_ref.3, s32[1,32]{1,0:T(1,128)} %to_ref.3, bf16[2048,256]{1,0:T(8,128)(2,1)} %get-tuple-element.18.signal_ref), custom_call_target="tpu_custom_call" | custom-call | flops 2147483648 | bytes 4194560 | tf_op jit(solution)/shard_map/near_t/pallas_call | solution.py:320
  57.2 16.6 %all-to-all-done.1.received_ref = bf16[64,40,128]{2,1,0:T(8,128)(2,1)S(1)} async-done(((bf16[64,40,128]{2,1,0:T(8,128)(2,1)}), bf16[64,40,128]{2,1,0:T(8,128)(2,1)S(1)}, u32[]{:S(2)}, u32[]{:S(2)}) %all-to-all-start.1) | async-done | bytes 655392 | tf_op jit(solution)/shard_map/all_to_all | solution.py:333
  73.8 0.1 share.1
  73.8 0.6 collective-permute-start.2
  74.5 2.4 %collective-permute-start.1 = (f32[4,256]{1,0:T(4,128)S(1)}, f32[4,256]{1,0:T(4,128)S(1)}, u32[]{:S(2)}, u32[]{:S(2)}) collective-permute-start(f32[4,256]{1,0:T(4,128)S(1)} %share.1), channel_id=1, source_target_pairs={{0,128},{64,192},{128,0},{192,64},{1,129},{65,193},{129,1},{193,65... | collective-permute-start | bytes 12296 | tf_op jit(solution)/shard_map/ppermute | solution.py:396
  76.9 1.8 %collective-permute-start = (f32[4,256]{1,0:T(4,128)S(1)}, f32[4,256]{1,0:T(4,128)S(1)}, u32[]{:S(2)}, u32[]{:S(2)}) collective-permute-start(f32[4,256]{1,0:T(4,128)S(1)} %share.1), channel_id=1, source_target_pairs={{0,64},{64,128},{128,192},{192,0},{1,65},{65,129},{129,193},{193,1... | collective-permute-start | bytes 12296 | tf_op jit(solution)/shard_map/ppermute | solution.py:396
  78.7 4.7 %final.1 = bf16[2048,256]{1,0:T(8,128)(2,1)} custom-call(bf16[64,40,128]{2,1,0:T(8,128)(2,1)S(1)} %all-to-all-done.1.received_ref, bf16[2048,512]{1,0:T(8,128)(2,1)} %get-tuple-element.13.matrix_hbm, f32[2048,256]{1,0:T(8,128)} %near_t.1.near_hbm, s32[1,512]{1,0:T(1,128)S(1)} %copy-done.2, s32[1,32]{1,0:T(1,128)S(1)} %copy-done.1), custom_call_target="tpu_custom_call" | custom-call | flops 2147483648 | bytes 5900416 | tf_op jit(solution)/shard_map/final/pallas_call | solution.py:320
  83.4 0.0 collective-permute-done.2
  83.4 0.0 collective-permute-done.1
  83.4 0.0 collective-permute-done
  83.4 0.6 add_multiply_fusion
Async XLA Ops:
  10.6 29.8 %all-to-all-start = ((bf16[64,16,256]{2,1,0:T(8,128)(2,1)}), bf16[64,16,256]{2,1,0:T(8,128)(2,1)S(1)}, u32[]{:S(2)}, u32[]{:S(2)}) async-start(bf16[64,16,256]{2,1,0:T(8,128)(2,1)} %get-tuple-element.11), calls=%async_computation | async-start | bytes 1048576 | tf_op jit(solution)/shard_map/all_to_all | solution.py:333
  22.7 17.7 %copy-start = (bf16[256,256]{1,0:T(8,128)(2,1)S(1)}, bf16[256,256]{1,0:T(8,128)(2,1)}, u32[]{:S(2)}) copy-start(bf16[256,256]{1,0:T(8,128)(2,1)} %weight_hbm.1) | copy-start | bytes 393220
  22.7 17.6 %copy-start.1 = (s32[1,32]{1,0:T(1,128)S(1)}, s32[1,32]{1,0:T(1,128)}, u32[]{:S(2)}) copy-start(s32[1,32]{1,0:T(1,128)} %hub_smem.3) | copy-start | bytes 388
  22.7 17.6 %copy-start.2 = (s32[1,512]{1,0:T(1,128)S(1)}, s32[1,512]{1,0:T(1,128)}, u32[]{:S(2)}) copy-start(s32[1,512]{1,0:T(1,128)} %get-tuple-element.15.send_hbm) | copy-start | bytes 6148
  47.5 26.3 %all-to-all-start.1 = ((bf16[64,40,128]{2,1,0:T(8,128)(2,1)}), bf16[64,40,128]{2,1,0:T(8,128)(2,1)S(1)}, u32[]{:S(2)}, u32[]{:S(2)}) async-start(bf16[64,40,128]{2,1,0:T(8,128)(2,1)} %get-tuple-element.17), calls=%async_computation.1 | async-start | bytes 1310720 | tf_op jit(solution)/shard_map/all_to_all | solution.py:333
  73.8 9.6 %collective-permute-start.2 = (f32[4,256]{1,0:T(4,128)S(1)}, f32[4,256]{1,0:T(4,128)S(1)}, u32[]{:S(2)}, u32[]{:S(2)}) collective-permute-start(f32[4,256]{1,0:T(4,128)S(1)} %share.1), channel_id=1, source_target_pairs={{0,192},{64,0},{128,64},{192,128},{1,193},{65,1},{129,65},{193,129... | collective-permute-start | bytes 12296 | tf_op jit(solution)/shard_map/ppermute | solution.py:396
  74.5 9.0 %collective-permute-start.1 = (f32[4,256]{1,0:T(4,128)S(1)}, f32[4,256]{1,0:T(4,128)S(1)}, u32[]{:S(2)}, u32[]{:S(2)}) collective-permute-start(f32[4,256]{1,0:T(4,128)S(1)} %share.1), channel_id=1, source_target_pairs={{0,128},{64,192},{128,0},{192,64},{1,129},{65,193},{129,1},{193,65... | collective-permute-start | bytes 12296 | tf_op jit(solution)/shard_map/ppermute | solution.py:396
  76.9 6.6 %collective-permute-start = (f32[4,256]{1,0:T(4,128)S(1)}, f32[4,256]{1,0:T(4,128)S(1)}, u32[]{:S(2)}, u32[]{:S(2)}) collective-permute-start(f32[4,256]{1,0:T(4,128)S(1)} %share.1), channel_id=1, source_target_pairs={{0,64},{64,128},{128,192},{192,0},{1,65},{65,129},{129,193},{193,1... | collective-permute-start | bytes 12296 | tf_op jit(solution)/shard_map/ppermute | solution.py:396

commit v5 on v4

--- a/solution.py
+++ b/solution.py
@@ -134,8 +134,8 @@
     return jnp.concatenate([received[:, i:i + 8].reshape(-1, 128) for i in (at, at + 8)], axis=1).astype(BF16)
 
 
-def edge_kernel(target_hbm, slot_hbm, strength_hbm, signal_hbm, hub_hbm, send_hbm, matrix_t_hbm, send_ref, out_ref,
-                target, slots, strength, signal, hub, send, matrix_t, keys, total, table, table_smem, sems):
+def edge_kernel(target_hbm, slot_hbm, strength_hbm, signal_hbm, hub_hbm, send_hbm, matrix_t_hbm, rest_t_hbm, send_ref, out_ref,
+                target, slots, strength, signal, hub, send, matrix_t, rest_t, keys, total, table, table_smem, sems):
     loads = [pltpu.make_async_copy(src, dst, sems.at[i]) for i, (src, dst) in enumerate(
         [(target_hbm, target), (slot_hbm, slots), (strength_hbm, strength), (signal_hbm, signal), (hub_hbm, hub),
          (send_hbm, send)])]
@@ -165,15 +165,19 @@
 
     def product(n):
         window, bucket = table_smem[0, n], table_smem[1, n]
-        left, right = [], []
+        left, right, low = [], [], []
         for line in range(lines):
             key = keys[pl.ds(lines * window + line, 1), :]
             row = jnp.where((key >> KEY_SHIFT) + BUCKETS // 2 == bucket, (key >> (SLOT_BITS + 12)) & (rows_in - 1), -1)
             level = (key & 4095).astype(F32) * (1.0 / LEVELS)
             slot = (key >> 12) & (slots_in - 1)
             left.append(jnp.where(place[:slots_in] == spread(slot, slots_in), jnp.ones((), BF16), jnp.zeros((), BF16)))
-            right.append(jnp.where(place[:rows_in] == spread(row, rows_in), spread(level, rows_in), jnp.zeros((), BF16)))
-        return jnp.maximum(bucket, 0), dot(jnp.concatenate(left, axis=1), jnp.concatenate(right, axis=1), NT)
+            hit = place[:rows_in] == spread(row, rows_in)
+            right.append(jnp.where(hit, spread(level, rows_in), jnp.zeros((), BF16)))
+            rest = level - level.astype(BF16).astype(F32)
+            low.append(jnp.where(hit, spread(rest, rows_in), jnp.zeros((), BF16)))
+        both = jnp.concatenate([jnp.concatenate(right, axis=1), jnp.concatenate(low, axis=1)], axis=0)
+        return jnp.maximum(bucket, 0), dot(jnp.concatenate(left, axis=1), both, NT)
 
     def step(i, carry):
         for bucket, value in [product(i * UNROLL + u) for u in range(UNROLL)]:
@@ -184,19 +188,23 @@
     across = 512 >> SLOT_BITS
     for i in range(2048 >> ROW_BITS):
         for j in range(across):
-            matrix_t[slots_in * j:slots_in * (j + 1), rows_in * i:rows_in * (i + 1)] = total[across * i + j].astype(BF16)
-    store = pltpu.make_async_copy(matrix_t, matrix_t_hbm, sems.at[7])
-    store.start()
+            full = total[across * i + j, :, :rows_in] + total[across * i + j, :, rows_in:]
+            high = full.astype(BF16)
+            spot = (slice(slots_in * j, slots_in * (j + 1)), slice(rows_in * i, rows_in * (i + 1)))
+            matrix_t[spot] = high
+            rest_t[spot] = (full - high.astype(F32)).astype(BF16)
+    stores = start([(matrix_t, matrix_t_hbm), (rest_t, rest_t_hbm)], sems.at[pl.ds(7, 2)])
     for copy in loads[3:]:
         copy.wait()
     send_row = send_order(send[...])
     send_ref[...] = send_row
     value = signal[...]
-    copies, partial = hub_copies(value, hub[...], send_row), dot(matrix_t[...], value)
-    columns = value.shape[1]
-    both = jnp.concatenate([copies.reshape(-1, 8, columns), partial.reshape(-1, 8, columns)], axis=1)
-    out_ref[...] = both.astype(BF16)
-    store.wait()
+    copies = hub_copies(value, hub[...], send_row)
+    partial = dot(matrix_t[...], value) + dot(rest_t[...], value)
+    high = partial.astype(BF16).astype(F32)
+    out_ref[...] = jnp.concatenate(halves(copies) + halves(high) + halves(partial - high), axis=1).astype(BF16)
+    for copy in stores:
+        copy.wait()
 
 
 def tile_products(transpose, tiles_ref, from_ref, to_ref, signal_ref, out_ref):
@@ -218,13 +226,15 @@
     return slice(256 * i, 256 * i + 256)
 
 
-def near_kernel(tiles_ref, from_ref, to_ref, signal_ref, matrix_t_ref, near_hbm, matrix_hbm, near, matrix, sems):
+def near_kernel(tiles_ref, from_ref, to_ref, signal_ref, matrix_t_ref, rest_t_ref, near_hbm, matrix_hbm, rest_hbm,
+                near, matrix, rest, sems):
     eye = one_hot(lax.broadcasted_iota(I32, (256, 256), 0) == lax.broadcasted_iota(I32, (256, 256), 1))
     for i in range(8):
         for j in range(2):
             matrix[rows_of(i), rows_of(j)] = dot(eye, matrix_t_ref[rows_of(j), rows_of(i)], NT).astype(BF16)
+            rest[rows_of(i), rows_of(j)] = dot(eye, rest_t_ref[rows_of(j), rows_of(i)], NT).astype(BF16)
     tile_products(False, tiles_ref, from_ref, to_ref, signal_ref, near)
-    for copy in start([(matrix, matrix_hbm), (near, near_hbm)], sems):
+    for copy in start([(matrix, matrix_hbm), (rest, rest_hbm), (near, near_hbm)], sems):
         copy.wait()
 
 
@@ -250,20 +260,25 @@
         total[pl.ds(hub_smem[0, h], 1), :] += back[h:h + 1, :]
 
 
-def layer_kernel(received_ref, matrix_hbm, matrix_t_hbm, near_hbm, cotangent_hbm, weight_hbm, hub_hbm, send_hbm,
+def layer_kernel(received_ref, matrix_hbm, rest_hbm, matrix_t_hbm, near_hbm, cotangent_hbm, weight_hbm, hub_hbm, send_hbm,
                  hub_smem, activated_hbm, upstream_hbm, out_hbm,
-                 matrix, matrix_t, total, cotangent, weight_ref, hub, send, activated, upstream,
+                 matrix, rest, matrix_t, total, cotangent, weight_ref, hub, send, activated, upstream,
                  outgoing, sems):
     loads = start(
         [(send_hbm, send), (hub_hbm, hub), (weight_hbm, weight_ref)]
         + sums_loads(matrix_hbm, near_hbm, matrix, total)
-        + [(cotangent_hbm, cotangent), (matrix_t_hbm, matrix_t)], sems)
+        + [(cotangent_hbm, cotangent), (matrix_t_hbm, matrix_t), (rest_hbm, rest)], sems)
     for copy in loads[:3]:
         copy.wait()
     received = received_ref[...].astype(F32)
-    columns = received.shape[2]
-    mirrored, returned = received[:, :8].reshape(-1, columns), received[:, 8:].reshape(-1, columns)
-    gather_sums(loads[3:3 + 2 * BLOCKS], matrix, mirrored.astype(BF16), returned.astype(BF16), send[...], hub_smem, total)
+    mirrored = joined(received, 0)
+    returned = jnp.concatenate([joined(received, 16), joined(received, 32)], axis=0)
+    send_row = send[...]
+    gather_sums(loads[3:3 + 2 * BLOCKS], matrix, mirrored, returned, jnp.concatenate([send_row, send_row], axis=1),
+                hub_smem, total)
+    loads[5 + 2 * BLOCKS].wait()
+    for rows in blocks(total.shape[0]):
+        total[rows, :] += dot(rest[rows, :], mirrored)
     weight = weight_ref[...]
     loads[3 + 2 * BLOCKS].wait()
     grad = None
@@ -279,13 +294,13 @@
         term = dot(aggregated, hidden_grad, TN)
         grad = term if grad is None else grad + term
         stores += start([(upstream.at[rows], upstream_hbm.at[rows]), (activated.at[rows], activated_hbm.at[rows])],
-                        sems.at[pl.ds(5 + 2 * BLOCKS + 2 * i, 2)])
+                        sems.at[pl.ds(6 + 2 * BLOCKS + 2 * i, 2)])
     value = upstream[...]
     loads[4 + 2 * BLOCKS].wait()
     partial = dot(matrix_t[...], value)
     copies = hub_copies(value, hub[...], send[...])
     outgoing[...] = jnp.concatenate(halves(copies) + halves(partial) + [shares(grad)], axis=1).astype(BF16)
-    stores += start([(outgoing, out_hbm)], sems.at[pl.ds(5 + 4 * BLOCKS, 1)])
+    stores += start([(outgoing, out_hbm)], sems.at[pl.ds(6 + 4 * BLOCKS, 1)])
     for copy in stores:
         copy.wait()
 
@@ -354,33 +369,34 @@
     tiles = tile_vals[0]
     square = (128, 128)
 
-    matrix_t, send, outgoing = run(
+    matrix_t, rest_t, send, outgoing = run(
         edge_kernel, "edges",
         (replica_target_row.reshape(square), mirror_slot.reshape(square), replica_edge_weight.reshape(square),
          features, hub_rows, send_t),
-        [((slots, rows), BF16), ((1, slots), I32), ((peers, 16, columns), BF16)],
+        [((slots, rows), BF16), ((slots, rows), BF16), ((1, slots), I32), ((peers, 48, 128), BF16)],
         [pltpu.VMEM(square, I32), pltpu.VMEM(square, I32), pltpu.VMEM(square, F32), pltpu.VMEM((rows, columns), BF16),
          pltpu.VMEM(hub_rows.shape, I32), pltpu.VMEM(send_t.shape, I32), pltpu.VMEM((slots, rows), BF16),
-         pltpu.VMEM(square, I32), pltpu.VMEM((BUCKETS, 1 << SLOT_BITS, 1 << ROW_BITS), F32), pltpu.VMEM((8, 128), I32),
-         pltpu.SMEM((8, 128), I32), pltpu.SemaphoreType.DMA((8,))],
-        hbm=range(6), hbm_out=(0,), flops=1 << 33, limit=LARGE,
+         pltpu.VMEM((slots, rows), BF16), pltpu.VMEM(square, I32),
+         pltpu.VMEM((BUCKETS, 1 << SLOT_BITS, 2 << ROW_BITS), F32), pltpu.VMEM((8, 128), I32),
+         pltpu.SMEM((8, 128), I32), pltpu.SemaphoreType.DMA((9,))],
+        hbm=range(6), hbm_out=(0, 1), flops=1 << 33, limit=LARGE,
     )
     received = exchange(outgoing)
     wide, tall, flat = pltpu.VMEM((rows, slots), BF16), pltpu.VMEM((slots, rows), BF16), pltpu.VMEM((rows, columns), BF16)
     sums, send_row = pltpu.VMEM((rows, columns), F32), pltpu.VMEM((1, slots), I32)
-    near, matrix = run(
-        near_kernel, "near", (tiles, tile_cols, tile_rows, features, matrix_t),
-        [((rows, columns), F32), ((rows, slots), BF16)], [sums, wide, pltpu.SemaphoreType.DMA((2,))],
-        smem=(1, 2), hbm_out=(0, 1), flops=1 << 31, limit=LARGE,
+    near, matrix, rest = run(
+        near_kernel, "near", (tiles, tile_cols, tile_rows, features, matrix_t, rest_t),
+        [((rows, columns), F32), ((rows, slots), BF16), ((rows, slots), BF16)],
+        [sums, wide, wide, pltpu.SemaphoreType.DMA((3,))], smem=(1, 2), hbm_out=(0, 1, 2), flops=1 << 31, limit=LARGE,
     )
     activated, upstream, outgoing = run(
         layer_kernel, "layer",
-        (received, matrix, matrix_t, near, cotangent, weight, hub_rows, send, hub_rows),
+        (received, matrix, rest, matrix_t, near, cotangent, weight, hub_rows, send, hub_rows),
         [((rows, columns), BF16), ((rows, columns), BF16), ((peers, 40, 128), BF16)],
-        [wide, tall, sums, flat, pltpu.VMEM(weight.shape, BF16),
+        [wide, wide, tall, sums, flat, pltpu.VMEM(weight.shape, BF16),
          pltpu.VMEM(hub_rows.shape, I32), send_row, flat, flat,
-         pltpu.VMEM((peers, 40, 128), BF16), pltpu.SemaphoreType.DMA((6 + 4 * BLOCKS,))],
-        smem=(8,), hbm=range(1, 8), hbm_out=(0, 1, 2), flops=1 << 32, limit=MOST,
+         pltpu.VMEM((peers, 40, 128), BF16), pltpu.SemaphoreType.DMA((7 + 4 * BLOCKS,))],
+        smem=(9,), hbm=range(1, 9), hbm_out=(0, 1, 2), flops=1 << 32, limit=MOST,
     )
     received = exchange(outgoing)
     (near,) = run(

time: 84.3 us -> 96.6 us (1.15)
  Pallas kernels: 31.1 us -> 39.7 us
  waiting for transfers between devices: 28.7 us -> 32.4 us
    pallas_call x6, Pallas kernels: 31.1 us -> 39.7 us  [run(): pl.pallas_call(kernel, out_shape=[jax.ShapeDtypeStruct(s, d) for s, d in...]
    all_to_all x2, waiting for transfers between devices: 28.7 us -> 32.4 us  [exchange(): return lax.all_to_all(x, 'dev', split_axis=0, concat_axis=0, tiled=True)]
  transfers between devices with their start and end apart: 5 -> 5, of which waited for: 2 -> 2; matrix products, arithmetic and copies ran while one was open for 0% -> 0% of each run, Pallas kernels for 17% -> 16%
where the time goes in v5:
time: 96.6 us; the launch traced here: 96.3 us
  Pallas kernels  39.7 us (41%)
  waiting for transfers between devices  32.4 us (34%)
  starting transfers between devices  22.8 us (24%)
    pallas_call x6, Pallas kernels, run(): pl.pallas_call(kernel, out_shape=[jax.ShapeDtypeStruct(s, d) for s, d in...  39.7 us
    all_to_all x2, waiting for transfers between devices, exchange(): return lax.all_to_all(x, 'dev', split_axis=0, concat_axis=0, tiled=True)  32.4 us
    all_to_all x2, starting transfers between devices, exchange(): return lax.all_to_all(x, 'dev', split_axis=0, concat_axis=0, tiled=True)  18 us
    ppermute x3, starting transfers between devices, local(): lax.ppermute(own, 'grp', [(g, (g + shift) % groups) for g in range(groups)])  4.83 us
  transfers between devices with their start and end apart: 5, of which 2 were waited for; matrix products, arithmetic and copies ran while one was open for 0% of the time, Pallas kernels for 16%

profile of v5, /device:TPU:2, one launch (start us, length us, event | category | flops | bytes accessed | tf_op | source)
XLA Modules:
  0.0 96.3 jit_solution(5377955940005386843)
XLA Ops:
  0.6 14.8 %edges.1 = (bf16[512,2048]{1,0:T(8,128)(2,1)}, bf16[512,2048]{1,0:T(8,128)(2,1)}, s32[1,512]{1,0:T(1,128)}, bf16[64,48,128]{2,1,0:T(8,128)(2,1)}) custom-call(s32[128,128]{1,0:T(8,128)} %bitcast.9, s32[128,128]{1,0:T(8,128)} %bitcast.10, f32[128,128]{1,0:T(8,128)} %bitcast.11, bf16[2048,256]{1,0:T(8,128)(2,1)} %signal_ref.1, s32[1,32]{1,0:T(1,128)} %hub_smem.3, ...), custom_call_target="tpu_custom_call" | custom-call | flops 8589934592 | bytes 6230144 | tf_op jit(solution)/shard_map/edges/pallas_call | solution.py:335
  15.4 12.3 %all-to-all-start = ((bf16[64,48,128]{2,1,0:T(8,128)(2,1)}), bf16[64,48,128]{2,1,0:T(8,128)(2,1)S(1)}, u32[]{:S(2)}, u32[]{:S(2)}) async-start(bf16[64,48,128]{2,1,0:T(8,128)(2,1)} %get-tuple-element.13), calls=%async_computation | async-start | bytes 1572864 | tf_op jit(solution)/shard_map/all_to_all | solution.py:348
  27.7 0.0 copy-start
  27.7 0.0 copy-start.1
  27.8 0.0 copy-start.2
  27.8 7.4 %near.1 = (f32[2048,256]{1,0:T(8,128)}, bf16[2048,512]{1,0:T(8,128)(2,1)}, bf16[2048,512]{1,0:T(8,128)(2,1)}) custom-call(bf16[32,128,128]{2,1,0:T(8,128)(2,1)} %bitcast.7, s32[1,32]{1,0:T(1,128)} %to_ref.3, s32[1,32]{1,0:T(1,128)} %from_ref.3, bf16[2048,256]{1,0:T(8,128)(2,1)} %signal_ref.1, bf16[512,2048]{1,0:T(8,128)(2,1)} %get-tuple-element.14.matrix_t_ref.matrix_t_hbm, ...), custom_call_target="tpu_custom_call" | custom-call | flops 2147483648 | bytes 12583168 | tf_op jit(solution)/shard_map/near/pallas_call | solution.py:335
  35.2 15.6 %all-to-all-done.received_ref = bf16[64,48,128]{2,1,0:T(8,128)(2,1)S(1)} async-done(((bf16[64,48,128]{2,1,0:T(8,128)(2,1)}), bf16[64,48,128]{2,1,0:T(8,128)(2,1)S(1)}, u32[]{:S(2)}, u32[]{:S(2)}) %all-to-all-start) | async-done | bytes 786464 | tf_op jit(solution)/shard_map/all_to_all | solution.py:348
  50.8 0.0 copy-done
  50.8 0.0 copy-done.1
  50.8 0.0 copy-done.2
  50.8 9.0 %layer.1 = (bf16[2048,256]{1,0:T(8,128)(2,1)}, bf16[2048,256]{1,0:T(8,128)(2,1)}, bf16[64,40,128]{2,1,0:T(8,128)(2,1)}) custom-call(bf16[64,48,128]{2,1,0:T(8,128)(2,1)S(1)} %all-to-all-done.received_ref, bf16[2048,512]{1,0:T(8,128)(2,1)} %get-tuple-element.16.matrix_hbm, bf16[2048,512]{1,0:T(8,128)(2,1)} %get-tuple-element.17.rest_hbm, ...), custom_call_target="tpu_custom_call" | custom-call | flops 4294967296 | bytes 13109504 | tf_op jit(solution)/shard_map/layer/pallas_call | solution.py:335
  59.8 5.7 %all-to-all-start.1 = ((bf16[64,40,128]{2,1,0:T(8,128)(2,1)}), bf16[64,40,128]{2,1,0:T(8,128)(2,1)S(1)}, u32[]{:S(2)}, u32[]{:S(2)}) async-start(bf16[64,40,128]{2,1,0:T(8,128)(2,1)} %get-tuple-element.21), calls=%async_computation.1 | async-start | bytes 1310720 | tf_op jit(solution)/shard_map/all_to_all | solution.py:348
  65.5 3.7 %near_t.1.near_hbm = f32[2048,256]{1,0:T(8,128)} custom-call(bf16[32,128,128]{2,1,0:T(8,128)(2,1)} %bitcast.8, s32[1,32]{1,0:T(1,128)} %from_ref.3, s32[1,32]{1,0:T(1,128)} %to_ref.3, bf16[2048,256]{1,0:T(8,128)(2,1)} %get-tuple-element.22.signal_ref), custom_call_target="tpu_custom_call" | custom-call | flops 2147483648 | bytes 4194560 | tf_op jit(solution)/shard_map/near_t/pallas_call | solution.py:335
  69.2 16.8 %all-to-all-done.1.received_ref = bf16[64,40,128]{2,1,0:T(8,128)(2,1)S(1)} async-done(((bf16[64,40,128]{2,1,0:T(8,128)(2,1)}), bf16[64,40,128]{2,1,0:T(8,128)(2,1)S(1)}, u32[]{:S(2)}, u32[]{:S(2)}) %all-to-all-start.1) | async-done | bytes 655392 | tf_op jit(solution)/shard_map/all_to_all | solution.py:348
  86.0 0.1 share.1
  86.1 0.6 collective-permute-start.2
  86.7 2.4 %collective-permute-start.1 = (f32[4,256]{1,0:T(4,128)S(1)}, f32[4,256]{1,0:T(4,128)S(1)}, u32[]{:S(2)}, u32[]{:S(2)}) collective-permute-start(f32[4,256]{1,0:T(4,128)S(1)} %share.1), channel_id=1, source_target_pairs={{0,128},{64,192},{128,0},{192,64},{1,129},{65,193},{129,1},{193,65... | collective-permute-start | bytes 12296 | tf_op jit(solution)/shard_map/ppermute | solution.py:412
  89.1 1.8 %collective-permute-start = (f32[4,256]{1,0:T(4,128)S(1)}, f32[4,256]{1,0:T(4,128)S(1)}, u32[]{:S(2)}, u32[]{:S(2)}) collective-permute-start(f32[4,256]{1,0:T(4,128)S(1)} %share.1), channel_id=1, source_target_pairs={{0,64},{64,128},{128,192},{192,0},{1,65},{65,129},{129,193},{193,1... | collective-permute-start | bytes 12296 | tf_op jit(solution)/shard_map/ppermute | solution.py:412
  90.9 4.7 %final.1 = bf16[2048,256]{1,0:T(8,128)(2,1)} custom-call(bf16[64,40,128]{2,1,0:T(8,128)(2,1)S(1)} %all-to-all-done.1.received_ref, bf16[2048,512]{1,0:T(8,128)(2,1)} %get-tuple-element.16.matrix_hbm, f32[2048,256]{1,0:T(8,128)} %near_t.1.near_hbm, s32[1,512]{1,0:T(1,128)S(1)} %copy-done.2, s32[1,32]{1,0:T(1,128)S(1)} %copy-done.1), custom_call_target="tpu_custom_call" | custom-call | flops 2147483648 | bytes 5900416 | tf_op jit(solution)/shard_map/final/pallas_call | solution.py:335
  95.6 0.0 collective-permute-done.2
  95.7 0.0 collective-permute-done.1
  95.7 0.0 collective-permute-done
  95.7 0.6 add_multiply_fusion
Async XLA Ops:
  15.4 35.4 %all-to-all-start = ((bf16[64,48,128]{2,1,0:T(8,128)(2,1)}), bf16[64,48,128]{2,1,0:T(8,128)(2,1)S(1)}, u32[]{:S(2)}, u32[]{:S(2)}) async-start(bf16[64,48,128]{2,1,0:T(8,128)(2,1)} %get-tuple-element.13), calls=%async_computation | async-start | bytes 1572864 | tf_op jit(solution)/shard_map/all_to_all | solution.py:348
  27.7 23.1 %copy-start = (bf16[256,256]{1,0:T(8,128)(2,1)S(1)}, bf16[256,256]{1,0:T(8,128)(2,1)}, u32[]{:S(2)}) copy-start(bf16[256,256]{1,0:T(8,128)(2,1)} %weight_hbm.1) | copy-start | bytes 393220
  27.7 23.1 %copy-start.1 = (s32[1,32]{1,0:T(1,128)S(1)}, s32[1,32]{1,0:T(1,128)}, u32[]{:S(2)}) copy-start(s32[1,32]{1,0:T(1,128)} %hub_smem.3) | copy-start | bytes 388
  27.8 23.1 %copy-start.2 = (s32[1,512]{1,0:T(1,128)S(1)}, s32[1,512]{1,0:T(1,128)}, u32[]{:S(2)}) copy-start(s32[1,512]{1,0:T(1,128)} %get-tuple-element.19.send_hbm) | copy-start | bytes 6148
  59.8 26.2 %all-to-all-start.1 = ((bf16[64,40,128]{2,1,0:T(8,128)(2,1)}), bf16[64,40,128]{2,1,0:T(8,128)(2,1)S(1)}, u32[]{:S(2)}, u32[]{:S(2)}) async-start(bf16[64,40,128]{2,1,0:T(8,128)(2,1)} %get-tuple-element.21), calls=%async_computation.1 | async-start | bytes 1310720 | tf_op jit(solution)/shard_map/all_to_all | solution.py:348
  86.1 9.6 %collective-permute-start.2 = (f32[4,256]{1,0:T(4,128)S(1)}, f32[4,256]{1,0:T(4,128)S(1)}, u32[]{:S(2)}, u32[]{:S(2)}) collective-permute-start(f32[4,256]{1,0:T(4,128)S(1)} %share.1), channel_id=1, source_target_pairs={{0,192},{64,0},{128,64},{192,128},{1,193},{65,1},{129,65},{193,129... | collective-permute-start | bytes 12296 | tf_op jit(solution)/shard_map/ppermute | solution.py:412
  86.7 9.0 %collective-permute-start.1 = (f32[4,256]{1,0:T(4,128)S(1)}, f32[4,256]{1,0:T(4,128)S(1)}, u32[]{:S(2)}, u32[]{:S(2)}) collective-permute-start(f32[4,256]{1,0:T(4,128)S(1)} %share.1), channel_id=1, source_target_pairs={{0,128},{64,192},{128,0},{192,64},{1,129},{65,193},{129,1},{193,65... | collective-permute-start | bytes 12296 | tf_op jit(solution)/shard_map/ppermute | solution.py:412
  89.1 6.6 %collective-permute-start = (f32[4,256]{1,0:T(4,128)S(1)}, f32[4,256]{1,0:T(4,128)S(1)}, u32[]{:S(2)}, u32[]{:S(2)}) collective-permute-start(f32[4,256]{1,0:T(4,128)S(1)} %share.1), channel_id=1, source_target_pairs={{0,64},{64,128},{128,192},{192,0},{1,65},{65,129},{129,193},{193,1... | collective-permute-start | bytes 12296 | tf_op jit(solution)/shard_map/ppermute | solution.py:412

commit v6 on v4

--- a/solution.py
+++ b/solution.py
@@ -134,37 +134,24 @@
     return jnp.concatenate([received[:, i:i + 8].reshape(-1, 128) for i in (at, at + 8)], axis=1).astype(BF16)
 
 
-def edge_kernel(target_hbm, slot_hbm, strength_hbm, signal_hbm, hub_hbm, send_hbm, matrix_t_hbm, send_ref, out_ref,
-                target, slots, strength, signal, hub, send, matrix_t, keys, total, table, table_smem, sems):
-    loads = [pltpu.make_async_copy(src, dst, sems.at[i]) for i, (src, dst) in enumerate(
-        [(target_hbm, target), (slot_hbm, slots), (strength_hbm, strength), (signal_hbm, signal), (hub_hbm, hub),
-         (send_hbm, send)])]
-    for copy in loads:
+def start(copies, sems):
+    made = [pltpu.make_async_copy(src, dst, sems.at[i]) for i, (src, dst) in enumerate(copies)]
+    for copy in made:
         copy.start()
-    for copy in loads[:3]:
-        copy.wait()
-    x = []
-    for i in range(16):
-        row, slot = target[8 * i:8 * i + 8, :], slots[8 * i:8 * i + 8, :]
-        level = jnp.round(strength[8 * i:8 * i + 8, :] * LEVELS).astype(I32)
-        bucket = (row >> ROW_BITS) * (512 >> SLOT_BITS) + (slot >> SLOT_BITS) - BUCKETS // 2
-        place_in = ((row & (1 << ROW_BITS) - 1) << SLOT_BITS) | (slot & (1 << SLOT_BITS) - 1)
-        x.append((bucket << KEY_SHIFT) | (place_in << 12) | level)
-    table[...] = pair_table(x)
-    copy = pltpu.make_async_copy(table, table_smem, sems.at[6])
-    copy.start()
+    return made
+
+
+def edge_products(keys, table, total, matrix_t):
     total[...] = jnp.zeros_like(total)
-    keys[...] = jnp.concatenate(sorted_keys(x), axis=0).T
-    copy.wait()
     rows_in, slots_in = 1 << ROW_BITS, 1 << SLOT_BITS
     lines = 128 // WINDOWS
-    place = lax.broadcasted_iota(I32, (256, 128), 0).astype(F32).astype(BF16)
+    place = lax.broadcasted_iota(I32, (128, 128), 0).astype(F32).astype(BF16)
 
     def spread(row, count):
         return jnp.broadcast_to(row.astype(F32), (count, 128)).astype(BF16)
 
     def product(n):
-        window, bucket = table_smem[0, n], table_smem[1, n]
+        window, bucket = table[0, n], table[1, n]
         left, right = [], []
         for line in range(lines):
             key = keys[pl.ds(lines * window + line, 1), :]
@@ -185,18 +172,38 @@
     for i in range(2048 >> ROW_BITS):
         for j in range(across):
             matrix_t[slots_in * j:slots_in * (j + 1), rows_in * i:rows_in * (i + 1)] = total[across * i + j].astype(BF16)
-    store = pltpu.make_async_copy(matrix_t, matrix_t_hbm, sems.at[7])
-    store.start()
+
+
+def edge_kernel(target_hbm, slot_hbm, strength_hbm, signal_hbm, hub_hbm, send_hbm, keys_hbm, table_hbm, send_ref, out_ref,
+                target, slots, strength, signal, hub, send, matrix_t, stash, keys, total, table, table_smem, sems):
+    loads = start([(target_hbm, target), (slot_hbm, slots), (strength_hbm, strength), (signal_hbm, signal), (hub_hbm, hub),
+                   (send_hbm, send)], sems.at[pl.ds(0, 6)])
+    for copy in loads[:3]:
+        copy.wait()
+    x = []
+    for i in range(16):
+        row, slot = target[8 * i:8 * i + 8, :], slots[8 * i:8 * i + 8, :]
+        level = jnp.round(strength[8 * i:8 * i + 8, :] * LEVELS).astype(I32)
+        bucket = (row >> ROW_BITS) * (512 >> SLOT_BITS) + (slot >> SLOT_BITS) - BUCKETS // 2
+        place_in = ((row & (1 << ROW_BITS) - 1) << SLOT_BITS) | (slot & (1 << SLOT_BITS) - 1)
+        x.append((bucket << KEY_SHIFT) | (place_in << 12) | level)
+    table[...] = pair_table(x)
+    stores = start([(table, table_smem), (table, table_hbm)], sems.at[pl.ds(6, 2)])
     for copy in loads[3:]:
         copy.wait()
     send_row = send_order(send[...])
     send_ref[...] = send_row
-    value = signal[...]
-    copies, partial = hub_copies(value, hub[...], send_row), dot(matrix_t[...], value)
-    columns = value.shape[1]
+    stash[...] = hub_copies(signal[...], hub[...], send_row).astype(BF16)
+    keys[...] = jnp.concatenate(sorted_keys(x), axis=0).T
+    stores += start([(keys, keys_hbm)], sems.at[pl.ds(8, 1)])
+    stores[0].wait()
+    edge_products(keys, table_smem, total, matrix_t)
+    copies, partial = stash[...].astype(F32), dot(matrix_t[...], signal[...])
+    columns = partial.shape[1]
     both = jnp.concatenate([copies.reshape(-1, 8, columns), partial.reshape(-1, 8, columns)], axis=1)
     out_ref[...] = both.astype(BF16)
-    store.wait()
+    for copy in stores[1:]:
+        copy.wait()
 
 
 def tile_products(transpose, tiles_ref, from_ref, to_ref, signal_ref, out_ref):
@@ -207,24 +214,20 @@
         out_ref[pl.ds(pl.multiple_of(to_ref[0, t] * 128, 128), 128), :] += value
 
 
-def start(copies, sems):
-    made = [pltpu.make_async_copy(src, dst, sems.at[i]) for i, (src, dst) in enumerate(copies)]
-    for copy in made:
-        copy.start()
-    return made
-
-
 def rows_of(i):
     return slice(256 * i, 256 * i + 256)
 
 
-def near_kernel(tiles_ref, from_ref, to_ref, signal_ref, matrix_t_ref, near_hbm, matrix_hbm, near, matrix, sems):
+def near_kernel(tiles_ref, from_ref, to_ref, signal_ref, keys_ref, table_ref, near_hbm, matrix_hbm, matrix_t_hbm,
+                near, matrix, matrix_t, total, sems):
+    edge_products(keys_ref, table_ref, total, matrix_t)
     eye = one_hot(lax.broadcasted_iota(I32, (256, 256), 0) == lax.broadcasted_iota(I32, (256, 256), 1))
     for i in range(8):
         for j in range(2):
-            matrix[rows_of(i), rows_of(j)] = dot(eye, matrix_t_ref[rows_of(j), rows_of(i)], NT).astype(BF16)
+            matrix[rows_of(i), rows_of(j)] = dot(eye, matrix_t[rows_of(j), rows_of(i)], NT).astype(BF16)
+    stores = start([(matrix, matrix_hbm), (matrix_t, matrix_t_hbm)], sems.at[pl.ds(0, 2)])
     tile_products(False, tiles_ref, from_ref, to_ref, signal_ref, near)
-    for copy in start([(matrix, matrix_hbm), (near, near_hbm)], sems):
+    for copy in stores + start([(near, near_hbm)], sems.at[pl.ds(2, 1)]):
         copy.wait()
 
 
@@ -354,24 +357,26 @@
     tiles = tile_vals[0]
     square = (128, 128)
 
-    matrix_t, send, outgoing = run(
+    wide, tall, flat = pltpu.VMEM((rows, slots), BF16), pltpu.VMEM((slots, rows), BF16), pltpu.VMEM((rows, columns), BF16)
+    sums, send_row = pltpu.VMEM((rows, columns), F32), pltpu.VMEM((1, slots), I32)
+    buckets = pltpu.VMEM((BUCKETS, 1 << SLOT_BITS, 1 << ROW_BITS), F32)
+    keys, table, send, outgoing = run(
         edge_kernel, "edges",
         (replica_target_row.reshape(square), mirror_slot.reshape(square), replica_edge_weight.reshape(square),
          features, hub_rows, send_t),
-        [((slots, rows), BF16), ((1, slots), I32), ((peers, 16, columns), BF16)],
-        [pltpu.VMEM(square, I32), pltpu.VMEM(square, I32), pltpu.VMEM(square, F32), pltpu.VMEM((rows, columns), BF16),
-         pltpu.VMEM(hub_rows.shape, I32), pltpu.VMEM(send_t.shape, I32), pltpu.VMEM((slots, rows), BF16),
-         pltpu.VMEM(square, I32), pltpu.VMEM((BUCKETS, 1 << SLOT_BITS, 1 << ROW_BITS), F32), pltpu.VMEM((8, 128), I32),
-         pltpu.SMEM((8, 128), I32), pltpu.SemaphoreType.DMA((8,))],
-        hbm=range(6), hbm_out=(0,), flops=1 << 33, limit=LARGE,
+        [(square, I32), ((8, 128), I32), ((1, slots), I32), ((peers, 16, columns), BF16)],
+        [pltpu.VMEM(square, I32), pltpu.VMEM(square, I32), pltpu.VMEM(square, F32), flat,
+         pltpu.VMEM(hub_rows.shape, I32), pltpu.VMEM(send_t.shape, I32), tall, pltpu.VMEM((slots, columns), BF16),
+         pltpu.VMEM(square, I32), buckets, pltpu.VMEM((8, 128), I32), pltpu.SMEM((8, 128), I32),
+         pltpu.SemaphoreType.DMA((9,))],
+        hbm=range(6), hbm_out=(0, 1), flops=1 << 33, limit=LARGE,
     )
     received = exchange(outgoing)
-    wide, tall, flat = pltpu.VMEM((rows, slots), BF16), pltpu.VMEM((slots, rows), BF16), pltpu.VMEM((rows, columns), BF16)
-    sums, send_row = pltpu.VMEM((rows, columns), F32), pltpu.VMEM((1, slots), I32)
-    near, matrix = run(
-        near_kernel, "near", (tiles, tile_cols, tile_rows, features, matrix_t),
-        [((rows, columns), F32), ((rows, slots), BF16)], [sums, wide, pltpu.SemaphoreType.DMA((2,))],
-        smem=(1, 2), hbm_out=(0, 1), flops=1 << 31, limit=LARGE,
+    near, matrix, matrix_t = run(
+        near_kernel, "near", (tiles, tile_cols, tile_rows, features, keys, table),
+        [((rows, columns), F32), ((rows, slots), BF16), ((slots, rows), BF16)],
+        [sums, wide, tall, buckets, pltpu.SemaphoreType.DMA((3,))],
+        smem=(1, 2, 5), hbm_out=(0, 1, 2), flops=1 << 33, limit=LARGE,
     )
     activated, upstream, outgoing = run(
         layer_kernel, "layer",

time: 84.3 us -> 83.3 us (0.988)
  waiting for transfers between devices: 28.7 us -> 25.8 us
  Pallas kernels: 31.1 us -> 32.9 us
    all_to_all x2, waiting for transfers between devices: 28.7 us -> 25.8 us  [exchange(): return lax.all_to_all(x, 'dev', split_axis=0, concat_axis=0, tiled=True)]
    pallas_call x6, Pallas kernels: 31.1 us -> 32.9 us  [run(): pl.pallas_call(kernel, out_shape=[jax.ShapeDtypeStruct(s, d) for s, d in...]
  transfers between devices with their start and end apart: 5 -> 5, of which waited for: 2 -> 2; matrix products, arithmetic and copies ran while one was open for 0% -> 0% of each run, Pallas kernels for 17% -> 20%
where the time goes in v6:
time: 83.3 us; the launch traced here: 82.9 us
  Pallas kernels  32.9 us (39%)
  waiting for transfers between devices  25.8 us (31%)
  starting transfers between devices  22.9 us (27%)
    pallas_call x6, Pallas kernels, run(): pl.pallas_call(kernel, out_shape=[jax.ShapeDtypeStruct(s, d) for s, d in...  32.9 us
    all_to_all x2, waiting for transfers between devices, exchange(): return lax.all_to_all(x, 'dev', split_axis=0, concat_axis=0, tiled=True)  25.8 us
    all_to_all x2, starting transfers between devices, exchange(): return lax.all_to_all(x, 'dev', split_axis=0, concat_axis=0, tiled=True)  18.1 us
    ppermute x3, starting transfers between devices, local(): lax.ppermute(own, 'grp', [(g, (g + shift) % groups) for g in range(groups)])  4.82 us
  transfers between devices with their start and end apart: 5, of which 2 were waited for; matrix products, arithmetic and copies ran while one was open for 0% of the time, Pallas kernels for 20%

profile of v6, /device:TPU:2, one launch (start us, length us, event | category | flops | bytes accessed | tf_op | source)
XLA Modules:
  0.0 82.9 jit_solution(15436161425225477767)
XLA Ops:
  0.6 8.8 %edges.1 = (s32[128,128]{1,0:T(8,128)}, s32[8,128]{1,0:T(8,128)}, s32[1,512]{1,0:T(1,128)}, bf16[64,16,256]{2,1,0:T(8,128)(2,1)}) custom-call(s32[128,128]{1,0:T(8,128)} %bitcast.9, s32[128,128]{1,0:T(8,128)} %bitcast.10, f32[128,128]{1,0:T(8,128)} %bitcast.11, bf16[2048,256]{1,0:T(8,128)(2,1)} %signal_ref.1, s32[1,32]{1,0:T(1,128)} %hub_smem.3, ...), custom_call_target="tpu_custom_call" | custom-call | flops 8589934592 | bytes 1843328 | tf_op jit(solution)/shard_map/edges/pallas_call | solution.py:323
  9.5 12.3 %all-to-all-start = ((bf16[64,16,256]{2,1,0:T(8,128)(2,1)}), bf16[64,16,256]{2,1,0:T(8,128)(2,1)S(1)}, u32[]{:S(2)}, u32[]{:S(2)}) async-start(bf16[64,16,256]{2,1,0:T(8,128)(2,1)} %get-tuple-element.13), calls=%async_computation | async-start | bytes 1048576 | tf_op jit(solution)/shard_map/all_to_all | solution.py:336
  21.8 0.0 copy-start
  21.8 0.0 copy-start.1
  21.8 0.0 copy-start.2
  21.8 8.4 %near.1 = (f32[2048,256]{1,0:T(8,128)}, bf16[2048,512]{1,0:T(8,128)(2,1)}, bf16[512,2048]{1,0:T(8,128)(2,1)}) custom-call(bf16[32,128,128]{2,1,0:T(8,128)(2,1)} %bitcast.7, s32[1,32]{1,0:T(1,128)} %to_ref.3, s32[1,32]{1,0:T(1,128)} %from_ref.3, bf16[2048,256]{1,0:T(8,128)(2,1)} %signal_ref.1, s32[128,128]{1,0:T(8,128)} %get-tuple-element.14.keys_ref, ...), custom_call_target="tpu_custom_call" | custom-call | flops 8589934592 | bytes 8458496 | tf_op jit(solution)/shard_map/near/pallas_call | solution.py:323
  30.2 9.0 %all-to-all-done.received_ref = bf16[64,16,256]{2,1,0:T(8,128)(2,1)S(1)} async-done(((bf16[64,16,256]{2,1,0:T(8,128)(2,1)}), bf16[64,16,256]{2,1,0:T(8,128)(2,1)S(1)}, u32[]{:S(2)}, u32[]{:S(2)}) %all-to-all-start) | async-done | bytes 524320 | tf_op jit(solution)/shard_map/all_to_all | solution.py:336
  39.2 0.0 copy-done
  39.2 0.0 copy-done.1
  39.2 0.0 copy-done.2
  39.3 7.1 %layer.1 = (bf16[2048,256]{1,0:T(8,128)(2,1)}, bf16[2048,256]{1,0:T(8,128)(2,1)}, bf16[64,40,128]{2,1,0:T(8,128)(2,1)}) custom-call(bf16[64,16,256]{2,1,0:T(8,128)(2,1)S(1)} %all-to-all-done.received_ref, bf16[2048,512]{1,0:T(8,128)(2,1)} %get-tuple-element.16.matrix_hbm, bf16[512,2048]{1,0:T(8,128)(2,1)} %get-tuple-element.17.matrix_t_hbm, ...), custom_call_target="tpu_custom_call" | custom-call | flops 4294967296 | bytes 10750208 | tf_op jit(solution)/shard_map/layer/pallas_call | solution.py:323
  46.4 5.8 %all-to-all-start.1 = ((bf16[64,40,128]{2,1,0:T(8,128)(2,1)}), bf16[64,40,128]{2,1,0:T(8,128)(2,1)S(1)}, u32[]{:S(2)}, u32[]{:S(2)}) async-start(bf16[64,40,128]{2,1,0:T(8,128)(2,1)} %get-tuple-element.21), calls=%async_computation.1 | async-start | bytes 1310720 | tf_op jit(solution)/shard_map/all_to_all | solution.py:336
  52.2 3.7 %near_t.1.near_hbm = f32[2048,256]{1,0:T(8,128)} custom-call(bf16[32,128,128]{2,1,0:T(8,128)(2,1)} %bitcast.8, s32[1,32]{1,0:T(1,128)} %from_ref.3, s32[1,32]{1,0:T(1,128)} %to_ref.3, bf16[2048,256]{1,0:T(8,128)(2,1)} %get-tuple-element.22.signal_ref), custom_call_target="tpu_custom_call" | custom-call | flops 2147483648 | bytes 4194560 | tf_op jit(solution)/shard_map/near_t/pallas_call | solution.py:323
  55.9 16.8 %all-to-all-done.1.received_ref = bf16[64,40,128]{2,1,0:T(8,128)(2,1)S(1)} async-done(((bf16[64,40,128]{2,1,0:T(8,128)(2,1)}), bf16[64,40,128]{2,1,0:T(8,128)(2,1)S(1)}, u32[]{:S(2)}, u32[]{:S(2)}) %all-to-all-start.1) | async-done | bytes 655392 | tf_op jit(solution)/shard_map/all_to_all | solution.py:336
  72.7 0.1 share.1
  72.8 0.6 collective-permute-start.2
  73.3 2.4 %collective-permute-start.1 = (f32[4,256]{1,0:T(4,128)S(1)}, f32[4,256]{1,0:T(4,128)S(1)}, u32[]{:S(2)}, u32[]{:S(2)}) collective-permute-start(f32[4,256]{1,0:T(4,128)S(1)} %share.1), channel_id=1, source_target_pairs={{0,128},{64,192},{128,0},{192,64},{1,129},{65,193},{129,1},{193,65... | collective-permute-start | bytes 12296 | tf_op jit(solution)/shard_map/ppermute | solution.py:401
  75.8 1.8 %collective-permute-start = (f32[4,256]{1,0:T(4,128)S(1)}, f32[4,256]{1,0:T(4,128)S(1)}, u32[]{:S(2)}, u32[]{:S(2)}) collective-permute-start(f32[4,256]{1,0:T(4,128)S(1)} %share.1), channel_id=1, source_target_pairs={{0,64},{64,128},{128,192},{192,0},{1,65},{65,129},{129,193},{193,1... | collective-permute-start | bytes 12296 | tf_op jit(solution)/shard_map/ppermute | solution.py:401
  77.6 4.7 %final.1 = bf16[2048,256]{1,0:T(8,128)(2,1)} custom-call(bf16[64,40,128]{2,1,0:T(8,128)(2,1)S(1)} %all-to-all-done.1.received_ref, bf16[2048,512]{1,0:T(8,128)(2,1)} %get-tuple-element.16.matrix_hbm, f32[2048,256]{1,0:T(8,128)} %near_t.1.near_hbm, s32[1,512]{1,0:T(1,128)S(1)} %copy-done.2, s32[1,32]{1,0:T(1,128)S(1)} %copy-done.1), custom_call_target="tpu_custom_call" | custom-call | flops 2147483648 | bytes 5900416 | tf_op jit(solution)/shard_map/final/pallas_call | solution.py:323
  82.3 0.0 collective-permute-done.2
  82.3 0.0 collective-permute-done.1
  82.3 0.0 collective-permute-done
  82.3 0.6 add_multiply_fusion
Async XLA Ops:
  9.5 29.8 %all-to-all-start = ((bf16[64,16,256]{2,1,0:T(8,128)(2,1)}), bf16[64,16,256]{2,1,0:T(8,128)(2,1)S(1)}, u32[]{:S(2)}, u32[]{:S(2)}) async-start(bf16[64,16,256]{2,1,0:T(8,128)(2,1)} %get-tuple-element.13), calls=%async_computation | async-start | bytes 1048576 | tf_op jit(solution)/shard_map/all_to_all | solution.py:336
  21.8 17.5 %copy-start = (bf16[256,256]{1,0:T(8,128)(2,1)S(1)}, bf16[256,256]{1,0:T(8,128)(2,1)}, u32[]{:S(2)}) copy-start(bf16[256,256]{1,0:T(8,128)(2,1)} %weight_hbm.1) | copy-start | bytes 393220
  21.8 17.5 %copy-start.1 = (s32[1,32]{1,0:T(1,128)S(1)}, s32[1,32]{1,0:T(1,128)}, u32[]{:S(2)}) copy-start(s32[1,32]{1,0:T(1,128)} %hub_smem.3) | copy-start | bytes 388
  21.8 17.5 %copy-start.2 = (s32[1,512]{1,0:T(1,128)S(1)}, s32[1,512]{1,0:T(1,128)}, u32[]{:S(2)}) copy-start(s32[1,512]{1,0:T(1,128)} %get-tuple-element.19.send_hbm) | copy-start | bytes 6148
  46.4 26.3 %all-to-all-start.1 = ((bf16[64,40,128]{2,1,0:T(8,128)(2,1)}), bf16[64,40,128]{2,1,0:T(8,128)(2,1)S(1)}, u32[]{:S(2)}, u32[]{:S(2)}) async-start(bf16[64,40,128]{2,1,0:T(8,128)(2,1)} %get-tuple-element.21), calls=%async_computation.1 | async-start | bytes 1310720 | tf_op jit(solution)/shard_map/all_to_all | solution.py:336
  72.8 9.6 %collective-permute-start.2 = (f32[4,256]{1,0:T(4,128)S(1)}, f32[4,256]{1,0:T(4,128)S(1)}, u32[]{:S(2)}, u32[]{:S(2)}) collective-permute-start(f32[4,256]{1,0:T(4,128)S(1)} %share.1), channel_id=1, source_target_pairs={{0,192},{64,0},{128,64},{192,128},{1,193},{65,1},{129,65},{193,129... | collective-permute-start | bytes 12296 | tf_op jit(solution)/shard_map/ppermute | solution.py:401
  73.3 9.0 %collective-permute-start.1 = (f32[4,256]{1,0:T(4,128)S(1)}, f32[4,256]{1,0:T(4,128)S(1)}, u32[]{:S(2)}, u32[]{:S(2)}) collective-permute-start(f32[4,256]{1,0:T(4,128)S(1)} %share.1), channel_id=1, source_target_pairs={{0,128},{64,192},{128,0},{192,64},{1,129},{65,193},{129,1},{193,65... | collective-permute-start | bytes 12296 | tf_op jit(solution)/shard_map/ppermute | solution.py:401
  75.8 6.6 %collective-permute-start = (f32[4,256]{1,0:T(4,128)S(1)}, f32[4,256]{1,0:T(4,128)S(1)}, u32[]{:S(2)}, u32[]{:S(2)}) collective-permute-start(f32[4,256]{1,0:T(4,128)S(1)} %share.1), channel_id=1, source_target_pairs={{0,64},{64,128},{128,192},{192,0},{1,65},{65,129},{129,193},{193,1... | collective-permute-start | bytes 12296 | tf_op jit(solution)/shard_map/ppermute | solution.py:401

commit v7 on v6

--- a/solution.py
+++ b/solution.py
@@ -95,12 +95,17 @@
     return jnp.where(mask, 1.0, 0.0).astype(BF16)
 
 
-def hub_copies(signal, hub_row, send_row):
-    hubs, rows = hub_row.shape[1], signal.shape[0]
+def hub_pick(hub_row, rows):
+    hubs = hub_row.shape[1]
     square = jnp.broadcast_to(hub_row, (hubs, hubs)).astype(F32)
     diagonal = lax.broadcasted_iota(I32, (hubs, hubs), 0) == lax.broadcasted_iota(I32, (hubs, hubs), 1)
     hub_col = jnp.sum(jnp.where(diagonal, square, 0.0), axis=1, keepdims=True).astype(I32)
-    pick = one_hot(lax.broadcasted_iota(I32, (hubs, rows), 1) == hub_col)
+    return one_hot(lax.broadcasted_iota(I32, (hubs, rows), 1) == hub_col)
+
+
+def hub_copies(signal, hub_row, send_row, pick=None):
+    hubs, rows = hub_row.shape[1], signal.shape[0]
+    pick = hub_pick(hub_row, rows) if pick is None else pick
     hub_values = dot(pick, signal).astype(BF16)
     return dot(slot_matrix(hubs, send_row), hub_values, TN)
 
@@ -142,7 +147,6 @@
 
 
 def edge_products(keys, table, total, matrix_t):
-    total[...] = jnp.zeros_like(total)
     rows_in, slots_in = 1 << ROW_BITS, 1 << SLOT_BITS
     lines = 128 // WINDOWS
     place = lax.broadcasted_iota(I32, (128, 128), 0).astype(F32).astype(BF16)
@@ -194,6 +198,7 @@
     send_row = send_order(send[...])
     send_ref[...] = send_row
     stash[...] = hub_copies(signal[...], hub[...], send_row).astype(BF16)
+    total[...] = jnp.zeros_like(total)
     keys[...] = jnp.concatenate(sorted_keys(x), axis=0).T
     stores += start([(keys, keys_hbm)], sems.at[pl.ds(8, 1)])
     stores[0].wait()
@@ -220,6 +225,7 @@
 
 def near_kernel(tiles_ref, from_ref, to_ref, signal_ref, keys_ref, table_ref, near_hbm, matrix_hbm, matrix_t_hbm,
                 near, matrix, matrix_t, total, sems):
+    total[...] = jnp.zeros_like(total)
     edge_products(keys_ref, table_ref, total, matrix_t)
     eye = one_hot(lax.broadcasted_iota(I32, (256, 256), 0) == lax.broadcasted_iota(I32, (256, 256), 1))
     for i in range(8):
@@ -256,13 +262,14 @@
 def layer_kernel(received_ref, matrix_hbm, matrix_t_hbm, near_hbm, cotangent_hbm, weight_hbm, hub_hbm, send_hbm,
                  hub_smem, activated_hbm, upstream_hbm, out_hbm,
                  matrix, matrix_t, total, cotangent, weight_ref, hub, send, activated, upstream,
-                 outgoing, sems):
+                 outgoing, picks, sems):
     loads = start(
         [(send_hbm, send), (hub_hbm, hub), (weight_hbm, weight_ref)]
         + sums_loads(matrix_hbm, near_hbm, matrix, total)
         + [(cotangent_hbm, cotangent), (matrix_t_hbm, matrix_t)], sems)
     for copy in loads[:3]:
         copy.wait()
+    picks[...] = hub_pick(hub[...], total.shape[0])
     received = received_ref[...].astype(F32)
     columns = received.shape[2]
     mirrored, returned = received[:, :8].reshape(-1, columns), received[:, 8:].reshape(-1, columns)
@@ -286,7 +293,7 @@
     value = upstream[...]
     loads[4 + 2 * BLOCKS].wait()
     partial = dot(matrix_t[...], value)
-    copies = hub_copies(value, hub[...], send[...])
+    copies = hub_copies(value, hub[...], send[...], picks[...])
     outgoing[...] = jnp.concatenate(halves(copies) + halves(partial) + [shares(grad)], axis=1).astype(BF16)
     stores += start([(outgoing, out_hbm)], sems.at[pl.ds(5 + 4 * BLOCKS, 1)])
     for copy in stores:
@@ -384,7 +391,8 @@
         [((rows, columns), BF16), ((rows, columns), BF16), ((peers, 40, 128), BF16)],
         [wide, tall, sums, flat, pltpu.VMEM(weight.shape, BF16),
          pltpu.VMEM(hub_rows.shape, I32), send_row, flat, flat,
-         pltpu.VMEM((peers, 40, 128), BF16), pltpu.SemaphoreType.DMA((6 + 4 * BLOCKS,))],
+         pltpu.VMEM((peers, 40, 128), BF16), pltpu.VMEM((hub_rows.shape[1], rows), BF16),
+         pltpu.SemaphoreType.DMA((6 + 4 * BLOCKS,))],
         smem=(8,), hbm=range(1, 8), hbm_out=(0, 1, 2), flops=1 << 32, limit=MOST,
     )
     received = exchange(outgoing)

time: 83.3 us -> 83.2 us (level)
  no operation moved by 1% of the time
where the time goes in v7:
time: 83.2 us; the launch traced here: 82.9 us
  Pallas kernels  32.9 us (40%)
  waiting for transfers between devices  25.8 us (31%)
  starting transfers between devices  22.9 us (28%)
    pallas_call x6, Pallas kernels, run(): pl.pallas_call(kernel, out_shape=[jax.ShapeDtypeStruct(s, d) for s, d in...  32.9 us
    all_to_all x2, waiting for transfers between devices, exchange(): return lax.all_to_all(x, 'dev', split_axis=0, concat_axis=0, tiled=True)  25.8 us
    all_to_all x2, starting transfers between devices, exchange(): return lax.all_to_all(x, 'dev', split_axis=0, concat_axis=0, tiled=True)  18.1 us
    ppermute x3, starting transfers between devices, local(): lax.ppermute(own, 'grp', [(g, (g + shift) % groups) for g in range(groups)])  4.82 us
  transfers between devices with their start and end apart: 5, of which 2 were waited for; matrix products, arithmetic and copies ran while one was open for 0% of the time, Pallas kernels for 20%

profile of v7, /device:TPU:2, one launch (start us, length us, event | category | flops | bytes accessed | tf_op | source)
XLA Modules:
  0.0 82.9 jit_solution(17956339554295468355)
XLA Ops:
  0.6 8.8 %edges.1 = (s32[128,128]{1,0:T(8,128)}, s32[8,128]{1,0:T(8,128)}, s32[1,512]{1,0:T(1,128)}, bf16[64,16,256]{2,1,0:T(8,128)(2,1)}) custom-call(s32[128,128]{1,0:T(8,128)} %bitcast.9, s32[128,128]{1,0:T(8,128)} %bitcast.10, f32[128,128]{1,0:T(8,128)} %bitcast.11, bf16[2048,256]{1,0:T(8,128)(2,1)} %signal_ref.1, s32[1,32]{1,0:T(1,128)} %hub_smem.3, ...), custom_call_target="tpu_custom_call" | custom-call | flops 8589934592 | bytes 1843328 | tf_op jit(solution)/shard_map/edges/pallas_call | solution.py:330
  9.4 12.3 %all-to-all-start = ((bf16[64,16,256]{2,1,0:T(8,128)(2,1)}), bf16[64,16,256]{2,1,0:T(8,128)(2,1)S(1)}, u32[]{:S(2)}, u32[]{:S(2)}) async-start(bf16[64,16,256]{2,1,0:T(8,128)(2,1)} %get-tuple-element.13), calls=%async_computation | async-start | bytes 1048576 | tf_op jit(solution)/shard_map/all_to_all | solution.py:343
  21.8 0.0 copy-start
  21.8 0.0 copy-start.1
  21.8 0.0 copy-start.2
  21.8 8.4 %near.1 = (f32[2048,256]{1,0:T(8,128)}, bf16[2048,512]{1,0:T(8,128)(2,1)}, bf16[512,2048]{1,0:T(8,128)(2,1)}) custom-call(bf16[32,128,128]{2,1,0:T(8,128)(2,1)} %bitcast.7, s32[1,32]{1,0:T(1,128)} %to_ref.3, s32[1,32]{1,0:T(1,128)} %from_ref.3, bf16[2048,256]{1,0:T(8,128)(2,1)} %signal_ref.1, s32[128,128]{1,0:T(8,128)} %get-tuple-element.14.keys_ref, ...), custom_call_target="tpu_custom_call" | custom-call | flops 8589934592 | bytes 8458496 | tf_op jit(solution)/shard_map/near/pallas_call | solution.py:330
  30.2 9.0 %all-to-all-done.received_ref = bf16[64,16,256]{2,1,0:T(8,128)(2,1)S(1)} async-done(((bf16[64,16,256]{2,1,0:T(8,128)(2,1)}), bf16[64,16,256]{2,1,0:T(8,128)(2,1)S(1)}, u32[]{:S(2)}, u32[]{:S(2)}) %all-to-all-start) | async-done | bytes 524320 | tf_op jit(solution)/shard_map/all_to_all | solution.py:343
  39.2 0.0 copy-done
  39.2 0.0 copy-done.1
  39.2 0.0 copy-done.2
  39.2 7.2 %layer.1 = (bf16[2048,256]{1,0:T(8,128)(2,1)}, bf16[2048,256]{1,0:T(8,128)(2,1)}, bf16[64,40,128]{2,1,0:T(8,128)(2,1)}) custom-call(bf16[64,16,256]{2,1,0:T(8,128)(2,1)S(1)} %all-to-all-done.received_ref, bf16[2048,512]{1,0:T(8,128)(2,1)} %get-tuple-element.16.matrix_hbm, bf16[512,2048]{1,0:T(8,128)(2,1)} %get-tuple-element.17.matrix_t_hbm, ...), custom_call_target="tpu_custom_call" | custom-call | flops 4294967296 | bytes 10750208 | tf_op jit(solution)/shard_map/layer/pallas_call | solution.py:330
  46.4 5.8 %all-to-all-start.1 = ((bf16[64,40,128]{2,1,0:T(8,128)(2,1)}), bf16[64,40,128]{2,1,0:T(8,128)(2,1)S(1)}, u32[]{:S(2)}, u32[]{:S(2)}) async-start(bf16[64,40,128]{2,1,0:T(8,128)(2,1)} %get-tuple-element.21), calls=%async_computation.1 | async-start | bytes 1310720 | tf_op jit(solution)/shard_map/all_to_all | solution.py:343
  52.2 3.7 %near_t.1.near_hbm = f32[2048,256]{1,0:T(8,128)} custom-call(bf16[32,128,128]{2,1,0:T(8,128)(2,1)} %bitcast.8, s32[1,32]{1,0:T(1,128)} %from_ref.3, s32[1,32]{1,0:T(1,128)} %to_ref.3, bf16[2048,256]{1,0:T(8,128)(2,1)} %get-tuple-element.22.signal_ref), custom_call_target="tpu_custom_call" | custom-call | flops 2147483648 | bytes 4194560 | tf_op jit(solution)/shard_map/near_t/pallas_call | solution.py:330
  55.9 16.8 %all-to-all-done.1.received_ref = bf16[64,40,128]{2,1,0:T(8,128)(2,1)S(1)} async-done(((bf16[64,40,128]{2,1,0:T(8,128)(2,1)}), bf16[64,40,128]{2,1,0:T(8,128)(2,1)S(1)}, u32[]{:S(2)}, u32[]{:S(2)}) %all-to-all-start.1) | async-done | bytes 655392 | tf_op jit(solution)/shard_map/all_to_all | solution.py:343
  72.7 0.1 share.1
  72.7 0.6 collective-permute-start.2
  73.3 2.4 %collective-permute-start.1 = (f32[4,256]{1,0:T(4,128)S(1)}, f32[4,256]{1,0:T(4,128)S(1)}, u32[]{:S(2)}, u32[]{:S(2)}) collective-permute-start(f32[4,256]{1,0:T(4,128)S(1)} %share.1), channel_id=1, source_target_pairs={{0,128},{64,192},{128,0},{192,64},{1,129},{65,193},{129,1},{193,65... | collective-permute-start | bytes 12296 | tf_op jit(solution)/shard_map/ppermute | solution.py:409
  75.8 1.8 %collective-permute-start = (f32[4,256]{1,0:T(4,128)S(1)}, f32[4,256]{1,0:T(4,128)S(1)}, u32[]{:S(2)}, u32[]{:S(2)}) collective-permute-start(f32[4,256]{1,0:T(4,128)S(1)} %share.1), channel_id=1, source_target_pairs={{0,64},{64,128},{128,192},{192,0},{1,65},{65,129},{129,193},{193,1... | collective-permute-start | bytes 12296 | tf_op jit(solution)/shard_map/ppermute | solution.py:409
  77.6 4.7 %final.1 = bf16[2048,256]{1,0:T(8,128)(2,1)} custom-call(bf16[64,40,128]{2,1,0:T(8,128)(2,1)S(1)} %all-to-all-done.1.received_ref, bf16[2048,512]{1,0:T(8,128)(2,1)} %get-tuple-element.16.matrix_hbm, f32[2048,256]{1,0:T(8,128)} %near_t.1.near_hbm, s32[1,512]{1,0:T(1,128)S(1)} %copy-done.2, s32[1,32]{1,0:T(1,128)S(1)} %copy-done.1), custom_call_target="tpu_custom_call" | custom-call | flops 2147483648 | bytes 5900416 | tf_op jit(solution)/shard_map/final/pallas_call | solution.py:330
  82.3 0.0 collective-permute-done.2
  82.3 0.0 collective-permute-done.1
  82.3 0.0 collective-permute-done
  82.3 0.6 add_multiply_fusion
Async XLA Ops:
  9.4 29.8 %all-to-all-start = ((bf16[64,16,256]{2,1,0:T(8,128)(2,1)}), bf16[64,16,256]{2,1,0:T(8,128)(2,1)S(1)}, u32[]{:S(2)}, u32[]{:S(2)}) async-start(bf16[64,16,256]{2,1,0:T(8,128)(2,1)} %get-tuple-element.13), calls=%async_computation | async-start | bytes 1048576 | tf_op jit(solution)/shard_map/all_to_all | solution.py:343
  21.8 17.5 %copy-start = (bf16[256,256]{1,0:T(8,128)(2,1)S(1)}, bf16[256,256]{1,0:T(8,128)(2,1)}, u32[]{:S(2)}) copy-start(bf16[256,256]{1,0:T(8,128)(2,1)} %weight_hbm.1) | copy-start | bytes 393220
  21.8 17.5 %copy-start.1 = (s32[1,32]{1,0:T(1,128)S(1)}, s32[1,32]{1,0:T(1,128)}, u32[]{:S(2)}) copy-start(s32[1,32]{1,0:T(1,128)} %hub_smem.3) | copy-start | bytes 388
  21.8 17.5 %copy-start.2 = (s32[1,512]{1,0:T(1,128)S(1)}, s32[1,512]{1,0:T(1,128)}, u32[]{:S(2)}) copy-start(s32[1,512]{1,0:T(1,128)} %get-tuple-element.19.send_hbm) | copy-start | bytes 6148
  46.4 26.3 %all-to-all-start.1 = ((bf16[64,40,128]{2,1,0:T(8,128)(2,1)}), bf16[64,40,128]{2,1,0:T(8,128)(2,1)S(1)}, u32[]{:S(2)}, u32[]{:S(2)}) async-start(bf16[64,40,128]{2,1,0:T(8,128)(2,1)} %get-tuple-element.21), calls=%async_computation.1 | async-start | bytes 1310720 | tf_op jit(solution)/shard_map/all_to_all | solution.py:343
  72.7 9.6 %collective-permute-start.2 = (f32[4,256]{1,0:T(4,128)S(1)}, f32[4,256]{1,0:T(4,128)S(1)}, u32[]{:S(2)}, u32[]{:S(2)}) collective-permute-start(f32[4,256]{1,0:T(4,128)S(1)} %share.1), channel_id=1, source_target_pairs={{0,192},{64,0},{128,64},{192,128},{1,193},{65,1},{129,65},{193,129... | collective-permute-start | bytes 12296 | tf_op jit(solution)/shard_map/ppermute | solution.py:409
  73.3 9.0 %collective-permute-start.1 = (f32[4,256]{1,0:T(4,128)S(1)}, f32[4,256]{1,0:T(4,128)S(1)}, u32[]{:S(2)}, u32[]{:S(2)}) collective-permute-start(f32[4,256]{1,0:T(4,128)S(1)} %share.1), channel_id=1, source_target_pairs={{0,128},{64,192},{128,0},{192,64},{1,129},{65,193},{129,1},{193,65... | collective-permute-start | bytes 12296 | tf_op jit(solution)/shard_map/ppermute | solution.py:409
  75.8 6.6 %collective-permute-start = (f32[4,256]{1,0:T(4,128)S(1)}, f32[4,256]{1,0:T(4,128)S(1)}, u32[]{:S(2)}, u32[]{:S(2)}) collective-permute-start(f32[4,256]{1,0:T(4,128)S(1)} %share.1), channel_id=1, source_target_pairs={{0,64},{64,128},{128,192},{192,0},{1,65},{65,129},{129,193},{193,1... | collective-permute-start | bytes 12296 | tf_op jit(solution)/shard_map/ppermute | solution.py:409
